TPU v7x, 32 devices: a whole 2x2x4 slice. The times are simulated.
32 devices in a mesh: dp: 8 (over z, x), seq: 4 (over y, core).
Axes of the slice: x: 2, y: 2, z: 4, core: 2. Of those that a mesh axis runs over, the one named last changes fastest.
Arguments:
- tokens: bfloat16 [10240, 2048], P(('dp', 'seq')), may hold values from -6 to 6
- segments: int32 [8, 1280], P('dp', 'seq'), may hold values from 0 to 4, never falling along the last dimension, each value on 1 to 1120 neighbouring positions
- cotangent: bfloat16 [10240, 2048], P(('dp', 'seq')), may hold values from -6 to 6
- w_query: float32 [2048, 256], P(('dp', 'seq')), may hold values from -0.1875 to 0.1875
- w_key: float32 [2048, 256], P(('dp', 'seq')), may hold values from -0.1875 to 0.1875
- w_value: float32 [2048, 2048], P(('dp', 'seq')), may hold values from -0.125 to 0.125
- w_out: float32 [2048, 2048], P(('dp', 'seq')), may hold values from -1 to 1
- w_gate: float32 [2048, 5504], P(('dp', 'seq')), may hold values from -0.125 to 0.125
- w_up: float32 [2048, 5504], P(('dp', 'seq')), may hold values from -0.125 to 0.125
- w_down: float32 [2048, 5504], P(('dp', 'seq')), may hold values from -0.078125 to 0.078125
- norm_attn: float32 [2048], P(('dp', 'seq')), may hold values from 0.5 to 1.5
- norm_mlp: float32 [2048], P(('dp', 'seq')), may hold values from 0.5 to 1.5
Outputs:
- output: bfloat16 [10240, 2048], P(('dp', 'seq'))
- grad_tokens: float32 [10240, 2048], P(('dp', 'seq'))
- grad_w_query: float32 [2048, 256], P(('dp', 'seq'))
- grad_w_key: float32 [2048, 256], P(('dp', 'seq'))
- grad_w_value: float32 [2048, 2048], P(('dp', 'seq'))
- grad_w_out: float32 [2048, 2048], P(('dp', 'seq'))
- grad_w_gate: float32 [2048, 5504], P(('dp', 'seq'))
- grad_w_up: float32 [2048, 5504], P(('dp', 'seq'))
- grad_w_down: float32 [2048, 5504], P(('dp', 'seq'))
- grad_norm_attn: float32 [2048], P(('dp', 'seq'))
- grad_norm_mlp: float32 [2048], P(('dp', 'seq'))
Inputs may be any that keep to these rules, and one draw needn't show every extreme that they name: `segments`: along each stream the document numbers never fall; each of the 5 numbers marks one document of 1 to 1120 tokens.
All inputs are finite; a program needn't handle non-finite values.
Results may differ from a plain program's by a relative error of at most 0.012.
The roundings to bfloat16 on the way count: a program that leaves them out, or rounds other values in their place, can miss the bound.
Values may be sent and summed in bfloat16 or wider, within the bound.
No kernel may reach another device: no remote copies, remote signals or barrier semaphores. Data moves between devices by JAX's collectives and lax.ppermute only.
A program may use at most 400 MiB of HBM per device.

v0:
```python
import math

import jax
import jax.numpy as jnp
from jax import lax
from jax.sharding import PartitionSpec as P

D = 2048
H = 16
DV = 128
F = 16
FF = 5504


EPSILON = 1e-06
PRECISE = lax.Precision.HIGHEST
CONTRACT_LAST = (((1,), (1,)), ((), ()))
CONTRACT_FIRST = (((0,), (0,)), ((), ()))


def entering(array, axis, join, neutral, backward):
    count = lax.axis_size(axis)
    place = lax.axis_index(axis)
    ahead = count - 1 - place if backward else place
    gathered = jax.tree.map(
        lambda a, kind: lax.all_gather(a.astype(kind), axis),
        array,
        (jnp.bfloat16, jnp.bfloat16, jnp.bfloat16),
    )
    state = jax.tree.map(lambda a, e: jnp.zeros_like(a) + jnp.asarray(e, a.dtype), array, neutral)

    def one(turn, state):
        source = count - 1 - turn if backward else turn
        return join(
            state,
            jax.tree.map(
                lambda a, own: lax.dynamic_index_in_dim(a, source, 0, False).astype(own.dtype),
                gathered,
                array,
            ),
        )

    return lax.fori_loop(0, ahead, one, state)


def features(inputs):
    feat_width = inputs.shape[-1]
    outer_prod = (inputs[..., :, None] * inputs[..., None, :]).reshape(
        inputs.shape[:-1] + (feat_width * feat_width,)
    )
    constant_one = jnp.ones(inputs.shape[:-1] + (1,), inputs.dtype)
    return jnp.concatenate(
        [
            constant_one,
            inputs * feat_width ** (-0.25),
            outer_prod * (1.0 / math.sqrt(2.0 * feat_width)),
        ],
        axis=-1,
    )


def feature_grad(grad_feat, inputs):
    feat_width = inputs.shape[-1]
    linear_part = grad_feat[..., 1 : 1 + feat_width] * feat_width ** (-0.25)
    square_part = grad_feat[..., 1 + feat_width :].reshape(inputs.shape + (feat_width,)) * (
        1.0 / math.sqrt(2.0 * feat_width)
    )
    return (
        linear_part
        + jnp.einsum("...ij,...j->...i", square_part, inputs, precision=PRECISE)
        + jnp.einsum("...ji,...j->...i", square_part, inputs, precision=PRECISE)
    )


def rms_scale(values):
    inverse = lax.rsqrt(jnp.mean(values * values, axis=-1, keepdims=True) + EPSILON)
    return (values * inverse, inverse)


def rms_back(grad_normed, normed, inverse):
    return inverse * (grad_normed - normed * jnp.mean(grad_normed * normed, axis=-1, keepdims=True))


def chain_join(earlier, later):
    early_state, early_norm, early_key = earlier
    late_state, late_norm, late_key = later
    absent = late_key < 0
    joined = early_key == late_key
    absent_big = absent[..., None, None, None]
    joined_big = joined[..., None, None, None]
    absent_mid = absent[..., None, None]
    joined_mid = joined[..., None, None]
    state_sum = jnp.where(
        absent_big, early_state, jnp.where(joined_big, early_state + late_state, late_state)
    )
    norm_sum = jnp.where(
        absent_mid, early_norm, jnp.where(joined_mid, early_norm + late_norm, late_norm)
    )
    merged_key = jnp.where(absent, early_key, late_key)
    return (state_sum, norm_sum, merged_key)


def carry_forward(state_sum, norm_sum, block_key):
    identity = (
        jnp.zeros_like(state_sum),
        jnp.zeros_like(norm_sum),
        jnp.full((), -1.0, jnp.float32),
    )
    return entering((state_sum, norm_sum, block_key), "seq", chain_join, identity, False)


def carry_backward(state_sum, norm_sum, block_key):
    identity = (
        jnp.zeros_like(state_sum),
        jnp.zeros_like(norm_sum),
        jnp.full((), -1.0, jnp.float32),
    )
    return entering((state_sum, norm_sum, block_key), "seq", chain_join, identity, True)


def per_device(
    tokens,
    segments,
    cotangent,
    w_query,
    w_key,
    w_value,
    w_out,
    w_gate,
    w_up,
    w_down,
    norm_attn,
    norm_mlp,
):
    fwd_weights = (
        lax.all_gather(w_query.astype(jnp.bfloat16), ("dp", "seq"), axis=0, tiled=True),
        lax.all_gather(w_key.astype(jnp.bfloat16), ("dp", "seq"), axis=0, tiled=True),
        lax.all_gather(w_value.astype(jnp.bfloat16), ("dp", "seq"), axis=0, tiled=True),
        lax.all_gather(w_out.astype(jnp.bfloat16), ("dp", "seq"), axis=0, tiled=True),
        lax.all_gather(w_gate.astype(jnp.bfloat16), ("dp", "seq"), axis=0, tiled=True),
        lax.all_gather(w_up.astype(jnp.bfloat16), ("dp", "seq"), axis=0, tiled=True),
        lax.all_gather(w_down.astype(jnp.bfloat16), ("dp", "seq"), axis=0, tiled=True),
        lax.all_gather(norm_attn.astype(jnp.bfloat16), ("dp", "seq"), axis=0, tiled=True),
        lax.all_gather(norm_mlp.astype(jnp.bfloat16), ("dp", "seq"), axis=0, tiled=True),
    )
    query_mat, key_mat, value_mat, out_mat, gate_mat, up_mat, down_mat, gain_attn, gain_mlp = (
        fwd_weights
    )
    tok_rows = tokens.shape[0]
    doc_ids = segments[0]
    inputs = tokens.astype(jnp.float32)
    normed_attn, inverse_attn = rms_scale(inputs)
    gain_one = gain_attn.astype(jnp.float32)
    normed_in = (normed_attn * gain_one).astype(jnp.bfloat16)
    queries = jnp.dot(normed_in, query_mat, preferred_element_type=jnp.float32)
    keys_pre = jnp.dot(normed_in, key_mat, preferred_element_type=jnp.float32)
    values = jnp.dot(normed_in, value_mat, preferred_element_type=jnp.float32)
    query_heads = queries.reshape(tok_rows, H, F)
    key_heads = keys_pre.reshape(tok_rows, H, F)
    feat_query = features(query_heads).astype(jnp.bfloat16)
    feat_key = features(key_heads).astype(jnp.bfloat16)
    value_low = values.astype(jnp.bfloat16).reshape(tok_rows, H, DV)
    query_wide = feat_query.astype(jnp.float32)
    key_wide = feat_key.astype(jnp.float32)
    value_wide = value_low.astype(jnp.float32)
    positions = jnp.arange(tok_rows)
    allowed = (
        (doc_ids[:, None] == doc_ids[None, :]) & (positions[None, :] <= positions[:, None])
    ).astype(jnp.float32)
    scores = (
        jnp.einsum("thf,shf->hts", feat_query, feat_key, preferred_element_type=jnp.float32)
        * allowed[None]
    )
    numer = jnp.einsum("hts,she->the", scores, value_wide, precision=PRECISE)
    denom = jnp.sum(scores, axis=2).T
    last_key = doc_ids[-1]
    last_sel = (doc_ids == last_key).astype(jnp.bfloat16)
    local_state = jnp.einsum(
        "thf,the->hfe",
        feat_key * last_sel[:, None, None],
        value_low,
        preferred_element_type=jnp.float32,
    )
    local_norm = jnp.einsum("thf,t->hf", key_wide, last_sel.astype(jnp.float32), precision=PRECISE)
    carry_state, carry_norm, carry_key = carry_forward(
        local_state, local_norm, last_key.astype(jnp.float32)
    )
    use_in = (doc_ids.astype(jnp.float32) == carry_key).astype(jnp.float32)
    numer = numer + use_in[:, None, None] * jnp.einsum(
        "thf,hfe->the", query_wide, carry_state, precision=PRECISE
    )
    denom = denom + use_in[:, None] * jnp.einsum(
        "thf,hf->th", query_wide, carry_norm, precision=PRECISE
    )
    heads_out = numer / denom[:, :, None]
    attended = heads_out.reshape(tok_rows, D).astype(jnp.bfloat16)
    residual = inputs + jnp.dot(attended, out_mat, preferred_element_type=jnp.float32)
    normed_res, inverse_mlp = rms_scale(residual)
    gain_two = gain_mlp.astype(jnp.float32)
    normed_mid = (normed_res * gain_two).astype(jnp.bfloat16)
    gate_use = gate_mat
    up_use = up_mat
    down_use = down_mat
    gate_pre = jnp.dot(normed_mid, gate_use, preferred_element_type=jnp.float32)
    up_pre = jnp.dot(normed_mid, up_use, preferred_element_type=jnp.float32)
    sigmoid_gate = jax.nn.sigmoid(gate_pre)
    hidden = (gate_pre * sigmoid_gate * up_pre).astype(jnp.bfloat16)
    branch_part = lax.dot_general(
        hidden, down_use, CONTRACT_LAST, preferred_element_type=jnp.float32
    )
    output = (residual + branch_part).astype(jnp.bfloat16)
    back_weights = (
        lax.all_gather(w_query.astype(jnp.bfloat16), ("dp", "seq"), axis=0, tiled=True),
        lax.all_gather(w_key.astype(jnp.bfloat16), ("dp", "seq"), axis=0, tiled=True),
        lax.all_gather(w_value.astype(jnp.bfloat16), ("dp", "seq"), axis=0, tiled=True),
        lax.all_gather(w_out.astype(jnp.bfloat16), ("dp", "seq"), axis=0, tiled=True),
        lax.all_gather(w_gate.astype(jnp.bfloat16), ("dp", "seq"), axis=0, tiled=True),
        lax.all_gather(w_up.astype(jnp.bfloat16), ("dp", "seq"), axis=0, tiled=True),
        lax.all_gather(w_down.astype(jnp.bfloat16), ("dp", "seq"), axis=0, tiled=True),
        lax.all_gather(norm_attn.astype(jnp.bfloat16), ("dp", "seq"), axis=0, tiled=True),
        lax.all_gather(norm_mlp.astype(jnp.bfloat16), ("dp", "seq"), axis=0, tiled=True),
    )
    query_mat, key_mat, value_mat, out_mat, gate_mat, up_mat, down_mat, gain_attn, gain_mlp = (
        back_weights
    )
    gate_use = gate_mat
    up_use = up_mat
    down_use = down_mat
    grad_out = cotangent.astype(jnp.float32)
    grad_hidden = jnp.dot(cotangent, down_use, preferred_element_type=jnp.float32)
    grad_gate = (
        grad_hidden * up_pre * sigmoid_gate * (1.0 + gate_pre * (1.0 - sigmoid_gate))
    ).astype(jnp.bfloat16)
    grad_up = (grad_hidden * gate_pre * sigmoid_gate).astype(jnp.bfloat16)
    mid_part = lax.dot_general(
        grad_gate, gate_use, CONTRACT_LAST, preferred_element_type=jnp.float32
    ) + lax.dot_general(grad_up, up_use, CONTRACT_LAST, preferred_element_type=jnp.float32)
    grad_gain_mlp = jnp.sum(mid_part * normed_res, axis=0)
    grad_resid = grad_out + rms_back(mid_part * gain_two, normed_res, inverse_mlp)
    grad_branch = grad_resid.astype(jnp.bfloat16)
    grad_attended = lax.dot_general(
        grad_branch, out_mat, CONTRACT_LAST, preferred_element_type=jnp.float32
    )
    grad_out_mat = lax.dot_general(
        attended, grad_branch, CONTRACT_FIRST, preferred_element_type=jnp.float32
    )
    grad_heads = grad_attended.reshape(tok_rows, H, DV)
    grad_numer = grad_heads / denom[:, :, None]
    grad_denom = -jnp.sum(grad_heads * heads_out, axis=2) / denom
    grad_scores = (
        jnp.einsum("the,she->hts", grad_numer, value_wide, precision=PRECISE)
        + grad_denom.T[:, :, None]
    ) * allowed[None]
    grad_value = jnp.einsum("hts,the->she", scores, grad_numer, precision=PRECISE)
    grad_fquery = jnp.einsum("hts,shf->thf", grad_scores, key_wide, precision=PRECISE)
    grad_fkey = jnp.einsum("hts,thf->shf", grad_scores, query_wide, precision=PRECISE)
    grad_fquery = grad_fquery + use_in[:, None, None] * (
        jnp.einsum("the,hfe->thf", grad_numer, carry_state, precision=PRECISE)
        + grad_denom[:, :, None] * carry_norm[None]
    )
    first_key = doc_ids[0]
    first_sel = (doc_ids == first_key).astype(jnp.float32)
    query_first = query_wide * first_sel[:, None, None]
    back_state = jnp.einsum("thf,the->hfe", query_first, grad_numer, precision=PRECISE)
    back_norm = jnp.einsum("thf,th->hf", query_first, grad_denom, precision=PRECISE)
    later_state, later_norm, later_key = carry_backward(
        back_state, back_norm, first_key.astype(jnp.float32)
    )
    use_out = (doc_ids.astype(jnp.float32) == later_key).astype(jnp.float32)
    grad_fkey = grad_fkey + use_out[:, None, None] * (
        jnp.einsum("she,hfe->shf", value_wide, later_state, precision=PRECISE) + later_norm[None]
    )
    grad_value = grad_value + use_out[:, None, None] * jnp.einsum(
        "shf,hfe->she", key_wide, later_state, precision=PRECISE
    )
    grad_query = (
        feature_grad(grad_fquery, query_heads).reshape(tok_rows, H * F).astype(jnp.bfloat16)
    )
    grad_key = feature_grad(grad_fkey, key_heads).reshape(tok_rows, H * F).astype(jnp.bfloat16)
    grad_values = grad_value.reshape(tok_rows, D).astype(jnp.bfloat16)
    grad_normed = lax.dot_general(
        grad_query, query_mat, CONTRACT_LAST, preferred_element_type=jnp.float32
    )
    grad_normed = grad_normed + lax.dot_general(
        grad_key, key_mat, CONTRACT_LAST, preferred_element_type=jnp.float32
    )
    grad_normed = grad_normed + lax.dot_general(
        grad_values, value_mat, CONTRACT_LAST, preferred_element_type=jnp.float32
    )
    grad_gain_attn = jnp.sum(grad_normed * normed_attn, axis=0)
    grad_tokens = grad_resid + rms_back(grad_normed * gain_one, normed_attn, inverse_attn)
    grad_query_mat = lax.dot_general(
        normed_in, grad_query, CONTRACT_FIRST, preferred_element_type=jnp.float32
    )
    grad_key_mat = lax.dot_general(
        normed_in, grad_key, CONTRACT_FIRST, preferred_element_type=jnp.float32
    )
    grad_value_mat = lax.dot_general(
        normed_in, grad_values, CONTRACT_FIRST, preferred_element_type=jnp.float32
    )
    attn_grads = (
        lax.psum_scatter(grad_query_mat, ("dp", "seq"), scatter_dimension=0, tiled=True),
        lax.psum_scatter(grad_key_mat, ("dp", "seq"), scatter_dimension=0, tiled=True),
        lax.psum_scatter(grad_value_mat, ("dp", "seq"), scatter_dimension=0, tiled=True),
        lax.psum_scatter(grad_out_mat, ("dp", "seq"), scatter_dimension=0, tiled=True),
        lax.psum_scatter(grad_gain_attn, ("dp", "seq"), scatter_dimension=0, tiled=True),
        lax.psum_scatter(grad_gain_mlp, ("dp", "seq"), scatter_dimension=0, tiled=True),
    )
    mlp_grads = lax.psum_scatter(
        jnp.concatenate(
            [
                lax.dot_general(
                    normed_mid, grad_gate, CONTRACT_FIRST, preferred_element_type=jnp.float32
                ),
                lax.dot_general(
                    normed_mid, grad_up, CONTRACT_FIRST, preferred_element_type=jnp.float32
                ),
                lax.dot_general(
                    cotangent, hidden, CONTRACT_FIRST, preferred_element_type=jnp.float32
                ),
            ],
            axis=1,
        ),
        ("dp", "seq"),
        scatter_dimension=0,
        tiled=True,
    )
    grad_gate_mat = mlp_grads[:, :FF]
    grad_up_mat = mlp_grads[:, FF : 2 * FF]
    grad_down_mat = mlp_grads[:, 2 * FF :]
    return (
        output,
        grad_tokens,
        attn_grads[0],
        attn_grads[1],
        attn_grads[2],
        attn_grads[3],
        grad_gate_mat,
        grad_up_mat,
        grad_down_mat,
        attn_grads[4],
        attn_grads[5],
    )


def solution(mesh):
    placed = (
        P(("dp", "seq"), None),
        P("dp", "seq"),
        P(("dp", "seq"), None),
        P(("dp", "seq"), None),
        P(("dp", "seq"), None),
        P(("dp", "seq"), None),
        P(("dp", "seq"), None),
        P(("dp", "seq"), None),
        P(("dp", "seq"), None),
        P(("dp", "seq"), None),
        P(("dp", "seq")),
        P(("dp", "seq")),
    )
    return jax.shard_map(
        per_device,
        mesh=mesh,
        in_specs=placed,
        out_specs=(
            P(("dp", "seq"), None),
            P(("dp", "seq"), None),
            P(("dp", "seq"), None),
            P(("dp", "seq"), None),
            P(("dp", "seq"), None),
            P(("dp", "seq"), None),
            P(("dp", "seq"), None),
            P(("dp", "seq"), None),
            P(("dp", "seq"), None),
            P(("dp", "seq")),
            P(("dp", "seq")),
        ),
        check_vma=False,
    )
```

profile of v0, /device:TPU:0, one launch (start us, length us, event | category | flops | bytes accessed | tf_op | source)
XLA Modules:
  0.0 2790.6 jit_solution(16920956075847574219)
XLA Ops:
  19.4 42.2 %all-reduce.7 = (bf16[2048]{0:T(1024)(128)(2,1)S(1)}, bf16[2048]{0:T(1024)(128)(2,1)S(1)}) all-reduce(bf16[2048]{0:T(1024)(128)(2,1)S(1)} %dynamic-update-slice, bf16[2048]{0:T(1024)(128)(2,1)S(1)} %dynamic-update-slice.2), channel_id=1, replica_groups=mesh['dp'=8,'seq'=4] {'dp','seq'}, use_global_device_ids=true, to_apply=%add | all-reduce | flops 4096 | bytes 16384
  73.8 74.5 %all-gather.14.cloned.1.call-done = bf16[2048,2048]{1,0:T(8,128)(2,1)} async-done(((bf16[64,2048]{1,0:T(8,128)(2,1)}), bf16[2048,2048]{1,0:T(8,128)(2,1)}) %all-gather.14.cloned.1.call-update) | async-done | bytes 8388624 | tf_op jit(solution)/shard_map/all_gather | solution.py:138
  183.3 20.8 all-gather.16.cloned.1.call-done
  215.0 26.7 all-gather.28.cloned.1.call-done
  252.0 9.5 bitcast_divide_fusion.1
  261.5 60.6 %all-gather.20.cloned.1.call-done = bf16[2048,2048]{1,0:T(8,128)(2,1)} async-done(((bf16[64,2048]{1,0:T(8,128)(2,1)}), bf16[2048,2048]{1,0:T(8,128)(2,1)}) %all-gather.20.cloned.1.call-update) | async-done | bytes 8388624 | tf_op jit(solution)/shard_map/all_gather | solution.py:139
  330.1 135.9 %all-gather.24.cloned.1.call-done = bf16[2048,5504]{1,0:T(8,128)(2,1)} async-done(((bf16[64,5504]{1,0:T(8,128)(2,1)}), bf16[2048,5504]{1,0:T(8,128)(2,1)}) %all-gather.24.cloned.1.call-update) | async-done | bytes 22544400 | tf_op jit(solution)/shard_map/all_gather | solution.py:141
  466.0 14.9 fusion.106
  480.9 128.8 %all-gather.22.cloned.1.call-done = bf16[2048,5504]{1,0:T(8,128)(2,1)} async-done(((bf16[64,5504]{1,0:T(8,128)(2,1)}), bf16[2048,5504]{1,0:T(8,128)(2,1)}) %all-gather.22.cloned.1.call-update) | async-done | bytes 22544400 | tf_op jit(solution)/shard_map/all_gather | solution.py:140
  609.7 14.8 fusion.105
  624.5 128.3 %all-gather.26.cloned.1.call-done = bf16[2048,5504]{1,0:T(8,128)(2,1)} async-done(((bf16[64,5504]{1,0:T(8,128)(2,1)}), bf16[2048,5504]{1,0:T(8,128)(2,1)}) %all-gather.26.cloned.1.call-update) | async-done | bytes 22544400 | tf_op jit(solution)/shard_map/all_gather | solution.py:142
  752.8 21.1 multiply_convert_fusion
  773.9 20.0 fusion.110
  793.9 19.9 fusion.109
  813.8 14.4 fusion.107
  828.2 15.3 multiply_reduce_fusion.5
  863.3 23.4 convolution_bitcast_fusion
  886.7 86.7 %pad_maximum_fusion = f32[2048,16512]{1,0:T(8,128)} fusion(f32[2048,5504]{1,0:T(8,128)} %convolution_bitcast_fusion, f32[2048,5504]{1,0:T(8,128)} %fusion.110, f32[2048,5504]{1,0:T(8,128)} %fusion.109), kind=kLoop, calls=%fused_computation.12 | loop fusion | flops 67633152 | bytes 270532608 | tf_op jit(solution)/shard_map/concatenate | solution.py:310
  993.1 10.1 fusion.5
  1003.2 11.3 fusion.11
  1021.5 18.3 fusion.4
  1040.5 14.3 while.31
  1069.1 16.0 fusion.55
  1092.3 11.2 fusion.47
  1104.6 10.3 fusion.51
  1118.5 18.0 fusion.29
  1145.7 38.7 %all-reduce.6 = (f32[2048]{0:T(1024)S(1)}, f32[2048]{0:T(1024)S(1)}) all-reduce(f32[2048]{0:T(1024)S(1)} %get-tuple-element.186, f32[2048]{0:T(1024)S(1)} %copy-done.63), channel_id=11, replica_groups=mesh['dp'=8,'seq'=4] {'dp','seq'}, use_global_device_ids=true, to_apply=%region_16.17.clone | all-reduce | flops 4096 | bytes 32768
  1191.1 948.7 %reduce-scatter.14.cloned.1.call-done = f32[64,16512]{1,0:T(8,128)} async-done(((f32[2048,16512]{1,0:T(8,128)}), f32[64,16512]{1,0:T(8,128)}) %reduce-scatter.14.cloned.1.call-update) | async-done | bytes 4227088 | tf_op jit(solution)/shard_map/reduce_scatter | solution.py:309
  2144.1 135.0 %reduce-scatter.6.cloned.1.call-done = f32[64,256]{1,0:T(8,128)} async-done(((f32[2048,256]{1,0:T(8,128)}), f32[64,256]{1,0:T(8,128)}) %reduce-scatter.6.cloned.1.call-update) | async-done | bytes 65552 | tf_op jit(solution)/shard_map/reduce_scatter | solution.py:302
  2279.1 135.5 %reduce-scatter.8.cloned.1.call-done = f32[64,256]{1,0:T(8,128)} async-done(((f32[2048,256]{1,0:T(8,128)}), f32[64,256]{1,0:T(8,128)}) %reduce-scatter.8.cloned.1.call-update) | async-done | bytes 65552 | tf_op jit(solution)/shard_map/reduce_scatter | solution.py:303
  2414.6 181.8 %reduce-scatter.12.cloned.1.call-done = f32[64,2048]{1,0:T(8,128)} async-done(((f32[2048,2048]{1,0:T(8,128)}), f32[64,2048]{1,0:T(8,128)}) %reduce-scatter.12.cloned.1.call-update) | async-done | bytes 524304 | tf_op jit(solution)/shard_map/reduce_scatter | solution.py:305
  2596.4 187.3 %reduce-scatter.10.cloned.1.call-done = f32[64,2048]{1,0:T(8,128)} async-done(((f32[2048,2048]{1,0:T(8,128)}), f32[64,2048]{1,0:T(8,128)}) %reduce-scatter.10.cloned.1.call-update) | async-done | bytes 524304 | tf_op jit(solution)/shard_map/reduce_scatter | solution.py:304
  (261 shorter events, 187.8 us)
Async XLA Ops:
  7.2 61.0 %all-gather.18.cloned.1.call-start = ((), (), s32[]{:S(2)}) async-start(), calls=%async_computation.7 | async-start | bytes 1081344 | tf_op jit(solution)/shard_map/all_gather | solution.py:137
  8.7 139.6 %all-gather.14.cloned.1.call-start = ((), (), s32[]{:S(2)}) async-start(), calls=%async_computation.5 | async-start | bytes 8650752 | tf_op jit(solution)/shard_map/all_gather | solution.py:138
  10.6 193.6 %all-gather.16.cloned.1.call-start = ((), (), s32[]{:S(2)}) async-start(), calls=%async_computation.6 | async-start | bytes 1081344 | tf_op jit(solution)/shard_map/all_gather | solution.py:136
  12.1 229.7 %all-gather.28.cloned.1.call-start = ((), (), s32[]{:S(2)}) async-start(), calls=%async_computation.17 | async-start | bytes 5591040 | tf_op jit(solution)/shard_map/all_gather | solution.py:26
  14.1 227.9 %copy-start.57 = (s32[320]{0:T(512)}, s32[320]{0:T(512)S(1)}, u32[]{:S(2)}) copy-start(s32[320]{0:T(512)S(1)} %reduce.4) | copy-start | bytes 3844
  17.7 186.5 %copy-start.51 = (f32[320]{0:T(512)}, f32[320]{0:T(512)S(1)}, u32[]{:S(2)}) copy-start(f32[320]{0:T(512)S(1)} %add_rsqrt_fusion.1) | copy-start | bytes 3844
  61.6 142.5 %copy-start.45 = (f32[2048]{0:T(1024)}, f32[2048]{0:T(1024)S(1)}, u32[]{:S(2)}) copy-start(f32[2048]{0:T(1024)S(1)} %convert_element_type.230) | copy-start | bytes 24580
  61.6 185.5 %copy-start.61 = (bf16[273]{0:T(512)(128)(2,1)}, bf16[273]{0:T(512)(128)(2,1)S(1)}, u32[]{:S(2)}) copy-start(bf16[273]{0:T(512)(128)(2,1)S(1)} %pad.6.clone) | copy-start | bytes 1642
  61.6 86.7 %copy-start.3 = (bf16[320,2048]{1,0:T(8,128)(2,1)S(1)}, bf16[320,2048]{1,0:T(8,128)(2,1)}, u32[]{:S(2)}) copy-start(bf16[320,2048]{1,0:T(8,128)(2,1)} %param.16) | copy-start | bytes 3932164
  70.6 136.7 %copy-start.47 = (bf16[320,16,16]{0,2,1:T(8,128)(2,1)}, bf16[320,16,16]{0,2,1:T(8,128)(2,1)S(1)}, u32[]{:S(2)}) copy-start(bf16[320,16,16]{0,2,1:T(8,128)(2,1)S(1)} %get-tuple-element.237) | copy-start | bytes 491524
  157.8 164.3 %all-gather.20.cloned.1.call-start = ((), (), s32[]{:S(2)}) async-start(), calls=%async_computation.8 | async-start | bytes 8650752 | tf_op jit(solution)/shard_map/all_gather | solution.py:139
  158.6 307.4 %all-gather.24.cloned.1.call-start = ((), (), s32[]{:S(2)}) async-start(), calls=%async_computation.10 | async-start | bytes 23248896 | tf_op jit(solution)/shard_map/all_gather | solution.py:141
  159.6 450.1 %all-gather.22.cloned.1.call-start = ((), (), s32[]{:S(2)}) async-start(), calls=%async_computation.9 | async-start | bytes 23248896 | tf_op jit(solution)/shard_map/all_gather | solution.py:140
  162.0 590.7 %all-gather.26.cloned.1.call-start = ((), (), s32[]{:S(2)}) async-start(), calls=%async_computation.11 | async-start | bytes 23248896 | tf_op jit(solution)/shard_map/all_gather | solution.py:142
  163.1 876.8 %all-gather.30.cloned.1.call-start = ((), (), s32[]{:S(2)}) async-start(), calls=%async_computation.18 | async-start | bytes 5591040 | tf_op jit(solution)/shard_map/all_gather | solution.py:26
  174.2 77.7 %copy-start.23 = (f32[320,320]{0,1:T(8,128)}, f32[320,320]{0,1:T(8,128)S(1)}, u32[]{:S(2)}) copy-start(f32[320,320]{0,1:T(8,128)S(1)} %fusion.74) | copy-start | bytes 1228804
  206.3 40.8 %copy-start.49 = (bf16[320,16,16]{0,2,1:T(8,128)(2,1)}, bf16[320,16,16]{0,2,1:T(8,128)(2,1)S(1)}, u32[]{:S(2)}) copy-start(bf16[320,16,16]{0,2,1:T(8,128)(2,1)S(1)} %get-tuple-element.239) | copy-start | bytes 491524
  215.0 32.1 %copy-start.53 = (f32[16,320]{1,0:T(8,128)}, f32[16,320]{1,0:T(8,128)S(1)}, u32[]{:S(2)}) copy-start(f32[16,320]{1,0:T(8,128)S(1)} %get-tuple-element.241) | copy-start | bytes 61444
  252.0 70.1 %copy-start.4 = (bf16[320,2048]{1,0:T(8,128)(2,1)S(1)}, bf16[320,2048]{1,0:T(8,128)(2,1)}, u32[]{:S(2)}) copy-start(bf16[320,2048]{1,0:T(8,128)(2,1)} %param.16) | copy-start | bytes 3932164
  480.9 271.9 %copy-start.35 = (bf16[320,2048]{1,0:T(8,128)(2,1)S(1)}, bf16[320,2048]{1,0:T(8,128)(2,1)}, u32[]{:S(2)}) copy-start(bf16[320,2048]{1,0:T(8,128)(2,1)} %param.18) | copy-start | bytes 3932164
  813.8 14.4 copy-start.20
  853.0 150.2 %copy-start.8 = (f32[40,16,8,128]{3,2,1,0:T(8,128)}, f32[40,16,8,128]{3,2,1,0:T(8,128)S(1)}, u32[]{:S(2)}) copy-start(f32[40,16,8,128]{3,2,1,0:T(8,128)S(1)} %convolution_bitcast_fusion.1) | copy-start | bytes 7864324
  863.3 1276.6 %reduce-scatter.14.cloned.1.call-start = ((), (), s32[]{:S(2)}) async-start(), calls=%async_computation.16 | async-start | bytes 139493376 | tf_op jit(solution)/shard_map/reduce_scatter | solution.py:309
  973.4 1305.7 %reduce-scatter.6.cloned.1.call-start = ((), (), s32[]{:S(2)}) async-start(), calls=%async_computation.12 | async-start | bytes 2162688 | tf_op jit(solution)/shard_map/reduce_scatter | solution.py:302
  976.5 13.0 copy-start.54
  976.5 12.9 copy-start.56
  976.5 12.9 copy-start.32
  1039.8 1374.8 %reduce-scatter.8.cloned.1.call-start = ((), (), s32[]{:S(2)}) async-start(), calls=%async_computation.13 | async-start | bytes 2162688 | tf_op jit(solution)/shard_map/reduce_scatter | solution.py:303
  1040.5 14.3 copy-start.58
  1069.1 1527.3 %reduce-scatter.12.cloned.1.call-start = ((), (), s32[]{:S(2)}) async-start(), calls=%async_computation.15 | async-start | bytes 17301504 | tf_op jit(solution)/shard_map/reduce_scatter | solution.py:305
  1085.1 1698.5 %reduce-scatter.10.cloned.1.call-start = ((), (), s32[]{:S(2)}) async-start(), calls=%async_computation.14 | async-start | bytes 17301504 | tf_op jit(solution)/shard_map/reduce_scatter | solution.py:304
  1118.5 18.0 copy-start.34
  (49 other events, 242.8 us)
Sparse Core Ops, SparseCore 0:
  11.5 56.6 all-gather.17
  71.6 76.7 all-gather.13
  151.8 52.2 all-gather.15
  206.1 35.6 all-gather.27
  244.5 77.5 all-gather.19
  325.3 140.6 all-gather.23
  469.4 140.2 all-gather.21
  612.5 140.2 all-gather.25
  863.4 34.8 all-gather.29
  973.6 1166.2 reduce-scatter.13
  2142.7 136.4 reduce-scatter.5
  2281.9 132.6 reduce-scatter.7
  2417.4 178.9 reduce-scatter.11
  2599.1 184.5 reduce-scatter.9
where the time goes:
time: 2800 us; the launch traced here: 2790 us
  waiting for transfers between devices  2170 us (78%)
  matrix products  344 us (12%)
  other arithmetic  126 us (4%)
  blocking collectives  99.3 us (4%)
    reduce_scatter x1, waiting for transfers between devices, per_device(): lax.psum_scatter(jnp.concatenate([lax.dot_general(normed_mid, grad_gate,...  949 us
    reduce_scatter x1, waiting for transfers between devices, per_device(): lax.psum_scatter(grad_value_mat, ('dp', 'seq'), scatter_dimension=0, tile...  187 us
    reduce_scatter x1, waiting for transfers between devices, per_device(): lax.psum_scatter(grad_out_mat, ('dp', 'seq'), scatter_dimension=0, tiled=...  182 us
    all_gather x1, waiting for transfers between devices, per_device(): lax.all_gather(w_up.astype(jnp.bfloat16), ('dp', 'seq'), axis=0, tiled=True)  136 us
    reduce_scatter x1, waiting for transfers between devices, per_device(): lax.psum_scatter(grad_key_mat, ('dp', 'seq'), scatter_dimension=0, tiled=...  135 us
    reduce_scatter x1, waiting for transfers between devices, per_device(): lax.psum_scatter(grad_query_mat, ('dp', 'seq'), scatter_dimension=0, tile...  135 us
    all_gather x1, waiting for transfers between devices, per_device(): lax.all_gather(w_gate.astype(jnp.bfloat16), ('dp', 'seq'), axis=0, tiled=...  129 us
    all_gather x1, waiting for transfers between devices, per_device(): lax.all_gather(w_down.astype(jnp.bfloat16), ('dp', 'seq'), axis=0, tiled=...  128 us
  transfers between devices with their start and end apart: 14, of which 13 were waited for; matrix products, arithmetic and copies ran while one was open for 14% of the time, Pallas kernels for 0%

commit v1 on v0

v1 whole, which is shorter than its diff:
```python
import jax
import jax.numpy as jnp
from jax import lax
from jax.sharding import Mesh
from jax.sharding import PartitionSpec as P

HEADS = 16
EPSILON = 1e-06
BF = jnp.bfloat16
F32 = jnp.float32


def index(ax):
    return lax.axis_index(ax)


def shift(v, ax, k=1):
    n = lax.axis_size(ax)
    return lax.ppermute(v, ax, [(i, (i + k) % n) for i in range(n)])


def absolute(rel, ax):
    n = len(rel)
    if n == 1:
        return list(rel)
    i = index(ax)
    out = []
    for j in range(n):
        picked = rel[0]
        for k in range(1, n):
            picked = jnp.where((i - j + n) % n == k, rel[k], picked)
        out.append(picked)
    return out


def ring(v, ax):
    out = [v]
    for _ in range(lax.axis_size(ax) - 1):
        out.append(shift(out[-1], ax))
    return out


def ring_sum(pieces, ax):
    acc = None
    for k in range(len(pieces) - 1, 0, -1):
        term = pieces[k].astype(F32)
        if acc is not None:
            term = term + acc
        acc = shift(term.astype(BF), ax, -1).astype(F32)
    own = pieces[0].astype(F32)
    return own if acc is None else own + acc


def gather_abs(v, axes):
    for ax in reversed(axes):
        v = jnp.concatenate(absolute(ring(v, ax), ax), axis=0)
    return v


def spread_columns(w, ax):
    n = lax.axis_size(ax)
    if n == 1:
        return w
    i = index(ax)
    width = w.shape[1] // n
    rel = []
    for k in range(n):
        block = lax.dynamic_slice_in_dim(w, ((i + k) % n) * width, width, 1)
        rel.append(block if k == 0 else shift(block, ax, k))
    return jnp.concatenate(absolute(rel, ax), axis=0)


def join_columns(g, ax):
    n = lax.axis_size(ax)
    if n == 1:
        return g
    i = index(ax)
    height = g.shape[0] // n
    rel = []
    for k in range(n):
        block = lax.dynamic_slice_in_dim(g, ((i + k) % n) * height, height, 0)
        rel.append(block if k == 0 else shift(block, ax, k))
    return jnp.concatenate(absolute(rel, ax), axis=1)


def vector_sum_scatter(v, axes):
    for ax in axes:
        n = lax.axis_size(ax)
        if n == 1:
            continue
        i = index(ax)
        part = v.shape[0] // n
        acc = lax.dynamic_slice_in_dim(v, i * part, part, 0)
        for k in range(1, n):
            acc = acc + shift(lax.dynamic_slice_in_dim(v, ((i + k) % n) * part, part, 0), ax, k)
        v = acc
    return v


def wide_gather(v, both):
    if both:
        half = v.shape[0] // 2
        upper, lower = v[:half], v[half:]
        x_up, x_low = shift(upper, "x"), shift(lower, "x")
        y_low, y_up = shift(lower, "y"), shift(upper, "y")
        chip = [v, x_up, x_low, y_up, y_low, shift(x_up, "y"), shift(y_low, "x")]
    else:
        chip = ring(v, "y")
    other = [shift(piece, "c") for piece in chip]
    return jnp.concatenate(chip + other, axis=0)


def wide_sum(mine, theirs, rows, both):
    term = mine + shift(theirs, "c").astype(F32)
    if not both:
        n = lax.axis_size("y")
        return ring_sum([term[k * rows : (k + 1) * rows] for k in range(n)], "y")
    half = rows // 2
    own = term[:rows]
    x_up, x_low = term[rows : rows + half], term[rows + half : 2 * rows]
    y_up, y_low = term[2 * rows : 2 * rows + half], term[2 * rows + half : 3 * rows]
    d_up, d_low = term[3 * rows : 3 * rows + half], term[3 * rows + half :]

    def send(a, ax):
        return shift(a.astype(BF), ax).astype(F32)

    got_up = send(y_up, "y")
    got_low = send(x_low, "x")
    x_up = x_up + send(d_up, "y")
    y_low = y_low + send(d_low, "x")
    return jnp.concatenate(
        [own[:half] + got_up + send(x_up, "x"), own[half:] + got_low + send(y_low, "y")], axis=0
    )


def stream_sum(partial, rows):
    nc, ny = lax.axis_size("c"), lax.axis_size("y")
    c, y = index("c"), index("y")
    d = partial.shape[1]
    by = partial.reshape(ny, nc, rows, d)
    terms = []
    for k in range(nc):
        terms.append(lax.dynamic_index_in_dim(by, (c - k + nc) % nc, 1, False))
    term = ring_sum(terms, "c")
    pieces = [lax.dynamic_index_in_dim(term, (y - k + ny) % ny, 0, False) for k in range(ny)]
    return ring_sum(pieces, "y")


def dot(a, b, dims, out=F32):
    return lax.dot_general(a, b, (dims, ((), ())), preferred_element_type=F32).astype(out)


NN = ((1,), (0,))
NT = ((1,), (1,))
TN = ((0,), (0,))


def inverse_rms(v):
    return lax.rsqrt(jnp.mean(v * v, axis=-1, keepdims=True) + EPSILON)


def rms_back(grad, normed, inverse):
    return inverse * (grad - normed * jnp.mean(grad * normed, axis=-1, keepdims=True))


def attention(q, k, v, allowed):
    u = jnp.einsum("thf,shf->hts", q, k, preferred_element_type=F32)
    scores = jnp.where(allowed[None], 1.0 + u * 0.25 + u * u * (1.0 / 32.0), 0.0)
    den = jnp.sum(scores, axis=2).T
    num = jnp.einsum("hts,she->the", scores.astype(BF), v, preferred_element_type=F32)
    return num / den[:, :, None], den


def attention_back(q, k, v, allowed, out, den, grad):
    u = jnp.einsum("thf,shf->hts", q, k, preferred_element_type=F32)
    scores = jnp.where(allowed[None], 1.0 + u * 0.25 + u * u * (1.0 / 32.0), 0.0)
    dnum = grad / den[:, :, None]
    dden = -jnp.sum(grad * out, axis=2) / den
    dnum = dnum.astype(BF)
    ds = jnp.einsum("the,she->hts", dnum, v, preferred_element_type=F32) + dden.T[:, :, None]
    du = jnp.where(allowed[None], ds * (0.25 + u * (1.0 / 16.0)), 0.0).astype(BF)
    dv = jnp.einsum("hts,the->she", scores.astype(BF), dnum, preferred_element_type=F32)
    dq = jnp.einsum("hts,shf->thf", du, k, preferred_element_type=F32)
    dk = jnp.einsum("hts,thf->shf", du, q, preferred_element_type=F32)
    return dq, dk, dv


def per_device(both, tokens, segments, cotangent, wq, wk, wv, wo, wg, wu, wd, g1, g2):
    rows, d = tokens.shape
    everything = ("z", "x", "y", "c")
    nz, nx, ny, nc = (lax.axis_size(a) for a in everything)
    ns = ny * nc
    stream = rows * ns
    heads = HEADS // ns
    fk = wq.shape[1] // HEADS
    fv = wv.shape[1] // HEADS
    own = wq.shape[0]

    def by_block(w):
        return w.astype(BF).reshape(own, ns, w.shape[1] // ns)

    pack = jnp.concatenate([by_block(wq), by_block(wk), by_block(wv)], axis=2)
    width = pack.shape[2]
    pack = pack.reshape(own, ns * width)
    pack = spread_columns(spread_columns(pack, "c"), "y")
    pack = jnp.concatenate(absolute(ring(pack, "x"), "x"), axis=0)
    qkv_mat = lax.all_gather(pack, "z", axis=0, tiled=True)

    ndp = nz * nx
    perm = []
    for dp in range(ndp):
        for u in range(ns):
            c, y = u // ny, u % ny
            perm.append((u * ndp + dp, dp * ns + y * nc + c))
    out_mat = lax.ppermute(wo.astype(BF), everything, perm)
    out_mat = jnp.concatenate(absolute(ring(out_mat, "x"), "x"), axis=0)
    out_mat = lax.all_gather(out_mat, "z", axis=0, tiled=True)

    gains = gather_abs(jnp.stack([g1, g2], axis=1).astype(BF).astype(F32), everything)
    gain_one, gain_two = gains[:, 0][None], gains[:, 1][None]

    def spread(w):
        w = spread_columns(spread_columns(w.astype(BF), "c"), "y")
        if both:
            return lax.all_gather(spread_columns(w, "x"), "z", axis=0, tiled=True)
        return lax.all_gather(w, ("z", "x"), axis=0, tiled=True)

    gate_mat, up_mat, down_mat = spread(wg), spread(wu), spread(wd)

    x_all = gather_abs(tokens, ("y", "c")).astype(F32)
    doc = gather_abs(segments[0], ("y", "c"))
    inv_all = inverse_rms(x_all)
    normed_all = x_all * inv_all
    a_all = (normed_all * gain_one).astype(BF)
    qkv = dot(a_all, qkv_mat, NN, BF)
    q = qkv[:, : heads * fk].reshape(stream, heads, fk)
    k = qkv[:, heads * fk : 2 * heads * fk].reshape(stream, heads, fk)
    v = qkv[:, 2 * heads * fk :].reshape(stream, heads, fv)
    at = jnp.arange(stream)
    allowed = (doc[:, None] == doc[None, :]) & (at[None, :] <= at[:, None])
    o, den = attention(q, k, v, allowed)
    att = o.reshape(stream, heads * fv).astype(BF)
    branch = stream_sum(dot(att, out_mat, NN), rows)
    residual = tokens.astype(F32) + branch
    inv_mlp = inverse_rms(residual)
    normed_res = residual * inv_mlp
    b = (normed_res * gain_two).astype(BF)

    b_all = wide_gather(b, both)
    dy_all = wide_gather(cotangent, both)
    total = b_all.shape[0]
    mid = total // 2
    gate = dot(b_all, gate_mat, NN)
    up = dot(b_all, up_mat, NN)
    dh = dot(dy_all, down_mat, NN)
    sig = jax.nn.sigmoid(gate)
    hidden = (gate * sig * up).astype(BF)
    dgate = (dh * up * sig * (1.0 + gate * (1.0 - sig))).astype(BF)
    dup = (dh * gate * sig).astype(BF)

    def back(r0, r1):
        return dot(dgate[r0:r1], gate_mat, NT) + dot(dup[r0:r1], up_mat, NT)

    db = wide_sum(back(0, mid), back(mid, total).astype(BF), rows, both)
    grad_gate = dot(b_all, dgate, TN, BF)
    grad_up = dot(b_all, dup, TN, BF)
    grad_down = dot(dy_all, hidden, TN, BF)
    ffn = wide_sum(
        dot(hidden[:mid], down_mat, NT), dot(hidden[mid:], down_mat, NT, BF), rows, both
    )
    output = (residual + ffn).astype(BF)

    def finish(g):
        if both:
            g = lax.psum_scatter(g, "z", scatter_dimension=0, tiled=True)
            g = join_columns(g, "x")
        else:
            g = lax.psum_scatter(g, ("z", "x"), scatter_dimension=0, tiled=True)
        return join_columns(join_columns(g, "y"), "c").astype(F32)

    grad_wg, grad_wu, grad_wd = finish(grad_gate), finish(grad_up), finish(grad_down)

    grad_g2 = vector_sum_scatter(jnp.sum(db * normed_res, axis=0), everything)
    dr = cotangent.astype(F32) + rms_back(db * gain_two, normed_res, inv_mlp)

    dz_all = gather_abs(dr.astype(BF), ("y", "c"))
    dc = dot(dz_all, out_mat, NT).reshape(stream, heads, fv)
    grad_wo = dot(att, dz_all, TN, BF)
    dq, dk, dv = attention_back(q, k, v, allowed, o, den, dc)
    dqkv = jnp.concatenate(
        [
            dq.reshape(stream, heads * fk).astype(BF),
            dk.reshape(stream, heads * fk).astype(BF),
            dv.reshape(stream, heads * fv).astype(BF),
        ],
        axis=1,
    )
    grad_qkv = dot(a_all, dqkv, TN, BF)
    da_part = dot(dqkv, qkv_mat, NT)
    grad_g1 = vector_sum_scatter(jnp.sum(da_part * normed_all, axis=0), everything)
    da = stream_sum(da_part, rows)
    x_own = tokens.astype(F32)
    inv_own = inverse_rms(x_own)
    grad_tokens = dr + rms_back(da * gain_one, x_own * inv_own, inv_own)

    def sum_rows(g):
        g = lax.psum_scatter(g, "z", scatter_dimension=0, tiled=True)
        height = g.shape[0] // nx
        x = index("x")
        return ring_sum(
            [lax.dynamic_slice_in_dim(g, ((x - k + nx) % nx) * height, height, 0) for k in range(nx)],
            "x",
        ).astype(BF)

    grad_wo = lax.ppermute(sum_rows(grad_wo), everything, [(t, s) for s, t in perm]).astype(F32)
    grad_qkv = join_columns(join_columns(sum_rows(grad_qkv), "y"), "c").astype(F32)
    grad_qkv = grad_qkv.reshape(own, ns, width)
    grad_wq = grad_qkv[:, :, : heads * fk].reshape(wq.shape)
    grad_wk = grad_qkv[:, :, heads * fk : 2 * heads * fk].reshape(wk.shape)
    grad_wv = grad_qkv[:, :, 2 * heads * fk :].reshape(wv.shape)
    return (
        output,
        grad_tokens,
        grad_wq,
        grad_wk,
        grad_wv,
        grad_wo,
        grad_wg,
        grad_wu,
        grad_wd,
        grad_g1,
        grad_g2,
    )


def solution(mesh):
    n_dp, n_seq = mesh.shape["dp"], mesh.shape["seq"]
    nz = 4 if n_dp % 4 == 0 else n_dp
    nc = 2 if n_seq % 2 == 0 else 1
    nx, ny = n_dp // nz, n_seq // nc
    fine = Mesh(mesh.devices.reshape(nz, nx, ny, nc), ("z", "x", "y", "c"))
    both = nx == 2 and ny == 2
    all_rows = P(("z", "x", "y", "c"), None)
    vector = P(("z", "x", "y", "c"))
    placed = (
        (all_rows, P(("z", "x"), ("y", "c")), all_rows) + (all_rows,) * 7 + (vector, vector)
    )

    def run(*args):
        return per_device(both, *args)

    return jax.shard_map(
        run,
        mesh=fine,
        in_specs=placed,
        out_specs=(all_rows,) * 9 + (vector, vector),
        check_vma=False,
    )
```

time: 2800 us -> 901 us (0.32)
  waiting for transfers between devices: 2170 us -> 334 us
  matrix products: 344 us -> 225 us
  blocking collectives: 99.3 us -> 0 us
  starting transfers between devices: 0.75 us -> 99.3 us
  local copies, waits for them, and re-layouts: 26.6 us -> 119 us
  other arithmetic: 126 us -> 91 us
    reduce_scatter x5, waiting for transfers between devices: 1590 us -> 8.52 us  [the longest x2 8.49 us: sum_rows(): g = lax.psum_scatter(g, 'z', scatter_dimension=0, tiled=True)]
    all_gather x9 -> x5, waiting for transfers between devices: 582 us -> 0.03 us  [the longest x1 0.02 us: per_device(): qkv_mat = lax.all_gather(pack, 'z', axis=0, tiled=True)]
    ppermute x0 -> x96, waiting for transfers between devices: none -> 325 us  [the longest x94 325 us: shift(): return lax.ppermute(v, ax, [(i, (i + k) % n) for i in range(n)])]
    dot_general x36 -> x24, matrix products: 344 us -> 225 us  [the longest x18 167 us: dot(): lax.dot_general(a, b, (dims, ((), ())), preferred_element_type=F32)]
    ppermute x0 -> x96, starting transfers between devices: none -> 98.7 us  [the longest x94 94.4 us: shift(): return lax.ppermute(v, ax, [(i, (i + k) % n) for i in range(n)])]
    unnamed x3 -> x0, blocking collectives: 88.4 us -> none
    concatenate x1 -> x29, other arithmetic: 86.7 us -> 14.9 us  [the longest x11 5.15 us: spread_columns(): return jnp.concatenate(absolute(rel, ax), axis=0)]
    unnamed x145 -> x207, local copies, waits for them, and re-layouts: 11.7 us -> 70.1 us
  transfers between devices with their start and end apart: 14 -> 106, of which waited for: 13 -> 33; matrix products, arithmetic and copies ran while one was open for 14% -> 43% of each run, Pallas kernels for 0% -> 0%
where the time goes in v1:
time: 901 us; the launch traced here: 885 us
  waiting for transfers between devices  334 us (37%)
  matrix products  225 us (25%)
  local copies, waits for them, and re-layouts  119 us (13%)
  starting transfers between devices  99.3 us (11%)
  other arithmetic  91 us (10%)
  between operations  16.1 us (2%)
    ppermute x94, waiting for transfers between devices, shift(): return lax.ppermute(v, ax, [(i, (i + k) % n) for i in range(n)])  325 us
    dot_general x18, matrix products, dot(): lax.dot_general(a, b, (dims, ((), ())), preferred_element_type=F32)  167 us
    ppermute x94, starting transfers between devices, shift(): return lax.ppermute(v, ax, [(i, (i + k) % n) for i in range(n)])  94.4 us
    unnamed x207, local copies, waits for them, and re-layouts  70.1 us
    select_n x34, other arithmetic, absolute(): picked = jnp.where((i - j + n) % n == k, rel[k], picked)  26.8 us
  transfers between devices with their start and end apart: 106, of which 33 were waited for; matrix products, arithmetic and copies ran while one was open for 43% of the time, Pallas kernels for 0%

profile of v1, /device:TPU:0, one launch (start us, length us, event | category | flops | bytes accessed | tf_op | source)
XLA Modules:
  0.0 884.6 jit_solution(12333077920180057807)
XLA Ops:
  21.7 7.5 collective-permute-done.10
  63.7 11.0 %collective-permute-start.36 = (bf16[64,2752]{1,0:T(8,128)(2,1)}, bf16[64,2752]{1,0:T(8,128)(2,1)S(1)}, u32[]{:S(2)}, u32[]{:S(2)}) collective-permute-start(bf16[64,2752]{1,0:T(8,128)(2,1)} %copy.63), channel_id=1, source_target_pairs={{0,1},{1,0},{2,3},{3,2},{4,5},{5,4},{6,7},{7,6},{8,9},{9,8},{10,11... | collective-permute-start | bytes 1056776 | tf_op jit(solution)/shard_map/ppermute | solution.py:19
  124.0 61.8 %collective-permute-done.34 = bf16[128,1376]{0,1:T(8,128)(2,1)} collective-permute-done((bf16[128,1376]{0,1:T(8,128)(2,1)}, bf16[128,1376]{0,1:T(8,128)(2,1)}, u32[]{:S(2)}, u32[]{:S(2)}) %collective-permute-start.34) | collective-permute-done | bytes 352288 | tf_op jit(solution)/shard_map/ppermute | solution.py:19
  206.3 7.3 convolution_convert_fusion.5
  215.7 12.4 %fusion.3 = (f32[4,1280]{1,0:T(4,128)S(1)}, f32[4,1280,1280]{1,2,0:T(8,128)}) fusion(pred[1280,1280]{0,1:T(8,128)(4,1)S(1)} %copy-done.50, bf16[1280,4,16]{0,2,1:T(8,128)(2,1)S(1)} %bitcast.112, bf16[1280,4,16]{0,2,1:T(8,128)(2,1)S(1)} %bitcast.101), kind=kOutput, calls=%fused_computation.5 | convolution fusion | flops 255585280 | bytes 28200960 | tf_op jit(solution)/shard_map/thf,shf->hts/dot_general | solution.py:167
  228.1 13.7 %fusion.94 = (bf16[1280,4,128]{0,2,1:T(8,128)(2,1)}, f32[1280,4,128]{0,2,1:T(8,128)}) fusion(f32[1280,4]{0,1:T(4,128)S(1)} %bitcast.124, bf16[1280,4,128]{0,2,1:T(8,128)(2,1)S(1)} %bitcast.107, f32[4,1280,1280]{1,2,0:T(8,128)} %get-tuple-element.155, pred[1280,1280]{0,1:T(8,128)(4,1)S(1)} %copy-done.50), kind=kOutput, calls=%fused_computation.347 | convolution fusion | flops 1724907520 | bytes 33116160 | tf_op jit(solution)/shard_map/hts,she->the/dot_general | solution.py:170
  266.5 17.1 %collective-permute-done.32 = bf16[256,688]{0,1:T(8,128)(2,1)S(1)} collective-permute-done((bf16[256,688]{0,1:T(8,128)(2,1)S(1)}, bf16[256,688]{0,1:T(8,128)(2,1)S(1)}, u32[]{:S(2)}, u32[]{:S(2)}) %collective-permute-start.32) | collective-permute-done | bytes 352288 | tf_op jit(solution)/shard_map/ppermute | solution.py:19
  304.5 23.8 %collective-permute-done.16 = bf16[320,2048]{1,0:T(8,128)(2,1)S(1)} collective-permute-done((bf16[320,2048]{1,0:T(8,128)(2,1)S(1)}, bf16[320,2048]{1,0:T(8,128)(2,1)S(1)}, u32[]{:S(2)}, u32[]{:S(2)}) %collective-permute-start.16) | collective-permute-done | bytes 1310752 | tf_op jit(solution)/shard_map/ppermute | solution.py:19
  335.7 13.3 %fusion.98 = f32[2560,688]{0,1:T(8,128)} fusion(bf16[2560,2048]{1,0:T(8,128)(2,1)} %constant_dynamic-update-slice_fusion.14, bf16[2048,688]{0,1:T(8,128)(2,1)} %all-gather.14.cloned.1.call-done), kind=kOutput, calls=%fused_computation.351 | convolution fusion | flops 7214202880 | bytes 20348928 | tf_op jit(solution)/shard_map/dot_general | solution.py:150
  349.5 14.1 %collective-permute-done.17 = bf16[160,2048]{1,0:T(8,128)(2,1)} collective-permute-done((bf16[160,2048]{1,0:T(8,128)(2,1)S(1)}, bf16[160,2048]{1,0:T(8,128)(2,1)}, u32[]{:S(2)}, u32[]{:S(2)}) %collective-permute-start.17) | collective-permute-done | bytes 655392 | tf_op jit(solution)/shard_map/ppermute | solution.py:19
  371.4 9.7 %collective-permute-done.21 = bf16[160,2048]{1,0:T(8,128)(2,1)S(1)} collective-permute-done((bf16[160,2048]{1,0:T(8,128)(2,1)}, bf16[160,2048]{1,0:T(8,128)(2,1)S(1)}, u32[]{:S(2)}, u32[]{:S(2)}) %collective-permute-start.21) | collective-permute-done | bytes 655392 | tf_op jit(solution)/shard_map/ppermute | solution.py:19
  390.6 12.9 %fusion.97 = f32[2560,688]{0,1:T(8,128)} fusion(bf16[2560,2048]{1,0:T(8,128)(2,1)} %constant_dynamic-update-slice_fusion, bf16[2048,688]{0,1:T(8,128)(2,1)} %all-gather.12.cloned.1.call-done), kind=kOutput, calls=%fused_computation.350 | convolution fusion | flops 7214202880 | bytes 20348928 | tf_op jit(solution)/shard_map/dot_general | solution.py:150
  403.5 17.9 %multiply_convert_fusion.1 = (bf16[2560,688]{0,1:T(8,128)(2,1)S(1)}, bf16[2560,688]{0,1:T(8,128)(2,1)S(1)}, bf16[2560,688]{0,1:T(8,128)(2,1)}) fusion(f32[2560,688]{0,1:T(8,128)} %fusion.98, f32[2560,688]{0,1:T(8,128)} %fusion.97, bf16[2560,2048]{1,0:T(8,128)(2,1)} %constant_dynamic-update-slice_fusion, bf16[2048,688]{0,1:T(8,128)(2,1)} %all-gather.10.cloned.1.call-done), kind=kOutput, calls=%fused_computation.19 | convolution fusion | flops 7242383360 | bytes 37961728 | tf_op jit(solution)/shard_map/dot_general | solution.py:150
  423.1 11.9 %convolution_convert_fusion.1 = bf16[2048,688]{0,1:T(8,128)(2,1)} fusion(bf16[2560,688]{0,1:T(8,128)(2,1)S(1)} %get-tuple-element.53, bf16[2560,2048]{1,0:T(8,128)(2,1)} %constant_dynamic-update-slice_fusion.14), kind=kOutput, calls=%fused_computation.35 | convolution fusion | flops 7215611904 | bytes 16826368 | tf_op jit(solution)/shard_map/dot_general | solution.py:150
  435.1 12.3 %convolution_convert_fusion.2 = bf16[2048,688]{0,1:T(8,128)(2,1)} fusion(bf16[2560,688]{0,1:T(8,128)(2,1)} %get-tuple-element.54, bf16[2560,2048]{1,0:T(8,128)(2,1)} %constant_dynamic-update-slice_fusion), kind=kOutput, calls=%fused_computation.36 | convolution fusion | flops 7215611904 | bytes 16826368 | tf_op jit(solution)/shard_map/dot_general | solution.py:150
  447.5 6.9 fusion.28
  454.4 6.6 add_convert_fusion
  467.5 11.3 %convolution_convert_fusion.3 = bf16[2048,688]{0,1:T(8,128)(2,1)} fusion(bf16[2560,688]{0,1:T(8,128)(2,1)S(1)} %get-tuple-element.52, bf16[2560,2048]{1,0:T(8,128)(2,1)} %constant_dynamic-update-slice_fusion), kind=kOutput, calls=%fused_computation.37 | convolution fusion | flops 7215611904 | bytes 16826368 | tf_op jit(solution)/shard_map/dot_general | solution.py:150
  480.6 8.7 fusion.31
  489.3 12.1 %fusion.95 = (bf16[1280,2048]{1,0:T(8,128)(2,1)S(1)}, f32[1280,2048]{1,0:T(8,128)S(1)}) fusion(bf16[1280,2048]{1,0:T(8,128)(2,1)} %collective-permute-done.59, f32[1280,2048]{1,0:T(8,128)} %fusion.31, bf16[2048,688]{0,1:T(8,128)(2,1)} %all-gather.10.cloned.1.call-done, bf16[2560,688]{0,1:T(8,128)(2,1)} %copy-done.37), kind=kOutput, calls=%fused_computation.348 | convolution fusion | flops 3617587200 | bytes 36036608 | tf_op jit(solution)/shard_map/dot_general | solution.py:150
  505.3 10.9 %fusion.96 = (bf16[1280,2048]{1,0:T(8,128)(2,1)S(1)}, f32[1280,2048]{1,0:T(8,128)}) fusion(bf16[1280,2048]{1,0:T(8,128)(2,1)} %collective-permute-done.39, bf16[2048,688]{0,1:T(8,128)(2,1)S(1)} %copy-done.80, bf16[2560,688]{0,1:T(8,128)(2,1)} %copy-done.84), kind=kOutput, calls=%fused_computation.349 | convolution fusion | flops 3614965760 | bytes 25550848 | tf_op jit(solution)/shard_map/dot_general | solution.py:150
  524.9 10.5 %collective-permute-done.41 = bf16[160,2048]{1,0:T(8,128)(2,1)} collective-permute-done((bf16[160,2048]{1,0:T(8,128)(2,1)}, bf16[160,2048]{1,0:T(8,128)(2,1)}, u32[]{:S(2)}, u32[]{:S(2)}) %collective-permute-start.41) | collective-permute-done | bytes 655392 | tf_op jit(solution)/shard_map/ppermute | solution.py:19
  539.6 9.8 %collective-permute-done.60 = bf16[160,2048]{1,0:T(8,128)(2,1)S(1)} collective-permute-done((bf16[160,2048]{1,0:T(8,128)(2,1)}, bf16[160,2048]{1,0:T(8,128)(2,1)S(1)}, u32[]{:S(2)}, u32[]{:S(2)}) %collective-permute-start.60) | collective-permute-done | bytes 655392 | tf_op jit(solution)/shard_map/ppermute | solution.py:19
  567.3 26.4 %collective-permute-done.42 = bf16[160,2048]{1,0:T(8,128)(2,1)} collective-permute-done((bf16[160,2048]{1,0:T(8,128)(2,1)}, bf16[160,2048]{1,0:T(8,128)(2,1)}, u32[]{:S(2)}, u32[]{:S(2)}) %collective-permute-start.42) | collective-permute-done | bytes 655392 | tf_op jit(solution)/shard_map/ppermute | solution.py:19
  601.6 6.1 collective-permute-done.43
  643.6 57.1 %collective-permute-done.76 = bf16[128,1376]{0,1:T(8,128)(2,1)} collective-permute-done((bf16[128,1376]{0,1:T(8,128)(2,1)}, bf16[128,1376]{0,1:T(8,128)(2,1)}, u32[]{:S(2)}, u32[]{:S(2)}) %collective-permute-start.76) | collective-permute-done | bytes 352288 | tf_op jit(solution)/shard_map/ppermute | solution.py:19
  717.3 13.5 %convolution_convert_fusion.6 = bf16[4,128,1280]{2,1,0:T(8,128)(2,1)} fusion(f32[1280,4,128]{0,2,1:T(8,128)} %bitcast.127, f32[1280,4]{0,1:T(4,128)S(1)} %bitcast.125, f32[4,1280,1280]{1,2,0:T(8,128)} %get-tuple-element.155, pred[1280,1280]{0,1:T(8,128)(4,1)S(1)} %copy-done.51), kind=kOutput, calls=%fused_computation.45 | convolution fusion | flops 1725562880 | bytes 31805440 | tf_op jit(solution)/shard_map/hts,the->she/dot_general | solution.py:182
  730.9 12.8 %fusion.2 = bf16[4,1280,1280]{1,2,0:T(8,128)(2,1)S(1)} fusion(bf16[1280,4,128]{0,2,1:T(8,128)(2,1)} %bitcast.108, f32[4,1280,1280]{1,2,0:T(8,128)} %get-tuple-element.155, f32[4,1280]{1,0:T(4,128)S(1)} %bitcast_divide_fusion, pred[1280,1280]{0,1:T(8,128)(4,1)S(1)} %copy-done.51, f32[1280,4,128]{0,2,1:T(8,128)} %bitcast.128, f32[1280,4]{0,1:T(4,128)S(1)} %bitcast.126), kind=kOutput, calls=%fused_computation.3 | convolution fusion | flops 1718353920 | bytes 44933120 | tf_op jit(solution)/shard_map/the,she->hts/dot_general | solution.py:180
  750.3 6.5 convolution_convert_fusion.4
  768.9 9.3 %fusion.8 = (f32[2048]{0:T(1024)S(1)}, f32[1280,2048]{1,0:T(8,128)S(1)}) fusion(f32[1280]{0:T(1024)S(1)} %copy-done.75, bf16[640,2048]{1,0:T(8,128)(2,1)} %copy-done.13, bf16[640,2048]{1,0:T(8,128)(2,1)S(1)} %copy-done.12, bf16[2048,640]{1,0:T(8,128)(2,1)} %all-gather.6.cloned.1.call-done, bf16[1280,512]{0,1:T(8,128)(2,1)} %bitcast.129, ...), kind=kOutput, calls=%fused_computation.12 | convolution fusion | flops 3378706432 | bytes 20001792 | tf_op jit(solution)/shard_map/dot_general | solution.py:150
  816.5 25.1 %collective-permute-done.94 = f32[128]{0:T(128)S(1)} collective-permute-done((f32[128]{0:T(128)S(1)}, f32[128]{0:T(128)S(1)}, u32[]{:S(2)}, u32[]{:S(2)}) %collective-permute-start.94) | collective-permute-done | bytes 544 | tf_op jit(solution)/shard_map/ppermute | solution.py:19
  846.5 8.5 reduce-scatter.8.cloned.1.call-done
  (580 shorter events, 379.8 us)
Async XLA Ops:
  7.2 199.1 %all-gather.6.cloned.1.call-start = ((), (), s32[]{:S(2)}) async-start(), calls=%async_computation.5 | async-start | bytes 3276800 | tf_op jit(solution)/shard_map/all_gather | solution.py:207
  30.3 216.2 %all-gather.8.cloned.1.call-start = ((), (), s32[]{:S(2)}) async-start(), calls=%async_computation.6 | async-start | bytes 2621440 | tf_op jit(solution)/shard_map/all_gather | solution.py:217
  31.6 227.0 %collective-permute-start.49 = (bf16[160,2048]{1,0:T(8,128)(2,1)}, bf16[160,2048]{1,0:T(8,128)(2,1)}, u32[]{:S(2)}, u32[]{:S(2)}) collective-permute-start(bf16[160,2048]{1,0:T(8,128)(2,1)} %get-tuple-element.97), channel_id=1, source_target_pairs={{0,2},{2,0},{1,3},{3,1},{4,6},{6,4},{5,7},{7,5},{8,10},{10,8},{9,1... | collective-permute-start | bytes 1966088 | tf_op jit(solution)/shard_map/ppermute | solution.py:19
  33.0 223.6 %collective-permute-start.47 = (bf16[160,2048]{1,0:T(8,128)(2,1)}, bf16[160,2048]{1,0:T(8,128)(2,1)}, u32[]{:S(2)}, u32[]{:S(2)}) collective-permute-start(bf16[160,2048]{1,0:T(8,128)(2,1)} %get-tuple-element.97), channel_id=1, source_target_pairs={{0,4},{4,0},{1,5},{5,1},{2,6},{6,2},{3,7},{7,3},{8,12},{12,8},{9,1... | collective-permute-start | bytes 1966088 | tf_op jit(solution)/shard_map/ppermute | solution.py:19
  34.6 42.0 %collective-permute-start.11 = (s32[320]{0:T(512)S(1)}, s32[320]{0:T(512)S(1)}, u32[]{:S(2)}, u32[]{:S(2)}) collective-permute-start(s32[320]{0:T(512)S(1)} %reduce), channel_id=1, source_target_pairs={{0,1},{1,0},{2,3},{3,2},{4,5},{5,4},{6,7},{7,6},{8,9},{9,8},{10,11... | collective-permute-start | bytes 3848 | tf_op jit(solution)/shard_map/ppermute | solution.py:19
  76.5 259.1 %all-gather.14.cloned.1.call-start = ((), (), s32[]{:S(2)}) async-start(), calls=%async_computation.9 | async-start | bytes 3522560 | tf_op jit(solution)/shard_map/all_gather | solution.py:225
  111.4 279.2 %all-gather.12.cloned.1.call-start = ((), (), s32[]{:S(2)}) async-start(), calls=%async_computation.8 | async-start | bytes 3522560 | tf_op jit(solution)/shard_map/all_gather | solution.py:225
  118.1 80.6 %collective-permute-start.1 = (bf16[640,2048]{1,0:T(8,128)(2,1)}, bf16[640,2048]{1,0:T(8,128)(2,1)}, u32[]{:S(2)}, u32[]{:S(2)}) collective-permute-start(bf16[640,2048]{1,0:T(8,128)(2,1)} %pad_maximum_fusion.6), channel_id=1, source_target_pairs={{0,2},{2,0},{1,3},{3,1},{4,6},{6,4},{5,7},{7,5},{8,10},{10,8},{9,1... | collective-permute-start | bytes 7864328 | tf_op jit(solution)/shard_map/ppermute | solution.py:19
  119.7 66.0 %collective-permute-start.34 = (bf16[128,1376]{0,1:T(8,128)(2,1)}, bf16[128,1376]{0,1:T(8,128)(2,1)}, u32[]{:S(2)}, u32[]{:S(2)}) collective-permute-start(bf16[128,1376]{0,1:T(8,128)(2,1)} %fusion.57), channel_id=1, source_target_pairs={{0,2},{2,0},{1,3},{3,1},{4,6},{6,4},{5,7},{7,5},{8,10},{10,8},{9,1... | collective-permute-start | bytes 1056776 | tf_op jit(solution)/shard_map/ppermute | solution.py:19
  121.1 139.8 %collective-permute-start.48 = (bf16[160,2048]{1,0:T(8,128)(2,1)}, bf16[160,2048]{1,0:T(8,128)(2,1)}, u32[]{:S(2)}, u32[]{:S(2)}) collective-permute-start(bf16[160,2048]{1,0:T(8,128)(2,1)} %get-tuple-element.98), channel_id=1, source_target_pairs={{0,2},{2,0},{1,3},{3,1},{4,6},{6,4},{5,7},{7,5},{8,10},{10,8},{9,1... | collective-permute-start | bytes 1966088 | tf_op jit(solution)/shard_map/ppermute | solution.py:19
  195.8 57.7 %collective-permute-start.46 = (bf16[160,2048]{1,0:T(8,128)(2,1)}, bf16[160,2048]{1,0:T(8,128)(2,1)}, u32[]{:S(2)}, u32[]{:S(2)}) collective-permute-start(bf16[160,2048]{1,0:T(8,128)(2,1)} %get-tuple-element.98), channel_id=1, source_target_pairs={{0,4},{4,0},{1,5},{5,1},{2,6},{6,2},{3,7},{7,3},{8,12},{12,8},{9,1... | collective-permute-start | bytes 1966088 | tf_op jit(solution)/shard_map/ppermute | solution.py:19
  198.5 205.1 %all-gather.10.cloned.1.call-start = ((), (), s32[]{:S(2)}) async-start(), calls=%async_computation.7 | async-start | bytes 3522560 | tf_op jit(solution)/shard_map/all_gather | solution.py:225
  198.7 60.3 %collective-permute-start.31 = (bf16[128,1376]{0,1:T(8,128)(2,1)}, bf16[128,1376]{0,1:T(8,128)(2,1)}, u32[]{:S(2)}, u32[]{:S(2)}) collective-permute-start(bf16[128,1376]{0,1:T(8,128)(2,1)} %fusion.59), channel_id=1, source_target_pairs={{0,2},{2,0},{1,3},{3,1},{4,6},{6,4},{5,7},{7,5},{8,10},{10,8},{9,1... | collective-permute-start | bytes 1056776 | tf_op jit(solution)/shard_map/ppermute | solution.py:19
  253.5 39.0 %collective-permute-start.15 = (bf16[2,320,2048]{2,1,0:T(8,128)(2,1)}, bf16[2,320,2048]{2,1,0:T(8,128)(2,1)}, u32[]{:S(2)}, u32[]{:S(2)}) collective-permute-start(bf16[2,320,2048]{2,1,0:T(8,128)(2,1)} %fusion.22), channel_id=1, source_target_pairs={{0,1},{1,0},{2,3},{3,2},{4,5},{5,4},{6,7},{7,6},{8,9},{9,8},{10,11... | collective-permute-start | bytes 7864328 | tf_op jit(solution)/shard_map/ppermute | solution.py:19
  284.7 238.5 %reduce-scatter.14.cloned.1.call-start = ((), (), s32[]{:S(2)}) async-start(), calls=%async_computation.14 | async-start | bytes 3522560 | tf_op jit(solution)/shard_map/reduce_scatter | solution.py:275
  349.2 38.6 %collective-permute-start.27 = (bf16[160,2048]{1,0:T(8,128)(2,1)S(1)}, bf16[160,2048]{1,0:T(8,128)(2,1)S(1)}, u32[]{:S(2)}, u32[]{:S(2)}) collective-permute-start(bf16[160,2048]{1,0:T(8,128)(2,1)S(1)} %collective-permute-done.20), channel_id=1, source_target_pairs={{0,1},{1,0},{2,3},{3,2},{4,5},{5,4},{6,7},{7,6},{8,9},{9,8},{10,11... | collective-permute-start | bytes 1966088 | tf_op jit(solution)/shard_map/ppermute | solution.py:19
  435.0 120.8 %reduce-scatter.12.cloned.1.call-start = ((), (), s32[]{:S(2)}) async-start(), calls=%async_computation.13 | async-start | bytes 3522560 | tf_op jit(solution)/shard_map/reduce_scatter | solution.py:275
  447.4 168.9 %reduce-scatter.10.cloned.1.call-start = ((), (), s32[]{:S(2)}) async-start(), calls=%async_computation.12 | async-start | bytes 3522560 | tf_op jit(solution)/shard_map/reduce_scatter | solution.py:275
  467.0 36.3 %collective-permute-start.39 = (bf16[1280,2048]{1,0:T(8,128)(2,1)}, bf16[1280,2048]{1,0:T(8,128)(2,1)}, u32[]{:S(2)}, u32[]{:S(2)}) collective-permute-start(bf16[1280,2048]{1,0:T(8,128)(2,1)} %convolution_convert_fusion), channel_id=1, source_target_pairs={{0,1},{1,0},{2,3},{3,2},{4,5},{5,4},{6,7},{7,6},{8,9},{9,8},{10,11... | collective-permute-start | bytes 15728648 | tf_op jit(solution)/shard_map/ppermute | solution.py:19
  478.8 366.1 %reduce-scatter.6.cloned.1.call-start = ((), (), s32[]{:S(2)}) async-start(), calls=%async_computation.10 | async-start | bytes 3276800 | tf_op jit(solution)/shard_map/reduce_scatter | solution.py:307
  522.6 40.9 %collective-permute-start.40 = (bf16[160,2048]{1,0:T(8,128)(2,1)}, bf16[160,2048]{1,0:T(8,128)(2,1)}, u32[]{:S(2)}, u32[]{:S(2)}) collective-permute-start(bf16[160,2048]{1,0:T(8,128)(2,1)} %get-tuple-element.65), channel_id=1, source_target_pairs={{0,2},{2,0},{1,3},{3,1},{4,6},{6,4},{5,7},{7,5},{8,10},{10,8},{9,1... | collective-permute-start | bytes 1966088 | tf_op jit(solution)/shard_map/ppermute | solution.py:19
  549.4 48.9 %collective-permute-start.63 = (bf16[160,2048]{1,0:T(8,128)(2,1)S(1)}, bf16[160,2048]{1,0:T(8,128)(2,1)}, u32[]{:S(2)}, u32[]{:S(2)}) collective-permute-start(bf16[160,2048]{1,0:T(8,128)(2,1)S(1)} %get-tuple-element.63), channel_id=1, source_target_pairs={{0,4},{4,0},{1,5},{5,1},{2,6},{6,2},{3,7},{7,3},{8,12},{12,8},{9,1... | collective-permute-start | bytes 1966088 | tf_op jit(solution)/shard_map/ppermute | solution.py:19
  551.1 42.7 %collective-permute-start.42 = (bf16[160,2048]{1,0:T(8,128)(2,1)}, bf16[160,2048]{1,0:T(8,128)(2,1)}, u32[]{:S(2)}, u32[]{:S(2)}) collective-permute-start(bf16[160,2048]{1,0:T(8,128)(2,1)} %fusion.45), channel_id=1, source_target_pairs={{0,4},{4,0},{1,5},{5,1},{2,6},{6,2},{3,7},{7,3},{8,12},{12,8},{9,1... | collective-permute-start | bytes 1966088 | tf_op jit(solution)/shard_map/ppermute | solution.py:19
  555.5 43.1 %collective-permute-start.65 = (bf16[160,2048]{1,0:T(8,128)(2,1)}, bf16[160,2048]{1,0:T(8,128)(2,1)}, u32[]{:S(2)}, u32[]{:S(2)}) collective-permute-start(bf16[160,2048]{1,0:T(8,128)(2,1)} %get-tuple-element.56), channel_id=1, source_target_pairs={{0,2},{2,0},{1,3},{3,1},{4,6},{6,4},{5,7},{7,5},{8,10},{10,8},{9,1... | collective-permute-start | bytes 1966088 | tf_op jit(solution)/shard_map/ppermute | solution.py:19
  563.6 44.1 %collective-permute-start.43 = (bf16[160,2048]{1,0:T(8,128)(2,1)S(1)}, bf16[160,2048]{1,0:T(8,128)(2,1)S(1)}, u32[]{:S(2)}, u32[]{:S(2)}) collective-permute-start(bf16[160,2048]{1,0:T(8,128)(2,1)S(1)} %get-tuple-element.67), channel_id=1, source_target_pairs={{0,4},{4,0},{1,5},{5,1},{2,6},{6,2},{3,7},{7,3},{8,12},{12,8},{9,1... | collective-permute-start | bytes 1966088 | tf_op jit(solution)/shard_map/ppermute | solution.py:19
  565.7 52.6 %collective-permute-start.81 = (bf16[256,688]{0,1:T(8,128)(2,1)}, bf16[256,688]{0,1:T(8,128)(2,1)}, u32[]{:S(2)}, u32[]{:S(2)}) collective-permute-start(bf16[256,688]{0,1:T(8,128)(2,1)} %constant_dynamic-slice_fusion), channel_id=1, source_target_pairs={{0,4},{4,0},{1,5},{5,1},{2,6},{6,2},{3,7},{7,3},{8,12},{12,8},{9,1... | collective-permute-start | bytes 1056776 | tf_op jit(solution)/shard_map/ppermute | solution.py:19
  632.9 76.8 %collective-permute-start.67 = (bf16[640,2048]{1,0:T(8,128)(2,1)}, bf16[640,2048]{1,0:T(8,128)(2,1)}, u32[]{:S(2)}, u32[]{:S(2)}) collective-permute-start(bf16[640,2048]{1,0:T(8,128)(2,1)} %pad_maximum_fusion.8), channel_id=1, source_target_pairs={{0,2},{2,0},{1,3},{3,1},{4,6},{6,4},{5,7},{7,5},{8,10},{10,8},{9,1... | collective-permute-start | bytes 7864328 | tf_op jit(solution)/shard_map/ppermute | solution.py:19
  634.2 66.6 %collective-permute-start.76 = (bf16[128,1376]{0,1:T(8,128)(2,1)}, bf16[128,1376]{0,1:T(8,128)(2,1)}, u32[]{:S(2)}, u32[]{:S(2)}) collective-permute-start(bf16[128,1376]{0,1:T(8,128)(2,1)} %fusion.65), channel_id=1, source_target_pairs={{0,2},{2,0},{1,3},{3,1},{4,6},{6,4},{5,7},{7,5},{8,10},{10,8},{9,1... | collective-permute-start | bytes 1056776 | tf_op jit(solution)/shard_map/ppermute | solution.py:19
  639.9 65.5 %collective-permute-start.83 = (bf16[64,2752]{1,0:T(8,128)(2,1)}, bf16[64,2752]{1,0:T(8,128)(2,1)}, u32[]{:S(2)}, u32[]{:S(2)}) collective-permute-start(bf16[64,2752]{1,0:T(8,128)(2,1)} %copy.79), channel_id=1, source_target_pairs={{0,1},{1,0},{2,3},{3,2},{4,5},{5,4},{6,7},{7,6},{8,9},{9,8},{10,11... | collective-permute-start | bytes 1056776 | tf_op jit(solution)/shard_map/ppermute | solution.py:19
  643.1 64.4 %collective-permute-start.80 = (bf16[64,2752]{1,0:T(8,128)(2,1)}, bf16[64,2752]{1,0:T(8,128)(2,1)}, u32[]{:S(2)}, u32[]{:S(2)}) collective-permute-start(bf16[64,2752]{1,0:T(8,128)(2,1)} %copy.76), channel_id=1, source_target_pairs={{0,1},{1,0},{2,3},{3,2},{4,5},{5,4},{6,7},{7,6},{8,9},{9,8},{10,11... | collective-permute-start | bytes 1056776 | tf_op jit(solution)/shard_map/ppermute | solution.py:19
  705.4 61.5 %collective-permute-start.77 = (bf16[64,2752]{1,0:T(8,128)(2,1)}, bf16[64,2752]{1,0:T(8,128)(2,1)}, u32[]{:S(2)}, u32[]{:S(2)}) collective-permute-start(bf16[64,2752]{1,0:T(8,128)(2,1)} %copy.73), channel_id=1, source_target_pairs={{0,1},{1,0},{2,3},{3,2},{4,5},{5,4},{6,7},{7,6},{8,9},{9,8},{10,11... | collective-permute-start | bytes 1056776 | tf_op jit(solution)/shard_map/ppermute | solution.py:19
  756.8 98.2 %reduce-scatter.8.cloned.1.call-start = ((), (), s32[]{:S(2)}) async-start(), calls=%async_computation.11 | async-start | bytes 2621440 | tf_op jit(solution)/shard_map/reduce_scatter | solution.py:307
  (161 other events, 2132.2 us)
Sparse Core Ops, SparseCore 0:
  30.4 69.8 all-gather.5
  102.5 45.8 all-gather.7
  150.0 56.7 all-gather.13
  208.2 56.7 all-gather.11
  284.8 57.5 all-gather.9
  435.2 54.7 reduce-scatter.13
  492.4 54.9 reduce-scatter.11
  549.7 54.9 reduce-scatter.9
  756.9 52.2 reduce-scatter.5
  811.4 43.4 reduce-scatter.7

commit v2 on v1

v2 whole, which is shorter than its diff:
```python
import functools

import jax
import jax.numpy as jnp
import numpy as np
from jax import lax
from jax.experimental import pallas as pl
from jax.experimental.pallas import tpu as pltpu
from jax.sharding import Mesh
from jax.sharding import PartitionSpec as P

HEADS = 16
EPSILON = 1e-06
BF = jnp.bfloat16
F32 = jnp.float32


def index(ax):
    return lax.axis_index(ax)


def shift(v, ax, k=1):
    n = lax.axis_size(ax)
    return lax.ppermute(v, ax, [(i, (i + k) % n) for i in range(n)])


def absolute(rel, ax):
    n = len(rel)
    if n == 1:
        return list(rel)
    i = index(ax)
    out = []
    for j in range(n):
        picked = rel[0]
        for k in range(1, n):
            picked = jnp.where((i - j + n) % n == k, rel[k], picked)
        out.append(picked)
    return out


def ring(v, ax):
    out = [v]
    for _ in range(lax.axis_size(ax) - 1):
        out.append(shift(out[-1], ax))
    return out


def ring_sum(pieces, ax):
    acc = None
    for k in range(len(pieces) - 1, 0, -1):
        term = pieces[k].astype(F32)
        if acc is not None:
            term = term + acc
        acc = shift(term.astype(BF), ax, -1).astype(F32)
    own = pieces[0].astype(F32)
    return own if acc is None else own + acc


def fan(v, ax):
    return [v] + [shift(v, ax, k) for k in range(1, lax.axis_size(ax))]


def exchange(blocks, axes):
    return lax.all_to_all(blocks, axes, 0, 0, tiled=True)


def cost(flops, nbytes):
    return pl.CostEstimate(flops=int(flops), bytes_accessed=int(nbytes), transcendentals=0)


def nothing(*refs):
    del refs


def after(v, *deps):
    return pl.pallas_call(
        nothing,
        out_shape=jax.ShapeDtypeStruct(v.shape, v.dtype),
        in_specs=[pl.BlockSpec(memory_space=pl.ANY)] * (1 + len(deps)),
        out_specs=pl.BlockSpec(memory_space=pl.ANY),
        input_output_aliases={0: 0},
        compiler_params=params(1),
        cost_estimate=cost(1, 1),
        name="after",
    )(v, *deps)


def stream_gather(v, ax_y="y", ax_c="c"):
    return [ring(piece, ax_c) for piece in ring(v, ax_y)]


def place_of(ry, rc):
    ny, nc = lax.axis_size("y"), lax.axis_size("c")
    return ((index("y") - ry + ny) % ny) * nc + (index("c") - rc + nc) % nc


def in_order(pieces):
    ny, nc = len(pieces), len(pieces[0])
    rows = pieces[0][0].shape[0]
    out = jnp.zeros((ny * nc * rows,) + pieces[0][0].shape[1:], pieces[0][0].dtype)
    for ry in range(ny):
        for rc in range(nc):
            out = lax.dynamic_update_slice_in_dim(out, pieces[ry][rc], place_of(ry, rc) * rows, 0)
    return out


def stream_sum(partial, rows):
    nc, ny = lax.axis_size("c"), lax.axis_size("y")
    sums = []
    for ry in range(ny):
        terms = [
            lax.dynamic_slice_in_dim(partial, place_of(ry, rc) * rows, rows, 0) for rc in range(nc)
        ]
        sums.append(ring_sum(terms, "c"))
    return ring_sum(sums, "y")


def wide_gather(v, both):
    if both:
        half = v.shape[0] // 2
        x, y = shift(v, "x"), shift(v, "y")
        groups = [[v], [x], [y], [shift(x[:half], "y"), shift(y[half:], "x")]]
    else:
        groups = [[piece] for piece in ring(v, "y")]
    return groups


def with_other(g):
    return (g, [shift(p, "c") for p in g])


def dot(a, b, dims, out=F32):
    return lax.dot_general(a, b, (dims, ((), ())), preferred_element_type=F32).astype(out)


NN = ((1,), (0,))
NT = ((1,), (1,))
TN = ((0,), (0,))


def inverse_rms(v):
    return lax.rsqrt(jnp.mean(v * v, axis=-1, keepdims=True) + EPSILON)


def rms_back(grad, normed, inverse):
    return inverse * (grad - normed * jnp.mean(grad * normed, axis=-1, keepdims=True))


def params(limit=60):
    return pltpu.CompilerParams(vmem_limit_bytes=limit << 20)


def block_of(stream):
    return 256 if stream % 256 == 0 else stream


def allowed_of(doc_col, doc_row, r0, block, length):
    rows = r0 + lax.broadcasted_iota(jnp.int32, (block, length), 0)
    cols = lax.broadcasted_iota(jnp.int32, (block, length), 1)
    return (doc_col == doc_row) & (cols <= rows)


def head_lanes(a, h, fk):
    lane = lax.broadcasted_iota(jnp.int32, a.shape, 1)
    return jnp.where((lane >= h * fk) & (lane < (h + 1) * fk), a, jnp.zeros_like(a))


def attention_kernel(heads, fk, fv, qkv, doc_row, doc_col, att, out, den):
    stream = qkv.shape[0]
    block = block_of(stream)
    wide = heads * fk
    for r0 in range(0, stream, block):
        length = r0 + block
        rows = slice(r0, length)
        allowed = allowed_of(doc_col[rows, :], doc_row[:, :length], r0, block, length)
        q = qkv[rows, :wide]
        k = qkv[:length, wide : 2 * wide]
        dens = []
        for h in range(heads):
            at = slice(h * fv, (h + 1) * fv)
            v = qkv[:length, 2 * wide + h * fv : 2 * wide + (h + 1) * fv]
            w = 1.0 + 0.25 * dot(head_lanes(q, h, fk), k, NT)
            scores = jnp.where(allowed, 0.5 * w * w + 0.5, 0.0)
            total = jnp.sum(scores, axis=1, keepdims=True)
            o = dot(scores.astype(BF), v, NN) / total
            out[rows, at] = o
            att[rows, at] = o.astype(BF)
            dens.append(total)
        den[rows, :] = jnp.concatenate(dens, axis=1)


def attention(qkv, doc, heads, fk, fv):
    stream = qkv.shape[0]
    return pl.pallas_call(
        functools.partial(attention_kernel, heads, fk, fv),
        out_shape=(
            jax.ShapeDtypeStruct((stream, heads * fv), BF),
            jax.ShapeDtypeStruct((stream, heads * fv), F32),
            jax.ShapeDtypeStruct((stream, heads), F32),
        ),
        compiler_params=params(),
        cost_estimate=cost(2 * heads * stream * stream * 256, stream * 6000),
        name="attention",
    )(qkv, doc[None, :], doc[:, None])


def attention_back_kernel(heads, fk, fv, qkv, doc_row, doc_col, out, den, grad, dqkv, dk, dv):
    stream = qkv.shape[0]
    block = block_of(stream)
    wide = heads * fk
    for r0 in range(stream - block, -1, -block):
        length = r0 + block
        rows = slice(r0, length)
        first = length == stream
        allowed = allowed_of(doc_col[rows, :], doc_row[:, :length], r0, block, length)
        q = qkv[rows, :wide]
        k = qkv[:length, wide : 2 * wide]
        dq = jnp.zeros((block, wide), F32)
        dk_add = jnp.zeros((length, wide), F32)
        for h in range(heads):
            at = slice(h * fv, (h + 1) * fv)
            v = qkv[:length, 2 * wide + h * fv : 2 * wide + (h + 1) * fv]
            q_head = head_lanes(q, h, fk)
            w = 1.0 + 0.25 * dot(q_head, k, NT)
            scores = jnp.where(allowed, 0.5 * w * w + 0.5, 0.0).astype(BF)
            inv = 1.0 / den[rows, h : h + 1]
            g = grad[rows, at].astype(F32)
            dnum = (g * inv).astype(BF)
            dden = -jnp.sum(g * out[rows, at], axis=1, keepdims=True) * inv
            ds = dot(dnum, v, NT) + dden
            du = jnp.where(allowed, ds * (0.25 * w), 0.0).astype(BF)
            dq = dq + dot(du, head_lanes(k, h, fk), NN)
            dk_add = dk_add + dot(du, q_head, TN)
            dv_add = dot(scores, dnum, TN)
            dv[:length, at] = dv_add if first else dv[:length, at] + dv_add
        dk[:length, :] = dk_add if first else dk[:length, :] + dk_add
        dqkv[rows, :wide] = dq.astype(BF)
    dqkv[:, wide : 2 * wide] = dk[...].astype(BF)
    dqkv[:, 2 * wide :] = dv[...].astype(BF)


def attention_back(qkv, doc, out, den, grad, heads, fk, fv):
    stream = qkv.shape[0]
    return pl.pallas_call(
        functools.partial(attention_back_kernel, heads, fk, fv),
        out_shape=jax.ShapeDtypeStruct(qkv.shape, BF),
        scratch_shapes=[
            pltpu.VMEM((stream, heads * fk), F32),
            pltpu.VMEM((stream, heads * fv), F32),
        ],
        compiler_params=params(),
        cost_estimate=cost(2 * heads * stream * stream * 640, stream * 8000),
        name="attention_back",
    )(qkv, doc[None, :], doc[:, None], out, den, grad)


def norm_in_kernel(places, *refs):
    pieces, gain = refs[: places.shape[0]], refs[places.shape[0]]
    a_out = refs[-1]
    for k, piece in enumerate(pieces):

        @pl.when(pl.program_id(0) == k)
        def _(piece=piece):
            x = piece[...].astype(F32)
            a_out[...] = (x * inverse_rms(x) * gain[...]).astype(BF)


def norm_in(pieces, places, gain):
    n = len(pieces)
    rows, d = pieces[0].shape

    def at(i, places):
        return (places[i], 0)

    def still(a):
        return pl.BlockSpec(a.shape, lambda i, places: (0, 0), pipeline_mode=pl.Buffered(1))

    return pl.pallas_call(
        norm_in_kernel,
        grid_spec=pltpu.PrefetchScalarGridSpec(
            num_scalar_prefetch=1,
            grid=(n,),
            in_specs=[still(p) for p in pieces] + [still(gain)],
            out_specs=pl.BlockSpec((rows, d), at),
        ),
        out_shape=jax.ShapeDtypeStruct((n * rows, d), BF),
        compiler_params=params(),
        cost_estimate=cost(n * rows * d, 4 * n * rows * d),
        name="norm_in",
    )(places, *pieces, gain)


def whole(a):
    rank = len(a.shape)
    return pl.BlockSpec(a.shape, lambda i: (0,) * rank, pipeline_mode=pl.Buffered(1))


def mat(m, w):
    parts, _, rows, cols = w.shape
    return pl.BlockSpec(
        (parts, 1, rows, cols), lambda i: (0, m, 0, 0), pipeline_mode=pl.Buffered(1)
    )


def rows_of(ref):
    parts, _, rows, cols = ref.shape
    return ref[...].reshape(parts * rows, cols)


def size_of(w):
    parts, _, rows, cols = w.shape
    return parts * rows, cols


def ffn_in_kernel(counts, *refs):
    n = sum(counts)
    parts, (wg, wu) = refs[:n], refs[n : n + 2]
    b_out, gate_out, up_out, h_out, b_ref = refs[-5:]
    start = 0
    for step, count in enumerate(counts):

        @pl.when(pl.program_id(0) == step)
        def _(some=parts[start : start + count]):
            at = 0
            for p in some:
                b_ref[at : at + p.shape[0], :] = p[...]
                at += p.shape[0]

        start += count
    b = b_ref[...]
    b_out[...] = b
    gate = dot(b, rows_of(wg), NN)
    up = dot(b, rows_of(wu), NN)
    gate_out[...] = gate
    up_out[...] = up
    h_out[...] = (gate * jax.nn.sigmoid(gate) * up).astype(BF)


def ffn_in(first, total, steps, w, buffers):
    block = sum(p.shape[0] for p in steps[0])
    d, ff = size_of(w)
    parts = [p for some in steps for p in some]
    operands = parts + [w, w]
    in_specs = [whole(p) for p in parts] + [mat(0, w), mat(1, w)]
    aliases = {}
    if buffers is not None:
        aliases = {len(operands) + j: j for j in range(4)}
        operands += list(buffers)
        in_specs += [pl.BlockSpec(memory_space=pl.ANY)] * 4
    widths = ((d, BF), (ff, F32), (ff, F32), (ff, BF))
    return pl.pallas_call(
        functools.partial(ffn_in_kernel, [len(some) for some in steps]),
        grid=(len(steps),),
        in_specs=in_specs,
        out_specs=tuple(pl.BlockSpec((block, w), lambda i: (first + i, 0)) for w, _ in widths),
        out_shape=tuple(jax.ShapeDtypeStruct((total, w), t) for w, t in widths),
        scratch_shapes=[pltpu.VMEM((block, d), BF)],
        input_output_aliases=aliases,
        compiler_params=params(),
        cost_estimate=cost(
            4 * len(steps) * block * d * ff, 4 * d * ff + len(steps) * block * (4 * d + 10 * ff)
        ),
        name="ffn_in",
    )(*operands)


def ffn_mid_kernel(gate, up, dy, wd, dg_out, du_out):
    sig = jax.nn.sigmoid(gate[...])
    dh = dot(dy[...], rows_of(wd), NN)
    dg_out[...] = (dh * up[...] * (sig * (1.0 + gate[...] * (1.0 - sig)))).astype(BF)
    du_out[...] = (dh * gate[...] * sig).astype(BF)


def ffn_mid(block, gate, up, dy, w):
    total, ff = gate.shape
    d = dy.shape[1]

    def at(i):
        return (i, 0)

    return pl.pallas_call(
        ffn_mid_kernel,
        grid=(total // block,),
        in_specs=[pl.BlockSpec((block, n), at) for n in (ff, ff, d)] + [mat(2, w)],
        out_specs=(pl.BlockSpec((block, ff), at),) * 2,
        out_shape=(jax.ShapeDtypeStruct((total, ff), BF),) * 2,
        compiler_params=params(),
        cost_estimate=cost(2 * total * d * ff, 2 * d * ff + total * (2 * d + 12 * ff)),
        name="ffn_mid",
    )(gate, up, dy, w)


def ffn_back_kernel(dgate, dup, wg, wu, *outs):
    db = dot(dgate[...], rows_of(wg), NT) + dot(dup[...], rows_of(wu), NT)
    db = db.astype(BF)
    for step, out in enumerate(outs):

        @pl.when(pl.program_id(0) == step)
        def _(out=out):
            out[...] = db


def ffn_back(first, count, block, dgate, dup, w):
    d, ff = size_of(w)
    rows = pl.BlockSpec((block, ff), lambda i: (first + i, 0))
    return pl.pallas_call(
        ffn_back_kernel,
        grid=(count,),
        in_specs=[rows, rows, mat(0, w), mat(1, w)],
        out_specs=(pl.BlockSpec((block, d), lambda i: (0, 0)),) * count,
        out_shape=(jax.ShapeDtypeStruct((block, d), BF),) * count,
        compiler_params=params(),
        cost_estimate=cost(4 * count * block * d * ff, 4 * d * ff + count * block * (2 * d + 4 * ff)),
        name="ffn_back",
    )(dgate, dup, w, w)


def dz_in_kernel(places, *refs):
    pieces, mat = refs[: places.shape[0]], refs[places.shape[0]]
    dz_out, dc_out = refs[-2:]
    for k, piece in enumerate(pieces):

        @pl.when(pl.program_id(0) == k)
        def _(piece=piece):
            dz_out[...] = piece[...]
            cols = mat.shape[3]
            dc_out[...] = sum(
                dot(piece[:, k * cols : (k + 1) * cols], columns_of(mat, k), NT)
                for k in range(mat.shape[1])
            )


def dz_in(pieces, places, mat):
    n = len(pieces)
    rows, d = pieces[0].shape
    width = mat.shape[0] * mat.shape[2]

    def at(i, places):
        return (places[i], 0)

    def still(a):
        zeros = (0,) * len(a.shape)
        return pl.BlockSpec(a.shape, lambda i, places: zeros, pipeline_mode=pl.Buffered(1))

    return pl.pallas_call(
        dz_in_kernel,
        grid_spec=pltpu.PrefetchScalarGridSpec(
            num_scalar_prefetch=1,
            grid=(n,),
            in_specs=[still(p) for p in pieces] + [still(mat)],
            out_specs=(pl.BlockSpec((rows, d), at), pl.BlockSpec((rows, width), at)),
        ),
        out_shape=(
            jax.ShapeDtypeStruct((n * rows, d), BF),
            jax.ShapeDtypeStruct((n * rows, width), F32),
        ),
        compiler_params=params(),
        cost_estimate=cost(2 * n * rows * d * width, 6 * n * rows * d),
        name="dz_in",
    )(places, *pieces, mat)


def weight_grad_kernel(a, b, out):
    out[...] = dot(a[...], b[...], TN, BF)


def weight_grad(a, b):
    rows, m = a.shape
    n = b.shape[1]
    block = 512 if m % 512 == 0 else m
    return pl.pallas_call(
        weight_grad_kernel,
        grid=(m // block,),
        in_specs=[pl.BlockSpec((rows, block), lambda i: (0, i)), whole(b)],
        out_specs=pl.BlockSpec((block, n), lambda i: (i, 0)),
        out_shape=jax.ShapeDtypeStruct((m, n), BF),
        compiler_params=params(),
        cost_estimate=cost(2 * rows * m * n, 2 * (rows * (m + n) + m * n)),
        name="weight_grad",
    )(a, b)


def pack_kernel(order, n_plain, *refs):
    out, plain, extra = refs[-1], refs[:n_plain], refs[n_plain:-1]
    rows = plain[0].shape[0]
    n = len(order)
    width = out.shape[2]
    for t, u in enumerate(order):
        some = []
        for ref in plain:
            cols = ref.shape[1] // n
            some.append(ref[:, u * cols : (u + 1) * cols].astype(BF))
        out[t, :rows, :] = jnp.concatenate(some, axis=1)
        some = []
        for ref in extra:
            gap = jnp.zeros((1, width - ref.shape[1]), F32)
            row = jnp.concatenate([ref[...], gap], axis=1) if gap.shape[1] else ref[...]
            some.append(jnp.broadcast_to(row, (8, width)))
        out[t, rows:, :] = jnp.concatenate(some, axis=0).astype(BF)


def pack_columns(order, plain, extra):
    rows = plain[0].shape[0]
    width = sum(w.shape[1] for w in plain) // len(order)
    tall = rows + 8 * len(extra)
    return pl.pallas_call(
        functools.partial(pack_kernel, order, len(plain)),
        out_shape=jax.ShapeDtypeStruct((len(order), tall, width), BF),
        compiler_params=params(),
        cost_estimate=cost(1, 6 * len(order) * tall * width),
        name="pack",
    )(*plain, *extra)


def split_kernel(order, *refs):
    out = refs[-1]
    for m, ref in enumerate(refs[:-1]):
        cols = ref.shape[1] // len(order)
        for t, u in enumerate(order):
            out[t, m] = ref[:, u * cols : (u + 1) * cols].astype(BF)


def split_columns(order, mats):
    rows, cols = mats[0].shape
    n = len(order)
    return pl.pallas_call(
        functools.partial(split_kernel, order),
        out_shape=jax.ShapeDtypeStruct((n, len(mats), rows, cols // n), BF),
        compiler_params=params(),
        cost_estimate=cost(1, 6 * len(mats) * rows * cols),
        name="split",
    )(*mats)


def down_kernel(dy, hid, hid_rows, wd, grad, terms):
    grad[...] = dot(dy[...], hid[...], TN, BF)
    terms[...] = dot(hid_rows[...], rows_of(wd), NT, BF)


def down_both(dy, hid, w):
    rows, d = dy.shape
    ff = hid.shape[1]
    steps = 8
    return pl.pallas_call(
        down_kernel,
        grid=(steps,),
        in_specs=[
            pl.BlockSpec((rows, d // steps), lambda i: (0, i)),
            whole(hid),
            pl.BlockSpec((rows // steps, ff), lambda i: (i, 0)),
            mat(2, w),
        ],
        out_specs=(
            pl.BlockSpec((d // steps, ff), lambda i: (i, 0)),
            pl.BlockSpec((rows // steps, d), lambda i: (i, 0)),
        ),
        out_shape=(
            jax.ShapeDtypeStruct((d, ff), BF),
            jax.ShapeDtypeStruct((rows, d), BF),
        ),
        compiler_params=params(),
        cost_estimate=cost(4 * rows * d * ff, 4 * (rows * d + rows * ff + d * ff)),
        name="down_both",
    )(dy, hid, hid, w)


def pair_grad_kernel(a, b0, b1, out):
    out[0, 0] = dot(a[...], b0[...], TN, BF)
    out[0, 1] = dot(a[...], b1[...], TN, BF)


def pair_grad(a, b0, b1, parts):
    rows, m = a.shape
    n = b0.shape[1]
    block = m // parts
    return pl.pallas_call(
        pair_grad_kernel,
        grid=(parts,),
        in_specs=[pl.BlockSpec((rows, block), lambda i: (0, i)), whole(b0), whole(b1)],
        out_specs=pl.BlockSpec((1, 2, block, n), lambda i: (i, 0, 0, 0)),
        out_shape=jax.ShapeDtypeStruct((parts, 2, block, n), BF),
        compiler_params=params(),
        cost_estimate=cost(4 * rows * m * n, 2 * (rows * (m + 2 * n) + 2 * m * n)),
        name="pair_grad",
    )(a, b0, b1)


def columns_of(w, k):
    n, _, rows, cols = w.shape
    return w[:, k].reshape(n * rows, cols)


def out_kernel(a, w, out):
    out[...] = jnp.concatenate(
        [dot(a[...], columns_of(w, k), NN, BF) for k in range(w.shape[1])], axis=1
    )


def out_terms(a, w):
    stream, n = a.shape
    d = w.shape[1] * w.shape[3]
    block = stream // 4
    return pl.pallas_call(
        out_kernel,
        grid=(4,),
        in_specs=[pl.BlockSpec((block, n), lambda i: (i, 0)), whole(w)],
        out_specs=pl.BlockSpec((block, d), lambda i: (i, 0)),
        out_shape=jax.ShapeDtypeStruct((stream, d), BF),
        compiler_params=params(),
        cost_estimate=cost(2 * stream * n * d, 2 * (stream * (n + d) + n * d)),
        name="out_terms",
    )(a, w)


def unpack_kernel(order, g, out):
    out[...] = jnp.concatenate([g[t, 0].astype(F32) for t in order], axis=1)


def unpack(g, m, order):
    n, _, rows, cols = g.shape
    return pl.pallas_call(
        functools.partial(unpack_kernel, order),
        grid=(1,),
        in_specs=[pl.BlockSpec((n, 1, rows, cols), lambda i: (0, m, 0, 0))],
        out_specs=pl.BlockSpec((rows, n * cols), lambda i: (0, 0)),
        out_shape=jax.ShapeDtypeStruct((rows, n * cols), F32),
        compiler_params=params(),
        cost_estimate=cost(1, 6 * n * rows * cols),
        name="unpack",
    )(g)


def sum_rows(g, *deps):
    nx = lax.axis_size("x")
    x = index("x")
    terms = [lax.dynamic_index_in_dim(g, (x - k + nx) % nx, 1, False) for k in range(nx)]
    mine = ring_sum(terms, "x").astype(BF)
    mine = after(mine.reshape(-1, mine.shape[-1]), *deps)
    return mine, lax.psum_scatter(mine, "z", scatter_dimension=0, tiled=True)


def per_device(both, tokens, segments, cotangent, wq, wk, wv, wo, wg, wu, wd, g1, g2):
    rows, d = tokens.shape
    everything = ("z", "x", "y", "c")
    nz, nx, ny, nc = (lax.axis_size(a) for a in everything)
    ns = ny * nc
    stream = rows * ns
    heads = HEADS // ns
    fk = wq.shape[1] // HEADS
    fv = wv.shape[1] // HEADS
    own = wq.shape[0]

    def order_of(sizes):
        order = np.arange(int(np.prod(sizes))).reshape(sizes[::-1])
        return order.transpose().reshape(-1).tolist()

    width = (wq.shape[1] + wk.shape[1] + wv.shape[1]) // ns
    pack = pack_columns(
        order_of((ny, nc)),
        (wq, wk, wv),
        (jnp.concatenate([g1, g2])[None], segments.astype(F32)),
    )
    pack = exchange(pack, ("y", "c"))
    doc = pack[:, own + 8, :rows].astype(jnp.int32).reshape(stream)
    pack = pack[:, : own + 8]

    group = ("x", "y", "c") if both else ("y", "c")
    sizes = (nx, ny, nc) if both else (ny, nc)
    ng = nx * ns if both else ns
    ff = wg.shape[1] // ng
    along = ("z",) if both else ("z", "x")
    na = nz if both else nz * nx
    blocks = split_columns(order_of(sizes), (wg, wu, wd))
    vy = ring(after(tokens, pack), "y")
    got = exchange(blocks, group).transpose(1, 0, 2, 3).reshape(-1, ff)
    late = after(cotangent, pack)
    dy_x = shift(late, "x")

    ndp = nz * nx

    def gather(w, axes):
        return lax.all_gather(w, axes, axis=0, tiled=True)

    def by_x(pieces):
        return jnp.concatenate(absolute([p[:, None] for p in pieces], "x"), axis=1)

    tall = ns * (own + 8)
    pack = pack.reshape(tall, width)
    joint_form = ns == nz and width % 512 == 128 and d % 512 == 0 and tall % 32 == 0
    if joint_form:
        left = [pack[k * tall // 4 : (k + 1) * tall // 4, width - 128 :] for k in range(4)]
        some = [wo[:, k : k + 512].astype(BF) for k in range(0, d, 512)]
        stacked = [pack[:, : width - 128], jnp.concatenate(left, axis=1)] + some
        joint = gather(jnp.concatenate(stacked, axis=0), "z").reshape(nz, -1, 512)
        cut = tall + tall // 4
        qkv_parts = ring(joint[:, :cut], "x")
        units = [order_of((ny, nc))[t % ns] for t in range(nx * ns)]
        out_w = jnp.stack([joint[u, cut:] for u in units])
        out_w = exchange(after(out_w, qkv_parts[-1]), ("x", "y", "c"))
        out_w = out_w.reshape(nx * ns, d // 512, own, 512)
        arrived_last = [joint]

        def qkv_of(m):
            rest = m[:, tall:].reshape(nz, tall // 4, 4, 128).transpose(0, 2, 1, 3)
            return jnp.concatenate([m[:, :tall], rest.reshape(nz, tall, 128)], axis=2)

    else:
        perm = []
        for dp in range(ndp):
            for u in range(ns):
                perm.append((u * ndp + dp, dp * ns + u % ny * nc + u // ny))
        qkv_z = gather(pack, "z")
        out_z = gather(lax.ppermute(wo.astype(BF), everything, perm), "z")
        qkv_parts = ring(qkv_z.reshape(nz, tall, width), "x")
        out_w = by_x(ring(out_z.reshape(nz, own, d), "x"))
        out_w = out_w.reshape(1, -1, d // 256, 256).transpose(0, 2, 1, 3)
        arrived_last = [qkv_z, out_z]

        def qkv_of(m):
            return m

    got = after(got, vy[-1], dy_x, *arrived_last)
    ffn_w = gather(got, along).reshape(na, 3, d // na, ff)
    qkv_all = by_x([qkv_of(m) for m in qkv_parts]).reshape(ndp * ns, own + 8, width)
    qkv_mat = qkv_all[:, :own].reshape(d, width)
    gains = qkv_all[:, own, : 2 * own].astype(F32)
    gain_one, gain_two = gains[:, :own].reshape(1, d), gains[:, own:].reshape(1, d)

    x_pieces = [ring(p, "c") for p in vy]
    places = jnp.stack([place_of(ry, rc) for ry in range(ny) for rc in range(nc)])
    flat = [p for some in x_pieces for p in some]
    a_all = norm_in(flat, places, gain_one)
    late = after(late, x_pieces[-1][0])
    if both:
        half = rows // 2
        dy_y = shift(late, "y")
        dy_near = [dy_y]
        dy_far = [shift(dy_x[:half], "y"), shift(after(dy_y[half:], qkv_parts[-1]), "x")]
        dy_groups = [[late], [dy_x], [dy_y], dy_far]
    else:
        dy_groups = [[p] for p in ring(late, "y")]
        dy_near, dy_far = dy_groups[1], dy_groups[-1]
    dy_groups = [(g, [shift(p, "c") for p in g]) for g in dy_groups]
    dy_all = jnp.concatenate([p for mine, theirs in dy_groups for p in mine + theirs], axis=0)
    qkv = dot(a_all, qkv_mat, NN, BF)
    att, o, den = attention(qkv, doc, heads, fk, fv)
    branch = stream_sum(out_terms(after(att, *dy_near, *dy_far), out_w), rows)
    residual = tokens.astype(F32) + branch
    inv_mlp = inverse_rms(residual)
    normed_res = residual * inv_mlp
    b = (normed_res * gain_two).astype(BF)

    groups = wide_gather(b, both)
    count = len(groups)
    b_far = groups[-1]
    total = 2 * count * rows
    near = [some for g in groups[:-1] for some in with_other(g)]
    near[0] = [after(near[0][0], dy_all)]
    buffers = ffn_in(0, total, near, ffn_w, None)
    b_far = with_other([after(p, buffers[3]) for p in b_far])
    buffers = ffn_in(2 * count - 2, total, list(b_far), ffn_w, buffers)
    b_all, gate, up, hidden = buffers
    dgate, dup = ffn_mid(rows, gate, up, dy_all, ffn_w)

    def back(some, dgate, *deps):
        out = ffn_back(2 * some[0], 2 * len(some), rows, dgate, dup, ffn_w)
        theirs = [after(p, *deps) if deps else p for p in out[1::2]]
        return [(m, t, shift(t, "c")) for m, t in zip(out[::2], theirs)]

    def joined(mine, _, other):
        return mine.astype(F32) + other.astype(F32)

    def send(a, ax):
        return shift(a, ax).astype(F32)

    half = rows // 2
    if both:
        far = joined(*back([3], dgate)[0]).astype(BF)
        up_got, low_got = send(far[:half], "y"), send(far[half:], "x")
        dgate = after(dgate, far)
        tx, ty = [joined(*t) for t in back([1, 2], dgate, up_got, low_got)]
        x_low, y_up = tx[half:].astype(BF), ty[:half].astype(BF)
        x_up, y_low = (tx[:half] + up_got).astype(BF), (ty[half:] + low_got).astype(BF)
        dgate = after(dgate, x_low, y_up)
        mine = back([0], dgate)[0]
        own_term = joined(*mine)
        hidden = after(hidden, x_up, y_low, own_term)
        grad_down, ffn_terms = down_both(dy_all, hidden, ffn_w)
        own_term = after(own_term, grad_down)
        db = jnp.concatenate(
            [
                own_term[:half] + send(y_up, "y") + send(x_up, "x"),
                own_term[half:] + send(x_low, "x") + send(y_low, "y"),
            ],
            axis=0,
        )
    else:
        terms = [joined(*t) for t in back(list(range(count)), dgate)]
        grad_down, ffn_terms = down_both(dy_all, hidden, ffn_w)
        db = ring_sum(terms, "y")
    dr = cotangent.astype(F32) + rms_back(db * gain_two, normed_res, inv_mlp)

    dz = dr.astype(BF)
    down_sum = lax.psum_scatter(after(grad_down, dz), along, scatter_dimension=0, tiled=True)
    dz_y = ring(dz, "y")
    dz_own = ring(dz, "c")
    arrived = dz_y[-1]
    soon = dz_own[-1]
    blocks = [ffn_terms[g * rows : (g + 1) * rows] for g in range(2 * count)]
    others = [shift(blocks[2 * g + 1], "c") for g in range(count)]
    first = [
        (blocks[2 * g].astype(F32) + others[g].astype(F32)).astype(BF) for g in range(1, count)
    ]
    grad_in = pair_grad(b_all, after(dgate, soon, *first), dup, na)
    dz_pieces = [dz_own] + [ring(after(p, grad_in), "c") for p in dz_y[1:]]
    places = after(places, grad_in)
    in_sum = lax.psum_scatter(
        after(grad_in.reshape(-1, ff), arrived, down_sum), along, scatter_dimension=0, tiled=True
    )
    dz_all, dc = dz_in([p for some in dz_pieces for p in some], places, out_w)
    grad_wo = weight_grad(att, dz_all)
    if joint_form:
        g = exchange(grad_wo.reshape(nx * ns, own, d), ("x", "y", "c"))
        g = jnp.sum(g.reshape(nx, ns, own, d).astype(F32), axis=0).astype(BF)
        wo_mine = jnp.concatenate([g[t] for t in np.argsort(order_of((ny, nc)))], axis=0)
    else:
        wo_mine, _ = sum_rows(grad_wo.reshape(nz, nx, own, d))
    wo_sum = lax.psum_scatter(
        after(wo_mine, in_sum), "z", scatter_dimension=0, tiled=True
    )

    dc = after(dc, grad_wo)
    if both:
        to_x, to_y, far = first
        low_got = shift(to_x[half:], "x")
        far, to_y = after(far, arrived), after(to_y, arrived)
        x_up = (to_x[:half].astype(F32) + send(far[:half], "y")).astype(BF)
        y_low = (to_y[half:].astype(F32) + send(far[half:], "x")).astype(BF)
        up_got = shift(to_y[:half], "y")
        dc = after(dc, x_up, y_low)
        x_got, y_got = shift(x_up, "x"), shift(y_low, "y")
    dqkv = attention_back(qkv, doc, o, den, dc, heads, fk, fv)
    late = [up_got, low_got, x_got, y_got] if both else []
    dqkv = after(dqkv, wo_mine, *late)
    da_part = dot(dqkv, qkv_mat, NT)
    grad_qkv = weight_grad(a_all, after(dqkv, da_part))
    da = stream_sum(da_part, rows)
    qkv_mine, qkv_sum = sum_rows(grad_qkv.reshape(nz, nx, ns * own, width), wo_sum, da)
    back = jnp.concatenate([down_sum.reshape(1, ng, own, ff), in_sum.reshape(2, ng, own, ff)])
    back = exchange(back.transpose(1, 0, 2, 3), group)
    order = np.argsort(order_of(sizes)).tolist()
    grad_wg, grad_wu, grad_wd = [unpack(back, m, order) for m in (1, 2, 0)]
    qkv_sum = after(qkv_sum, grad_wg, grad_wu, grad_wd)
    own_term = after(blocks[0], grad_qkv).astype(F32) + others[0].astype(F32)
    if both:
        ffn = own_term + jnp.concatenate(
            [
                up_got.astype(F32) + x_got.astype(F32),
                low_got.astype(F32) + y_got.astype(F32),
            ],
            axis=0,
        )
    else:
        ffn = ring_sum([own_term] + first, "y")
    output = (residual + ffn).astype(BF)
    x_own = tokens.astype(F32)
    inv_own = inverse_rms(x_own)
    grad_tokens = dr + rms_back(da * gain_one, x_own * inv_own, inv_own)

    qkv_sum = exchange(qkv_sum.reshape(ns, own, width), ("y", "c"))
    qkv_sum = qkv_sum.reshape(ny, nc, own, width).transpose(2, 1, 0, 3)
    qkv_sum = qkv_sum.reshape(own, ns, width).astype(F32)
    grad_wq = qkv_sum[:, :, : heads * fk].reshape(wq.shape)
    grad_wk = qkv_sum[:, :, heads * fk : 2 * heads * fk].reshape(wk.shape)
    grad_wv = qkv_sum[:, :, 2 * heads * fk :].reshape(wv.shape)
    if joint_form:
        grad_wo = wo_sum.astype(F32)
    else:
        grad_wo = lax.ppermute(wo_sum, everything, [(t, s) for s, t in perm]).astype(F32)

    def gain_grad(gain, *pairs):
        total = sum(jnp.sum(w.astype(BF).astype(F32) * g, axis=1) for w, g in pairs)
        return total / gain.astype(BF).astype(F32)

    return (
        output,
        grad_tokens,
        grad_wq,
        grad_wk,
        grad_wv,
        grad_wo,
        grad_wg,
        grad_wu,
        grad_wd,
        gain_grad(g1, (wq, grad_wq), (wk, grad_wk), (wv, grad_wv)),
        gain_grad(g2, (wg, grad_wg), (wu, grad_wu)),
    )


def solution(mesh):
    n_dp, n_seq = mesh.shape["dp"], mesh.shape["seq"]
    nz = 4 if n_dp % 4 == 0 else n_dp
    nc = 2 if n_seq % 2 == 0 else 1
    nx, ny = n_dp // nz, n_seq // nc
    fine = Mesh(mesh.devices.reshape(nz, nx, ny, nc), ("z", "x", "y", "c"))
    both = nx == 2 and ny == 2
    all_rows = P(("z", "x", "y", "c"), None)
    vector = P(("z", "x", "y", "c"))
    placed = (
        (all_rows, P(("z", "x"), ("y", "c")), all_rows) + (all_rows,) * 7 + (vector, vector)
    )

    def run(*args):
        return per_device(both, *args)

    return jax.shard_map(
        run,
        mesh=fine,
        in_specs=placed,
        out_specs=(all_rows,) * 9 + (vector, vector),
        check_vma=False,
    )
```

time: 901 us -> 738 us (0.82)
  matrix products: 225 us -> 13.2 us
  Pallas kernels: 0 us -> 211 us
  waiting for transfers between devices: 334 us -> 236 us
  starting transfers between devices: 99.3 us -> 63.9 us
  other arithmetic: 91 us -> 58.7 us
  local copies, waits for them, and re-layouts: 119 us -> 131 us
    pallas_call x0 -> x51, Pallas kernels: none -> 211 us  [the longest x3 34.1 us: ffn_back(): pl.pallas_call(ffn_back_kernel, grid=(count,), in_specs=[rows, rows, mat(...]
    dot_general x18 -> x2, matrix products: 167 us -> 13.2 us  [dot(): lax.dot_general(a, b, (dims, ((), ())), preferred_element_type=F32)]
    ppermute x94 -> x52, waiting for transfers between devices: 325 us -> 174 us  [shift(): return lax.ppermute(v, ax, [(i, (i + k) % n) for i in range(n)])]
    dot_general x6 -> x0, matrix products: 57.7 us -> none  [the longest x1 13.7 us: attention(): jnp.einsum('hts,she->the', scores.astype(BF), v, preferred_element_type=F32)]
    ppermute x94 -> x52, starting transfers between devices: 94.4 us -> 37.3 us  [shift(): return lax.ppermute(v, ax, [(i, (i + k) % n) for i in range(n)])]
    all_to_all x0 -> x6, waiting for transfers between devices: none -> 50.8 us  [exchange(): return lax.all_to_all(blocks, axes, 0, 0, tiled=True)]
    select_n x34 -> x1, other arithmetic: 26.8 us -> 0.65 us  [absolute(): picked = jnp.where((i - j + n) % n == k, rel[k], picked)]
    all_to_all x0 -> x6, starting transfers between devices: none -> 25.5 us  [exchange(): return lax.all_to_all(blocks, axes, 0, 0, tiled=True)]
  transfers between devices with their start and end apart: 106 -> 64, of which waited for: 33 -> 25; matrix products, arithmetic and copies ran while one was open for 43% -> 17% of each run, Pallas kernels for 0% -> 22%
where the time goes in v2:
time: 738 us; the launch traced here: 730 us
  waiting for transfers between devices  236 us (32%)
  Pallas kernels  211 us (29%)
  local copies, waits for them, and re-layouts  131 us (18%)
  starting transfers between devices  63.9 us (9%)
  other arithmetic  58.7 us (8%)
  between operations  15.7 us (2%)
  matrix products  13.2 us (2%)
    ppermute x52, waiting for transfers between devices, shift(): return lax.ppermute(v, ax, [(i, (i + k) % n) for i in range(n)])  174 us
    unnamed x223, local copies, waits for them, and re-layouts  86.4 us
    all_to_all x6, waiting for transfers between devices, exchange(): return lax.all_to_all(blocks, axes, 0, 0, tiled=True)  50.8 us
    ppermute x52, starting transfers between devices, shift(): return lax.ppermute(v, ax, [(i, (i + k) % n) for i in range(n)])  37.3 us
    pallas_call x3, Pallas kernels, ffn_back(): pl.pallas_call(ffn_back_kernel, grid=(count,), in_specs=[rows, rows, mat(...  34.1 us
    pallas_call x2, Pallas kernels, ffn_in(): pl.pallas_call(functools.partial(ffn_in_kernel, [len(some) for some in st...  30.3 us
    all_to_all x6, starting transfers between devices, exchange(): return lax.all_to_all(blocks, axes, 0, 0, tiled=True)  25.5 us
    pallas_call x1, Pallas kernels, down_both(): pl.pallas_call(down_kernel, grid=(steps,), in_specs=[pl.BlockSpec((rows,...  23 us
  transfers between devices with their start and end apart: 64, of which 25 were waited for; matrix products, arithmetic and copies ran while one was open for 17% of the time, Pallas kernels for 22%

profile of v2, /device:TPU:0, one launch (start us, length us, event | category | flops | bytes accessed | tf_op | source)
XLA Modules:
  0.0 729.8 jit_solution(16663342001990164713)
XLA Ops:
  16.1 7.6 %all-to-all-done = bf16[4,80,640]{2,1,0:T(8,128)(2,1)S(1)} async-done(((bf16[4,80,640]{2,1,0:T(8,128)(2,1)}), bf16[4,80,640]{2,1,0:T(8,128)(2,1)S(1)}, u32[]{:S(2)}, u32[]{:S(2)}) %all-to-all-start) | async-done | bytes 409632 | tf_op jit(solution)/shard_map/all_to_all | solution.py:64
  38.6 20.5 %collective-permute-done.1.refs_2_.refs_1_ = bf16[320,2048]{1,0:T(8,128)(2,1)S(1)} collective-permute-done((bf16[320,2048]{1,0:T(8,128)(2,1)S(1)}, bf16[320,2048]{1,0:T(8,128)(2,1)S(1)}, u32[]{:S(2)}, u32[]{:S(2)}) %collective-permute-start.1) | collective-permute-done | bytes 1310752 | tf_op jit(solution)/shard_map/ppermute | solution.py:24
  61.6 22.9 %all-to-all-done.2 = bf16[8,3,64,688]{3,2,1,0:T(8,128)(2,1)} async-done(((bf16[8,3,64,688]{3,2,1,0:T(8,128)(2,1)}), bf16[8,3,64,688]{3,2,1,0:T(8,128)(2,1)}, u32[]{:S(2)}, u32[]{:S(2)}) %all-to-all-start.2) | async-done | bytes 2113568 | tf_op jit(solution)/shard_map/all_to_all | solution.py:64
  95.6 17.0 %collective-permute-done.4.refs_1_ = bf16[320,2048]{1,0:T(8,128)(2,1)} collective-permute-done((bf16[320,2048]{1,0:T(8,128)(2,1)}, bf16[320,2048]{1,0:T(8,128)(2,1)}, u32[]{:S(2)}, u32[]{:S(2)}) %collective-permute-start.4) | collective-permute-done | bytes 1310752 | tf_op jit(solution)/shard_map/ppermute | solution.py:24
  126.6 21.8 %collective-permute-done.3.refs_1_ = bf16[4,360,512]{2,1,0:T(8,128)(2,1)} collective-permute-done((bf16[4,360,512]{2,1,0:T(8,128)(2,1)}, bf16[4,360,512]{2,1,0:T(8,128)(2,1)}, u32[]{:S(2)}, u32[]{:S(2)}) %collective-permute-start.3) | collective-permute-done | bytes 1474592 | tf_op jit(solution)/shard_map/ppermute | solution.py:24
  161.2 7.4 %norm_in.1.a = bf16[1280,2048]{1,0:T(8,128)(2,1)} custom-call(s32[4]{0:T(128)} %pad_add_fusion.places.refs_0_, bf16[320,2048]{1,0:T(8,128)(2,1)} %copy-done.29, bf16[320,2048]{1,0:T(8,128)(2,1)} %collective-permute-done.refs_1_, bf16[320,2048]{1,0:T(8,128)(2,1)} %copy-done.28, bf16[320,2048]{1,0:T(8,128)(2,1)} %collective-permute-done.2.refs_3_, ...), custom_call_target="tpu_custom_call" | custom-call | flops 2621440 | bytes 10485760 | tf_op jit(solution)/shard_map/norm_in/pallas_call | solution.py:278
  168.6 8.8 %convolution_convert_fusion.qkv = bf16[1280,640]{1,0:T(8,128)(2,1)} fusion(bf16[1280,2048]{1,0:T(8,128)(2,1)} %norm_in.1.a, bf16[2048,640]{1,0:T(8,128)(2,1)} %bitcast.102), kind=kOutput, calls=%fused_computation.3 | convolution fusion | flops 3356262400 | bytes 9502720 | tf_op jit(solution)/shard_map/dot_general | solution.py:133
  177.4 10.8 %attention.1 = (bf16[1280,512]{1,0:T(8,128)(2,1)}, f32[1280,512]{1,0:T(8,128)}, f32[1280,4]{1,0:T(8,128)}) custom-call(bf16[1280,640]{1,0:T(8,128)(2,1)} %convolution_convert_fusion.qkv, s32[1,1280]{1,0:T(1,128)} %reshape.286.doc_row, s32[1280,1]{1,0:T(8,128)} %reshape.291.doc_col), custom_call_target="tpu_custom_call" | custom-call | flops 3355443200 | bytes 7680000 | tf_op jit(solution)/shard_map/attention/pallas_call | solution.py:194
  190.5 7.0 out_terms.1
  210.3 28.9 %collective-permute-done.10 = bf16[320,2048]{1,0:T(8,128)(2,1)} collective-permute-done((bf16[320,2048]{1,0:T(8,128)(2,1)}, bf16[320,2048]{1,0:T(8,128)(2,1)}, u32[]{:S(2)}, u32[]{:S(2)}) %collective-permute-start.10) | collective-permute-done | bytes 1310752 | tf_op jit(solution)/shard_map/ppermute | solution.py:24
  252.9 20.6 %collective-permute-done.20.refs_4_ = bf16[320,2048]{1,0:T(8,128)(2,1)S(1)} collective-permute-done((bf16[320,2048]{1,0:T(8,128)(2,1)S(1)}, bf16[320,2048]{1,0:T(8,128)(2,1)S(1)}, u32[]{:S(2)}, u32[]{:S(2)}) %collective-permute-start.20) | collective-permute-done | bytes 1310752 | tf_op jit(solution)/shard_map/ppermute | solution.py:24
  287.1 20.5 %ffn_in.2 = (bf16[2560,2048]{1,0:T(8,128)(2,1)}, f32[2560,688]{1,0:T(8,128)}, f32[2560,688]{1,0:T(8,128)}, bf16[2560,688]{1,0:T(8,128)(2,1)}) custom-call(bf16[320,2048]{1,0:T(8,128)(2,1)} %copy-done.44, bf16[320,2048]{1,0:T(8,128)(2,1)} %copy-done.95, bf16[320,2048]{1,0:T(8,128)(2,1)} %copy-done.85, bf16[320,2048]{1,0:T(8,128)(2,1)} %collective-permute-done.19.refs_3_, ...), custom_call_target="tpu_custom_call" | custom-call | flops 10821304320 | bytes 34574336 | tf_op jit(solution)/shard_map/ffn_in/pallas_call | solution.py:351
  315.1 9.8 %ffn_in.3 = (bf16[2560,2048]{1,0:T(8,128)(2,1)}, f32[2560,688]{1,0:T(8,128)}, f32[2560,688]{1,0:T(8,128)}, bf16[2560,688]{1,0:T(8,128)(2,1)}) custom-call(bf16[160,2048]{1,0:T(8,128)(2,1)} %copy-done.50, bf16[160,2048]{1,0:T(8,128)(2,1)} %copy-done.49, ...), custom_call_target="tpu_custom_call", output_to_operand_aliasing={{0}: (6, {}), {1}: (7, {}), {2}: (8, {}), {3}: (9, {})} | custom-call | flops 3607101440 | bytes 15282176 | tf_op jit(solution)/shard_map/ffn_in/pallas_call | solution.py:351
  324.8 17.9 %ffn_mid.1 = (bf16[2560,688]{1,0:T(8,128)(2,1)}, bf16[2560,688]{1,0:T(8,128)(2,1)}) custom-call(f32[2560,688]{1,0:T(8,128)} %get-tuple-element.42.gate, f32[2560,688]{1,0:T(8,128)} %get-tuple-element.43.up, bf16[2560,2048]{1,0:T(8,128)(2,1)} %copy-done.12, bf16[4,3,512,688]{3,2,1,0:T(8,128)(2,1)} %bitcast.92), custom_call_target="tpu_custom_call" | custom-call | flops 7214202880 | bytes 34439168 | tf_op jit(solution)/shard_map/ffn_mid/pallas_call | solution.py:381
  342.7 9.4 %ffn_back.3 = (bf16[320,2048]{1,0:T(8,128)(2,1)}, bf16[320,2048]{1,0:T(8,128)(2,1)}) custom-call(bf16[2560,688]{1,0:T(8,128)(2,1)} %get-tuple-element.44.dgate.refs_0_, bf16[2560,688]{1,0:T(8,128)(2,1)} %get-tuple-element.45.dup.b1, bf16[4,3,512,688]{3,2,1,0:T(8,128)(2,1)} %bitcast.93, bf16[4,3,512,688]{3,2,1,0:T(8,128)(2,1)} %bitcast.94), custom_call_target="tpu_custom_call" | custom-call | flops 3607101440 | bytes 10018816 | tf_op jit(solution)/shard_map/ffn_back/pallas_call | solution.py:406
  361.3 15.3 %ffn_back.4 = (bf16[320,2048]{1,0:T(8,128)(2,1)}, bf16[320,2048]{1,0:T(8,128)(2,1)}, bf16[320,2048]{1,0:T(8,128)(2,1)}, bf16[320,2048]{1,0:T(8,128)(2,1)}) custom-call(bf16[2560,688]{1,0:T(8,128)(2,1)} %copy-done.1, bf16[2560,688]{1,0:T(8,128)(2,1)} %get-tuple-element.45.dup.b1, bf16[4,3,512,688]{3,2,1,0:T(8,128)(2,1)} %bitcast.95, ...), custom_call_target="tpu_custom_call" | custom-call | flops 7214202880 | bytes 14401536 | tf_op jit(solution)/shard_map/ffn_back/pallas_call | solution.py:406
  388.0 9.4 %ffn_back.5 = (bf16[320,2048]{1,0:T(8,128)(2,1)}, bf16[320,2048]{1,0:T(8,128)(2,1)}) custom-call(bf16[2560,688]{1,0:T(8,128)(2,1)} %copy-done.3, bf16[2560,688]{1,0:T(8,128)(2,1)} %get-tuple-element.45.dup.b1, bf16[4,3,512,688]{3,2,1,0:T(8,128)(2,1)} %bitcast.97, bf16[4,3,512,688]{3,2,1,0:T(8,128)(2,1)} %bitcast.98), custom_call_target="tpu_custom_call" | custom-call | flops 3607101440 | bytes 10018816 | tf_op jit(solution)/shard_map/ffn_back/pallas_call | solution.py:406
  407.3 23.0 %down_both.1 = (bf16[2048,688]{1,0:T(8,128)(2,1)}, bf16[2560,2048]{1,0:T(8,128)(2,1)}) custom-call(bf16[2560,2048]{1,0:T(8,128)(2,1)} %copy-done.12, bf16[2560,688]{1,0:T(8,128)(2,1)} %copy-done.9, bf16[2560,688]{1,0:T(8,128)(2,1)} %copy-done.9, bf16[4,3,512,688]{3,2,1,0:T(8,128)(2,1)} %bitcast.99), custom_call_target="tpu_custom_call" | custom-call | flops 14428405760 | bytes 33652736 | tf_op jit(solution)/shard_map/down_both/pallas_call | solution.py:544
  436.9 5.6 fusion.16
  457.7 22.3 %pair_grad.1.refs_1_ = bf16[4,2,512,688]{3,2,1,0:T(8,128)(2,1)} custom-call(bf16[2560,2048]{1,0:T(8,128)(2,1)} %get-tuple-element.57.a, bf16[2560,688]{1,0:T(8,128)(2,1)} %copy-done.5, bf16[2560,688]{1,0:T(8,128)(2,1)} %get-tuple-element.45.dup.b1), custom_call_target="tpu_custom_call" | custom-call | flops 14428405760 | bytes 23166976 | tf_op jit(solution)/shard_map/pair_grad/pallas_call | solution.py:576
  480.0 5.8 copy.130.refs_0_
  485.9 11.2 %reduce-scatter.5.cloned.1.call-done.refs_2_ = bf16[512,688]{1,0:T(8,128)(2,1)} async-done(((bf16[2048,688]{1,0:T(8,128)(2,1)}), bf16[512,688]{1,0:T(8,128)(2,1)}) %reduce-scatter.5.cloned.1.call-update) | async-done | bytes 704528 | tf_op jit(solution)/shard_map/reduce_scatter | solution.py:804
  515.5 9.4 %dz_in.1 = (bf16[1280,2048]{1,0:T(8,128)(2,1)}, f32[1280,512]{1,0:T(8,128)}) custom-call(s32[4]{0:T(128)} %copy-done.59, bf16[320,2048]{1,0:T(8,128)(2,1)} %copy-done.46, bf16[320,2048]{1,0:T(8,128)(2,1)} %copy-done.53, bf16[320,2048]{1,0:T(8,128)(2,1)} %copy-done.17, bf16[320,2048]{1,0:T(8,128)(2,1)} %collective-permute-done.40.refs_3_, ...), custom_call_target="tpu_custom_call" | custom-call | flops 2684354560 | bytes 15728640 | tf_op jit(solution)/shard_map/dz_in/pallas_call | solution.py:445
  524.9 7.1 weight_grad.2.refs_1_
  532.0 4.6 all-to-all-start.3
  547.1 19.9 %attention_back.1.refs_0_ = bf16[1280,640]{1,0:T(8,128)(2,1)} custom-call(bf16[1280,640]{1,0:T(8,128)(2,1)} %convolution_convert_fusion.qkv, s32[1,1280]{1,0:T(1,128)} %reshape.286.doc_row, s32[1280,1]{1,0:T(8,128)} %reshape.291.doc_col, f32[1280,512]{1,0:T(8,128)} %get-tuple-element.55.out, f32[1280,4]{1,0:T(8,128)} %get-tuple-element.56.den, ...), custom_call_target="tpu_custom_call" | custom-call | flops 8388608000 | bytes 10240000 | tf_op jit(solution)/shard_map/attention_back/pallas_call | solution.py:244
  576.8 13.6 %collective-permute-done.45.refs_4_ = bf16[160,2048]{1,0:T(8,128)(2,1)} collective-permute-done((bf16[160,2048]{1,0:T(8,128)(2,1)S(1)}, bf16[160,2048]{1,0:T(8,128)(2,1)}, u32[]{:S(2)}, u32[]{:S(2)}) %collective-permute-start.45) | collective-permute-done | bytes 655392 | tf_op jit(solution)/shard_map/ppermute | solution.py:24
  590.4 4.4 fusion.22.refs_1_
  605.7 8.0 %weight_grad.3.refs_1_ = bf16[2048,640]{1,0:T(8,128)(2,1)} custom-call(bf16[1280,2048]{1,0:T(8,128)(2,1)} %norm_in.1.a, bf16[1280,640]{1,0:T(8,128)(2,1)} %copy-done.40), custom_call_target="tpu_custom_call" | custom-call | flops 3355443200 | bytes 9502720 | tf_op jit(solution)/shard_map/weight_grad/pallas_call | solution.py:471
  624.3 23.4 %collective-permute-done.51 = bf16[4,256,640]{2,1,0:T(8,128)(2,1)} collective-permute-done((bf16[4,256,640]{2,1,0:T(8,128)(2,1)}, bf16[4,256,640]{2,1,0:T(8,128)(2,1)}, u32[]{:S(2)}, u32[]{:S(2)}) %collective-permute-start.51) | collective-permute-done | bytes 1310752 | tf_op jit(solution)/shard_map/ppermute | solution.py:24
  650.5 4.5 collective-permute-done.50
  682.0 17.1 %all-to-all-done.4.g = bf16[8,3,64,688]{3,2,1,0:T(8,128)(2,1)} async-done(((bf16[8,3,64,688]{3,2,1,0:T(8,128)(2,1)}), bf16[8,3,64,688]{3,2,1,0:T(8,128)(2,1)}, u32[]{:S(2)}, u32[]{:S(2)}) %all-to-all-start.4) | async-done | bytes 2113568 | tf_op jit(solution)/shard_map/all_to_all | solution.py:64
  (468 shorter events, 278.7 us)
Async XLA Ops:
  16.1 71.8 %all-gather.3.cloned.1.call-start = ((), (), s32[]{:S(2)}) async-start(), calls=%async_computation.10 | async-start | bytes 3153920 | tf_op jit(solution)/shard_map/all_gather | solution.py:682
  27.4 31.7 %collective-permute-start.1 = (bf16[320,2048]{1,0:T(8,128)(2,1)S(1)}, bf16[320,2048]{1,0:T(8,128)(2,1)S(1)}, u32[]{:S(2)}, u32[]{:S(2)}) collective-permute-start(bf16[320,2048]{1,0:T(8,128)(2,1)S(1)} %after.31.refs_0_), channel_id=1, source_target_pairs={{0,2},{2,0},{1,3},{3,1},{4,6},{6,4},{5,7},{7,5},{8,10},{10,8},{9,1... | collective-permute-start | bytes 3932168 | tf_op jit(solution)/shard_map/ppermute | solution.py:24
  27.8 32.1 %collective-permute-start.5 = (bf16[320,2048]{1,0:T(8,128)(2,1)}, bf16[320,2048]{1,0:T(8,128)(2,1)}, u32[]{:S(2)}, u32[]{:S(2)}) collective-permute-start(bf16[320,2048]{1,0:T(8,128)(2,1)} %after.32.refs_0_), channel_id=1, source_target_pairs={{0,4},{4,0},{1,5},{5,1},{2,6},{6,2},{3,7},{7,3},{8,12},{12,8},{9,1... | collective-permute-start | bytes 3932168 | tf_op jit(solution)/shard_map/ppermute | solution.py:24
  34.2 50.3 %all-to-all-start.2 = ((bf16[8,3,64,688]{3,2,1,0:T(8,128)(2,1)}), bf16[8,3,64,688]{3,2,1,0:T(8,128)(2,1)}, u32[]{:S(2)}, u32[]{:S(2)}) async-start(bf16[8,3,64,688]{3,2,1,0:T(8,128)(2,1)} %split.1), calls=%async_computation.2 | async-start | bytes 4718592 | tf_op jit(solution)/shard_map/all_to_all | solution.py:64
  38.5 248.6 %all-gather.5.cloned.1.call-start = ((), (), s32[]{:S(2)}) async-start(), calls=%async_computation.11 | async-start | bytes 11796480 | tf_op jit(solution)/shard_map/all_gather | solution.py:682
  59.9 52.7 %collective-permute-start.4 = (bf16[320,2048]{1,0:T(8,128)(2,1)}, bf16[320,2048]{1,0:T(8,128)(2,1)}, u32[]{:S(2)}, u32[]{:S(2)}) collective-permute-start(bf16[320,2048]{1,0:T(8,128)(2,1)} %after.33), channel_id=1, source_target_pairs={{0,2},{2,0},{1,3},{3,1},{4,6},{6,4},{5,7},{7,5},{8,10},{10,8},{9,1... | collective-permute-start | bytes 3932168 | tf_op jit(solution)/shard_map/ppermute | solution.py:24
  92.4 68.8 %collective-permute-start = (bf16[320,2048]{1,0:T(8,128)(2,1)}, bf16[320,2048]{1,0:T(8,128)(2,1)}, u32[]{:S(2)}, u32[]{:S(2)}) collective-permute-start(bf16[320,2048]{1,0:T(8,128)(2,1)} %copy-done.29), channel_id=1, source_target_pairs={{0,1},{1,0},{2,3},{3,2},{4,5},{5,4},{6,7},{7,6},{8,9},{9,8},{10,11... | collective-permute-start | bytes 3932168 | tf_op jit(solution)/shard_map/ppermute | solution.py:24
  94.4 95.1 %collective-permute-start.6 = (bf16[160,2048]{1,0:T(8,128)(2,1)}, bf16[160,2048]{1,0:T(8,128)(2,1)S(1)}, u32[]{:S(2)}, u32[]{:S(2)}) collective-permute-start(bf16[160,2048]{1,0:T(8,128)(2,1)} %slice.259), channel_id=1, source_target_pairs={{0,2},{2,0},{1,3},{3,1},{4,6},{6,4},{5,7},{7,5},{8,10},{10,8},{9,1... | collective-permute-start | bytes 1966088 | tf_op jit(solution)/shard_map/ppermute | solution.py:24
  95.4 65.8 %collective-permute-start.2 = (bf16[320,2048]{1,0:T(8,128)(2,1)}, bf16[320,2048]{1,0:T(8,128)(2,1)}, u32[]{:S(2)}, u32[]{:S(2)}) collective-permute-start(bf16[320,2048]{1,0:T(8,128)(2,1)} %copy-done.28), channel_id=1, source_target_pairs={{0,1},{1,0},{2,3},{3,2},{4,5},{5,4},{6,7},{7,6},{8,9},{9,8},{10,11... | collective-permute-start | bytes 3932168 | tf_op jit(solution)/shard_map/ppermute | solution.py:24
  115.8 32.5 %collective-permute-start.3 = (bf16[4,360,512]{2,1,0:T(8,128)(2,1)}, bf16[4,360,512]{2,1,0:T(8,128)(2,1)}, u32[]{:S(2)}, u32[]{:S(2)}) collective-permute-start(bf16[4,360,512]{2,1,0:T(8,128)(2,1)} %slice.250), channel_id=1, source_target_pairs={{0,4},{4,0},{1,5},{5,1},{2,6},{6,2},{3,7},{7,3},{8,12},{12,8},{9,1... | collective-permute-start | bytes 4423688 | tf_op jit(solution)/shard_map/ppermute | solution.py:24
  148.3 41.1 %collective-permute-start.7 = (bf16[160,2048]{1,0:T(8,128)(2,1)}, bf16[160,2048]{1,0:T(8,128)(2,1)S(1)}, u32[]{:S(2)}, u32[]{:S(2)}) collective-permute-start(bf16[160,2048]{1,0:T(8,128)(2,1)} %after.34), channel_id=1, source_target_pairs={{0,4},{4,0},{1,5},{5,1},{2,6},{6,2},{3,7},{7,3},{8,12},{12,8},{9,1... | collective-permute-start | bytes 1966088 | tf_op jit(solution)/shard_map/ppermute | solution.py:24
  150.4 40.2 %all-to-all-start.1 = ((bf16[8,256,512]{2,1,0:T(8,128)(2,1)}), bf16[8,256,512]{2,1,0:T(8,128)(2,1)}, u32[]{:S(2)}, u32[]{:S(2)}) async-start(bf16[8,256,512]{2,1,0:T(8,128)(2,1)} %after.36), calls=%async_computation.1 | async-start | bytes 4194304 | tf_op jit(solution)/shard_map/all_to_all | solution.py:64
  154.7 342.3 %reduce-scatter.5.cloned.1.call-start = ((), (), s32[]{:S(2)}) async-start(), calls=%async_computation.12 | async-start | bytes 3932160 | tf_op jit(solution)/shard_map/reduce_scatter | solution.py:804
  207.8 31.4 %collective-permute-start.10 = (bf16[320,2048]{1,0:T(8,128)(2,1)}, bf16[320,2048]{1,0:T(8,128)(2,1)}, u32[]{:S(2)}, u32[]{:S(2)}) collective-permute-start(bf16[320,2048]{1,0:T(8,128)(2,1)} %add_convert_fusion.5), channel_id=1, source_target_pairs={{0,2},{2,0},{1,3},{3,1},{4,6},{6,4},{5,7},{7,5},{8,10},{10,8},{9,1... | collective-permute-start | bytes 3932168 | tf_op jit(solution)/shard_map/ppermute | solution.py:24
  209.7 38.2 %collective-permute-start.11 = (bf16[320,2048]{1,0:T(8,128)(2,1)}, bf16[320,2048]{1,0:T(8,128)(2,1)}, u32[]{:S(2)}, u32[]{:S(2)}) collective-permute-start(bf16[320,2048]{1,0:T(8,128)(2,1)} %after.33), channel_id=1, source_target_pairs={{0,1},{1,0},{2,3},{3,2},{4,5},{5,4},{6,7},{7,6},{8,9},{9,8},{10,11... | collective-permute-start | bytes 3932168 | tf_op jit(solution)/shard_map/ppermute | solution.py:24
  209.7 41.7 %collective-permute-start.12 = (bf16[320,2048]{1,0:T(8,128)(2,1)}, bf16[320,2048]{1,0:T(8,128)(2,1)}, u32[]{:S(2)}, u32[]{:S(2)}) collective-permute-start(bf16[320,2048]{1,0:T(8,128)(2,1)} %collective-permute-done.5.refs_2_), channel_id=1, source_target_pairs={{0,1},{1,0},{2,3},{3,2},{4,5},{5,4},{6,7},{7,6},{8,9},{9,8},{10,11... | collective-permute-start | bytes 3932168 | tf_op jit(solution)/shard_map/ppermute | solution.py:24
  397.6 32.7 %collective-permute-start.31 = (bf16[160,2048]{1,0:T(8,128)(2,1)}, bf16[160,2048]{1,0:T(8,128)(2,1)}, u32[]{:S(2)}, u32[]{:S(2)}) collective-permute-start(bf16[160,2048]{1,0:T(8,128)(2,1)} %slice.332.refs_2_), channel_id=1, source_target_pairs={{0,2},{2,0},{1,3},{3,1},{4,6},{6,4},{5,7},{7,5},{8,10},{10,8},{9,1... | collective-permute-start | bytes 1966088 | tf_op jit(solution)/shard_map/ppermute | solution.py:24
  398.1 32.2 %collective-permute-start.33 = (bf16[160,2048]{1,0:T(8,128)(2,1)}, bf16[160,2048]{1,0:T(8,128)(2,1)}, u32[]{:S(2)}, u32[]{:S(2)}) collective-permute-start(bf16[160,2048]{1,0:T(8,128)(2,1)} %slice.333.refs_1_), channel_id=1, source_target_pairs={{0,4},{4,0},{1,5},{5,1},{2,6},{6,2},{3,7},{7,3},{8,12},{12,8},{9,1... | collective-permute-start | bytes 1966088 | tf_op jit(solution)/shard_map/ppermute | solution.py:24
  436.4 181.5 %reduce-scatter.7.cloned.1.call-start = ((), (), s32[]{:S(2)}) async-start(), calls=%async_computation.13 | async-start | bytes 7864320 | tf_op jit(solution)/shard_map/reduce_scatter | solution.py:817
  443.5 42.4 %collective-permute-start.39 = (bf16[320,2048]{1,0:T(8,128)(2,1)S(1)}, bf16[320,2048]{1,0:T(8,128)(2,1)S(1)}, u32[]{:S(2)}, u32[]{:S(2)}) collective-permute-start(bf16[320,2048]{1,0:T(8,128)(2,1)S(1)} %get-tuple-element.63.refs_0_.refs_1_), channel_id=1, source_target_pairs={{0,2},{2,0},{1,3},{3,1},{4,6},{6,4},{5,7},{7,5},{8,10},{10,8},{9,1... | collective-permute-start | bytes 3932168 | tf_op jit(solution)/shard_map/ppermute | solution.py:24
  532.0 35.0 %all-to-all-start.3 = ((bf16[8,64,2048]{2,1,0:T(8,128)(2,1)}), bf16[8,64,2048]{2,1,0:T(8,128)(2,1)}, u32[]{:S(2)}, u32[]{:S(2)}) async-start(bf16[8,64,2048]{2,1,0:T(8,128)(2,1)} %bitcast.82), calls=%async_computation.3 | async-start | bytes 4194304 | tf_op jit(solution)/shard_map/all_to_all | solution.py:64
  536.6 121.7 %reduce-scatter.9.cloned.1.call-start = ((), (), s32[]{:S(2)}) async-start(), calls=%async_computation.14 | async-start | bytes 1310720 | tf_op jit(solution)/shard_map/reduce_scatter | solution.py:828
  538.7 38.2 %collective-permute-start.44 = (bf16[160,2048]{1,0:T(8,128)(2,1)}, bf16[160,2048]{1,0:T(8,128)(2,1)}, u32[]{:S(2)}, u32[]{:S(2)}) collective-permute-start(bf16[160,2048]{1,0:T(8,128)(2,1)} %slice.285), channel_id=1, source_target_pairs={{0,4},{4,0},{1,5},{5,1},{2,6},{6,2},{3,7},{7,3},{8,12},{12,8},{9,1... | collective-permute-start | bytes 1966088 | tf_op jit(solution)/shard_map/ppermute | solution.py:24
  540.5 36.3 %collective-permute-start.43 = (bf16[160,2048]{1,0:T(8,128)(2,1)}, bf16[160,2048]{1,0:T(8,128)(2,1)}, u32[]{:S(2)}, u32[]{:S(2)}) collective-permute-start(bf16[160,2048]{1,0:T(8,128)(2,1)} %slice.284), channel_id=1, source_target_pairs={{0,2},{2,0},{1,3},{3,1},{4,6},{6,4},{5,7},{7,5},{8,10},{10,8},{9,1... | collective-permute-start | bytes 1966088 | tf_op jit(solution)/shard_map/ppermute | solution.py:24
  543.3 47.1 %collective-permute-start.45 = (bf16[160,2048]{1,0:T(8,128)(2,1)S(1)}, bf16[160,2048]{1,0:T(8,128)(2,1)}, u32[]{:S(2)}, u32[]{:S(2)}) collective-permute-start(bf16[160,2048]{1,0:T(8,128)(2,1)S(1)} %add_convert_fusion.7.refs_1_), channel_id=1, source_target_pairs={{0,4},{4,0},{1,5},{5,1},{2,6},{6,2},{3,7},{7,3},{8,12},{12,8},{9,1... | collective-permute-start | bytes 1966088 | tf_op jit(solution)/shard_map/ppermute | solution.py:24
  545.2 45.2 %collective-permute-start.46 = (bf16[160,2048]{1,0:T(8,128)(2,1)S(1)}, bf16[160,2048]{1,0:T(8,128)(2,1)}, u32[]{:S(2)}, u32[]{:S(2)}) collective-permute-start(bf16[160,2048]{1,0:T(8,128)(2,1)S(1)} %add_convert_fusion.6.refs_2_), channel_id=1, source_target_pairs={{0,2},{2,0},{1,3},{3,1},{4,6},{6,4},{5,7},{7,5},{8,10},{10,8},{9,1... | collective-permute-start | bytes 1966088 | tf_op jit(solution)/shard_map/ppermute | solution.py:24
  616.4 31.4 %collective-permute-start.51 = (bf16[4,256,640]{2,1,0:T(8,128)(2,1)}, bf16[4,256,640]{2,1,0:T(8,128)(2,1)}, u32[]{:S(2)}, u32[]{:S(2)}) collective-permute-start(bf16[4,256,640]{2,1,0:T(8,128)(2,1)} %dynamic-slice_bitcast_fusion), channel_id=1, source_target_pairs={{0,4},{4,0},{1,5},{5,1},{2,6},{6,2},{3,7},{7,3},{8,12},{12,8},{9,1... | collective-permute-start | bytes 3932168 | tf_op jit(solution)/shard_map/ppermute | solution.py:24
  617.9 32.6 %collective-permute-start.48 = (bf16[320,2048]{1,0:T(8,128)(2,1)}, bf16[320,2048]{1,0:T(8,128)(2,1)}, u32[]{:S(2)}, u32[]{:S(2)}) collective-permute-start(bf16[320,2048]{1,0:T(8,128)(2,1)} %get-tuple-element.67), channel_id=1, source_target_pairs={{0,1},{1,0},{2,3},{3,2},{4,5},{5,4},{6,7},{7,6},{8,9},{9,8},{10,11... | collective-permute-start | bytes 3932168 | tf_op jit(solution)/shard_map/ppermute | solution.py:24
  619.4 87.2 %reduce-scatter.11.cloned.1.call-start = ((), (), s32[]{:S(2)}) async-start(), calls=%async_computation.15 | async-start | bytes 1638400 | tf_op jit(solution)/shard_map/reduce_scatter | solution.py:639
  623.5 31.5 %collective-permute-start.50 = (bf16[320,2048]{1,0:T(8,128)(2,1)}, bf16[320,2048]{1,0:T(8,128)(2,1)}, u32[]{:S(2)}, u32[]{:S(2)}) collective-permute-start(bf16[320,2048]{1,0:T(8,128)(2,1)} %add_convert_fusion), channel_id=1, source_target_pairs={{0,2},{2,0},{1,3},{3,1},{4,6},{6,4},{5,7},{7,5},{8,10},{10,8},{9,1... | collective-permute-start | bytes 3932168 | tf_op jit(solution)/shard_map/ppermute | solution.py:24
  624.3 49.8 %collective-permute-start.47 = (bf16[320,2048]{1,0:T(8,128)(2,1)}, bf16[320,2048]{1,0:T(8,128)(2,1)}, u32[]{:S(2)}, u32[]{:S(2)}) collective-permute-start(bf16[320,2048]{1,0:T(8,128)(2,1)} %get-tuple-element.70), channel_id=1, source_target_pairs={{0,1},{1,0},{2,3},{3,2},{4,5},{5,4},{6,7},{7,6},{8,9},{9,8},{10,11... | collective-permute-start | bytes 3932168 | tf_op jit(solution)/shard_map/ppermute | solution.py:24
  666.2 32.9 %all-to-all-start.4 = ((bf16[8,3,64,688]{3,2,1,0:T(8,128)(2,1)}), bf16[8,3,64,688]{3,2,1,0:T(8,128)(2,1)}, u32[]{:S(2)}, u32[]{:S(2)}) async-start(bf16[8,3,64,688]{3,2,1,0:T(8,128)(2,1)} %maximum_bitcast_fusion), calls=%async_computation.8 | async-start | bytes 4718592 | tf_op jit(solution)/shard_map/all_to_all | solution.py:64
  (131 other events, 944.0 us)
Sparse Core Ops, SparseCore 0:
  24.9 54.1 all-gather.2
  89.7 167.7 all-gather.4
  436.6 60.4 reduce-scatter.4
  503.8 110.7 reduce-scatter.6
  619.5 26.3 reduce-scatter.8
  661.9 30.3 reduce-scatter.10

commit v3 on v2

--- a/solution.py
+++ b/solution.py
@@ -112,7 +112,12 @@
             lax.dynamic_slice_in_dim(partial, place_of(ry, rc) * rows, rows, 0) for rc in range(nc)
         ]
         sums.append(ring_sum(terms, "c"))
-    return ring_sum(sums, "y")
+    if ny == 1:
+        return sums[0], jnp.zeros_like(sums[0], BF)
+    acc = sums[-1]
+    for k in range(ny - 2, 0, -1):
+        acc = sums[k] + shift(acc.astype(BF), "y", -1).astype(F32)
+    return sums[0], shift(acc.astype(BF), "y", -1)
 
 
 def wide_gather(v, both):
@@ -254,6 +259,83 @@
     )(qkv, doc[None, :], doc[:, None], out, den, grad)
 
 
+def qkv_in_kernel(places, at, *refs):
+    n = places.shape[0]
+    pieces, parts = refs[:n], refs[n : n + 2]
+    a_out, qkv_out, w, gains, a_ref = refs[-5:]
+    nz, _, main = parts[0].shape
+    own = parts[0].shape[1] - 80
+    quarter = own // 4
+
+    @pl.when(pl.program_id(0) == 0)
+    def _():
+        for z in range(nz):
+            for k, part in enumerate(parts):
+                base = pl.multiple_of((2 * z + at[k]) * own, own)
+                w[pl.ds(base, own), :main] = part[z, :own, :]
+                rows = part[z, own + 64 : own + 80, :].astype(F32)
+                g = []
+                for t in range(4):
+                    there = pl.multiple_of(base + quarter * t, quarter)
+                    lanes = slice(128 * t, 128 * (t + 1))
+                    w[pl.ds(there, quarter), main:] = part[z, own : own + quarter, lanes]
+                    g.append((rows[:1, 128 * t :][:, :64], rows[:1, 128 * t + 64 :][:, :64]))
+                for m in range(2):
+                    gains[m : m + 1, pl.ds(base, own)] = jnp.concatenate([p[m] for p in g], axis=1)
+
+    for k, piece in enumerate(pieces):
+
+        @pl.when(pl.program_id(0) == k)
+        def _(piece=piece):
+            x = piece[...].astype(F32)
+            a_ref[...] = (x * inverse_rms(x) * gains[:1, :]).astype(BF)
+
+    a = a_ref[...]
+    a_out[...] = a
+    qkv_out[...] = dot(a, w[...], NN, BF)
+
+
+def qkv_in(pieces, places, parts, at):
+    n = len(pieces)
+    rows, d = pieces[0].shape
+    width = parts[0].shape[2] + 128
+
+    def row_block(i, places, at):
+        return (places[i], 0)
+
+    def still(a):
+        zeros = (0,) * len(a.shape)
+        return pl.BlockSpec(a.shape, lambda i, places, at: zeros, pipeline_mode=pl.Buffered(1))
+
+    def fixed(i, places, at):
+        return (0, 0)
+
+    return pl.pallas_call(
+        qkv_in_kernel,
+        grid_spec=pltpu.PrefetchScalarGridSpec(
+            num_scalar_prefetch=2,
+            grid=(n,),
+            in_specs=[still(p) for p in pieces] + [still(p) for p in parts],
+            out_specs=(
+                pl.BlockSpec((rows, d), row_block),
+                pl.BlockSpec((rows, width), row_block),
+                pl.BlockSpec((d, width), fixed),
+                pl.BlockSpec((2, d), fixed),
+            ),
+            scratch_shapes=[pltpu.VMEM((rows, d), BF)],
+        ),
+        out_shape=(
+            jax.ShapeDtypeStruct((n * rows, d), BF),
+            jax.ShapeDtypeStruct((n * rows, width), BF),
+            jax.ShapeDtypeStruct((d, width), BF),
+            jax.ShapeDtypeStruct((2, d), F32),
+        ),
+        compiler_params=params(),
+        cost_estimate=cost(2 * n * rows * d * width, 6 * n * rows * d),
+        name="qkv_in",
+    )(places, at, *pieces, *parts)
+
+
 def norm_in_kernel(places, *refs):
     pieces, gain = refs[: places.shape[0]], refs[places.shape[0]]
     a_out = refs[-1]
@@ -532,9 +614,14 @@
     )(*mats)
 
 
-def down_kernel(dy, hid, hid_rows, wd, grad, terms):
+def down_kernel(dy, hid, hid_rows, wd, grad, *terms):
     grad[...] = dot(dy[...], hid[...], TN, BF)
-    terms[...] = dot(hid_rows[...], rows_of(wd), NT, BF)
+    term = dot(hid_rows[...], rows_of(wd), NT, BF)
+    for step, out in enumerate(terms):
+
+        @pl.when(pl.program_id(0) == step)
+        def _(out=out):
+            out[...] = term
 
 
 def down_both(dy, hid, w):
@@ -552,19 +639,18 @@
         ],
         out_specs=(
             pl.BlockSpec((d // steps, ff), lambda i: (i, 0)),
-            pl.BlockSpec((rows // steps, d), lambda i: (i, 0)),
-        ),
-        out_shape=(
-            jax.ShapeDtypeStruct((d, ff), BF),
-            jax.ShapeDtypeStruct((rows, d), BF),
-        ),
+        )
+        + (pl.BlockSpec((rows // steps, d), lambda i: (0, 0)),) * steps,
+        out_shape=(jax.ShapeDtypeStruct((d, ff), BF),)
+        + (jax.ShapeDtypeStruct((rows // steps, d), BF),) * steps,
         compiler_params=params(),
         cost_estimate=cost(4 * rows * d * ff, 4 * (rows * d + rows * ff + d * ff)),
         name="down_both",
     )(dy, hid, hid, w)
 
 
-def pair_grad_kernel(a, b0, b1, out):
+def pair_grad_kernel(a, b0, b1, out, mark):
+    mark[...] = jnp.zeros_like(mark)
     out[0, 0] = dot(a[...], b0[...], TN, BF)
     out[0, 1] = dot(a[...], b1[...], TN, BF)
 
@@ -577,8 +663,14 @@
         pair_grad_kernel,
         grid=(parts,),
         in_specs=[pl.BlockSpec((rows, block), lambda i: (0, i)), whole(b0), whole(b1)],
-        out_specs=pl.BlockSpec((1, 2, block, n), lambda i: (i, 0, 0, 0)),
-        out_shape=jax.ShapeDtypeStruct((parts, 2, block, n), BF),
+        out_specs=(
+            pl.BlockSpec((1, 2, block, n), lambda i: (i, 0, 0, 0)),
+            pl.BlockSpec((8, 128), lambda i: (0, 0)),
+        ),
+        out_shape=(
+            jax.ShapeDtypeStruct((parts, 2, block, n), BF),
+            jax.ShapeDtypeStruct((8, 128), F32),
+        ),
         compiler_params=params(),
         cost_estimate=cost(4 * rows * m * n, 2 * (rows * (m + 2 * n) + 2 * m * n)),
         name="pair_grad",
@@ -630,13 +722,12 @@
     )(g)
 
 
-def sum_rows(g, *deps):
+def sum_rows(g):
     nx = lax.axis_size("x")
     x = index("x")
     terms = [lax.dynamic_index_in_dim(g, (x - k + nx) % nx, 1, False) for k in range(nx)]
     mine = ring_sum(terms, "x").astype(BF)
-    mine = after(mine.reshape(-1, mine.shape[-1]), *deps)
-    return mine, lax.psum_scatter(mine, "z", scatter_dimension=0, tiled=True)
+    return terms[-1], mine.reshape(-1, mine.shape[-1])
 
 
 def per_device(both, tokens, segments, cotangent, wq, wk, wv, wo, wg, wu, wd, g1, g2):
@@ -662,7 +753,6 @@
     )
     pack = exchange(pack, ("y", "c"))
     doc = pack[:, own + 8, :rows].astype(jnp.int32).reshape(stream)
-    pack = pack[:, : own + 8]
 
     group = ("x", "y", "c") if both else ("y", "c")
     sizes = (nx, ny, nc) if both else (ny, nc)
@@ -672,7 +762,8 @@
     na = nz if both else nz * nx
     blocks = split_columns(order_of(sizes), (wg, wu, wd))
     vy = ring(after(tokens, pack), "y")
-    got = exchange(blocks, group).transpose(1, 0, 2, 3).reshape(-1, ff)
+    exchanged = exchange(blocks, group)
+    got = exchanged.transpose(1, 0, 2, 3).reshape(-1, ff)
     late = after(cotangent, pack)
     dy_x = shift(late, "x")
 
@@ -684,15 +775,14 @@
     def by_x(pieces):
         return jnp.concatenate(absolute([p[:, None] for p in pieces], "x"), axis=1)
 
-    tall = ns * (own + 8)
-    pack = pack.reshape(tall, width)
-    joint_form = ns == nz and width % 512 == 128 and d % 512 == 0 and tall % 32 == 0
+    joint_form = ns == nz == 4 and nx == 2 and own == 64 and width == 640 and d % 512 == 0
     if joint_form:
-        left = [pack[k * tall // 4 : (k + 1) * tall // 4, width - 128 :] for k in range(4)]
+        left = jnp.concatenate([pack[t, :own, 512:] for t in range(ns)], axis=1)
+        extra = jnp.concatenate([pack[t, own : own + 8, :128] for t in range(ns)], axis=1)
         some = [wo[:, k : k + 512].astype(BF) for k in range(0, d, 512)]
-        stacked = [pack[:, : width - 128], jnp.concatenate(left, axis=1)] + some
+        stacked = [pack[:, :own, :512].reshape(ns * own, 512), left, extra, extra] + some
         joint = gather(jnp.concatenate(stacked, axis=0), "z").reshape(nz, -1, 512)
-        cut = tall + tall // 4
+        cut = ns * own + own + 16
         qkv_parts = ring(joint[:, :cut], "x")
         units = [order_of((ny, nc))[t % ns] for t in range(nx * ns)]
         out_w = jnp.stack([joint[u, cut:] for u in units])
@@ -700,52 +790,50 @@
         out_w = out_w.reshape(nx * ns, d // 512, own, 512)
         arrived_last = [joint]
 
-        def qkv_of(m):
-            rest = m[:, tall:].reshape(nz, tall // 4, 4, 128).transpose(0, 2, 1, 3)
-            return jnp.concatenate([m[:, :tall], rest.reshape(nz, tall, 128)], axis=2)
-
     else:
         perm = []
         for dp in range(ndp):
             for u in range(ns):
                 perm.append((u * ndp + dp, dp * ns + u % ny * nc + u // ny))
-        qkv_z = gather(pack, "z")
+        tall = ns * (own + 8)
+        qkv_z = gather(pack[:, : own + 8].reshape(tall, width), "z")
         out_z = gather(lax.ppermute(wo.astype(BF), everything, perm), "z")
         qkv_parts = ring(qkv_z.reshape(nz, tall, width), "x")
         out_w = by_x(ring(out_z.reshape(nz, own, d), "x"))
         out_w = out_w.reshape(1, -1, d // 256, 256).transpose(0, 2, 1, 3)
         arrived_last = [qkv_z, out_z]
 
-        def qkv_of(m):
-            return m
-
     got = after(got, vy[-1], dy_x, *arrived_last)
     ffn_w = gather(got, along).reshape(na, 3, d // na, ff)
-    qkv_all = by_x([qkv_of(m) for m in qkv_parts]).reshape(ndp * ns, own + 8, width)
-    qkv_mat = qkv_all[:, :own].reshape(d, width)
-    gains = qkv_all[:, own, : 2 * own].astype(F32)
-    gain_one, gain_two = gains[:, :own].reshape(1, d), gains[:, own:].reshape(1, d)
-
     x_pieces = [ring(p, "c") for p in vy]
     places = jnp.stack([place_of(ry, rc) for ry in range(ny) for rc in range(nc)])
     flat = [p for some in x_pieces for p in some]
-    a_all = norm_in(flat, places, gain_one)
-    late = after(late, x_pieces[-1][0])
+    if joint_form:
+        at = jnp.stack([index("x"), 1 - index("x")])
+        a_all, qkv, qkv_mat, gains = qkv_in(flat, places, qkv_parts, at)
+        gain_one, gain_two = gains[:1], gains[1:]
+    else:
+        qkv_all = by_x(qkv_parts).reshape(ndp * ns, own + 8, width)
+        qkv_mat = qkv_all[:, :own].reshape(d, width)
+        gains = qkv_all[:, own, : 2 * own].astype(F32)
+        gain_one, gain_two = gains[:, :own].reshape(1, d), gains[:, own:].reshape(1, d)
+        a_all = norm_in(flat, places, gain_one)
+        qkv = dot(a_all, qkv_mat, NN, BF)
+    late = after(late, exchanged)
     if both:
         half = rows // 2
-        dy_y = shift(late, "y")
+        dy_x, dy_y = after(dy_x, qkv_parts[-1]), after(shift(late, "y"), qkv_parts[-1])
         dy_near = [dy_y]
-        dy_far = [shift(dy_x[:half], "y"), shift(after(dy_y[half:], qkv_parts[-1]), "x")]
+        dy_far = [shift(dy_x[:half], "y"), shift(dy_y[half:], "x")]
         dy_groups = [[late], [dy_x], [dy_y], dy_far]
     else:
         dy_groups = [[p] for p in ring(late, "y")]
         dy_near, dy_far = dy_groups[1], dy_groups[-1]
     dy_groups = [(g, [shift(p, "c") for p in g]) for g in dy_groups]
     dy_all = jnp.concatenate([p for mine, theirs in dy_groups for p in mine + theirs], axis=0)
-    qkv = dot(a_all, qkv_mat, NN, BF)
     att, o, den = attention(qkv, doc, heads, fk, fv)
-    branch = stream_sum(out_terms(after(att, *dy_near, *dy_far), out_w), rows)
-    residual = tokens.astype(F32) + branch
+    mine, got_r = stream_sum(out_terms(after(att, *dy_near, *dy_far), out_w), rows)
+    residual = tokens.astype(F32) + mine + got_r.astype(F32)
     inv_mlp = inverse_rms(residual)
     normed_res = residual * inv_mlp
     b = (normed_res * gain_two).astype(BF)
@@ -785,8 +873,8 @@
         mine = back([0], dgate)[0]
         own_term = joined(*mine)
         hidden = after(hidden, x_up, y_low, own_term)
-        grad_down, ffn_terms = down_both(dy_all, hidden, ffn_w)
-        own_term = after(own_term, grad_down)
+        grad_down, *blocks = down_both(dy_all, hidden, ffn_w)
+        own_term = after(own_term, blocks[0])
         db = jnp.concatenate(
             [
                 own_term[:half] + send(y_up, "y") + send(x_up, "x"),
@@ -796,7 +884,7 @@
         )
     else:
         terms = [joined(*t) for t in back(list(range(count)), dgate)]
-        grad_down, ffn_terms = down_both(dy_all, hidden, ffn_w)
+        grad_down, *blocks = down_both(dy_all, hidden, ffn_w)
         db = ring_sum(terms, "y")
     dr = cotangent.astype(F32) + rms_back(db * gain_two, normed_res, inv_mlp)
 
@@ -806,51 +894,56 @@
     dz_own = ring(dz, "c")
     arrived = dz_y[-1]
     soon = dz_own[-1]
-    blocks = [ffn_terms[g * rows : (g + 1) * rows] for g in range(2 * count)]
     others = [shift(blocks[2 * g + 1], "c") for g in range(count)]
     first = [
         (blocks[2 * g].astype(F32) + others[g].astype(F32)).astype(BF) for g in range(1, count)
     ]
-    grad_in = pair_grad(b_all, after(dgate, soon, *first), dup, na)
-    dz_pieces = [dz_own] + [ring(after(p, grad_in), "c") for p in dz_y[1:]]
-    places = after(places, grad_in)
+    grad_in, mark = pair_grad(b_all, after(dgate, soon, *first), dup, na)
+    dz_pieces = [dz_own] + [ring(after(p, mark), "c") for p in dz_y[1:]]
+    dz_all, dc = dz_in([p for some in dz_pieces for p in some], places, out_w)
+    far_got = shift(after(first[-1][: rows // 2], arrived), "y")
+    grad_wo = weight_grad(att, after(dz_all, far_got))
     in_sum = lax.psum_scatter(
-        after(grad_in.reshape(-1, ff), arrived, down_sum), along, scatter_dimension=0, tiled=True
+        after(grad_in.reshape(-1, ff), grad_wo, down_sum),
+        along,
+        scatter_dimension=0,
+        tiled=True,
     )
-    dz_all, dc = dz_in([p for some in dz_pieces for p in some], places, out_w)
-    grad_wo = weight_grad(att, dz_all)
-    if joint_form:
-        g = exchange(grad_wo.reshape(nx * ns, own, d), ("x", "y", "c"))
-        g = jnp.sum(g.reshape(nx, ns, own, d).astype(F32), axis=0).astype(BF)
-        wo_mine = jnp.concatenate([g[t] for t in np.argsort(order_of((ny, nc)))], axis=0)
-    else:
-        wo_mine, _ = sum_rows(grad_wo.reshape(nz, nx, own, d))
-    wo_sum = lax.psum_scatter(
-        after(wo_mine, in_sum), "z", scatter_dimension=0, tiled=True
-    )
-
     dc = after(dc, grad_wo)
     if both:
         to_x, to_y, far = first
         low_got = shift(to_x[half:], "x")
-        far, to_y = after(far, arrived), after(to_y, arrived)
-        x_up = (to_x[:half].astype(F32) + send(far[:half], "y")).astype(BF)
         y_low = (to_y[half:].astype(F32) + send(far[half:], "x")).astype(BF)
-        up_got = shift(to_y[:half], "y")
-        dc = after(dc, x_up, y_low)
+        x_up = (to_x[:half].astype(F32) + far_got.astype(F32)).astype(BF)
+        up_got = shift(after(to_y[:half], arrived), "y")
+        y_low = after(y_low, arrived)
         x_got, y_got = shift(x_up, "x"), shift(y_low, "y")
+    ffn_got = [up_got, low_got, x_got, y_got] if both else []
     dqkv = attention_back(qkv, doc, o, den, dc, heads, fk, fv)
-    late = [up_got, low_got, x_got, y_got] if both else []
-    dqkv = after(dqkv, wo_mine, *late)
+    dqkv = after(dqkv, *ffn_got)
+    if joint_form:
+        g = after(grad_wo, dqkv).reshape(nx * ns, own, d)
+        wo_there = exchange(g, ("x", "y", "c"))
+        g = jnp.sum(wo_there.reshape(nx, ns, own, d).astype(F32), axis=0).astype(BF)
+        wo_mine = jnp.concatenate([g[t] for t in np.argsort(order_of((ny, nc)))], axis=0)
+    else:
+        _, wo_mine = sum_rows(grad_wo.reshape(nz, nx, own, d))
+        wo_there = wo_mine
     da_part = dot(dqkv, qkv_mat, NT)
-    grad_qkv = weight_grad(a_all, after(dqkv, da_part))
-    da = stream_sum(da_part, rows)
-    qkv_mine, qkv_sum = sum_rows(grad_qkv.reshape(nz, nx, ns * own, width), wo_sum, da)
+    grad_qkv = after(weight_grad(a_all, after(dqkv, da_part)), wo_there)
+    da, da_got = stream_sum(da_part, rows)
+    leaving, qkv_mine = sum_rows(grad_qkv.reshape(nz, nx, ns * own, width))
+    del leaving
+    qkv_sum = lax.psum_scatter(
+        after(qkv_mine, in_sum, da_got), "z", scatter_dimension=0, tiled=True
+    )
+    qkv_z = qkv_sum
+    da = da + da_got.astype(F32)
     back = jnp.concatenate([down_sum.reshape(1, ng, own, ff), in_sum.reshape(2, ng, own, ff)])
     back = exchange(back.transpose(1, 0, 2, 3), group)
     order = np.argsort(order_of(sizes)).tolist()
+    qkv_sum = exchange(after(qkv_sum, wo_mine).reshape(ns, own, width), ("y", "c"))
     grad_wg, grad_wu, grad_wd = [unpack(back, m, order) for m in (1, 2, 0)]
-    qkv_sum = after(qkv_sum, grad_wg, grad_wu, grad_wd)
     own_term = after(blocks[0], grad_qkv).astype(F32) + others[0].astype(F32)
     if both:
         ffn = own_term + jnp.concatenate(
@@ -866,8 +959,10 @@
     x_own = tokens.astype(F32)
     inv_own = inverse_rms(x_own)
     grad_tokens = dr + rms_back(da * gain_one, x_own * inv_own, inv_own)
-
-    qkv_sum = exchange(qkv_sum.reshape(ns, own, width), ("y", "c"))
+    wo_sum = lax.psum_scatter(
+        after(wo_mine, qkv_z, grad_tokens, output), "z", scatter_dimension=0, tiled=True
+    )
+
     qkv_sum = qkv_sum.reshape(ny, nc, own, width).transpose(2, 1, 0, 3)
     qkv_sum = qkv_sum.reshape(own, ns, width).astype(F32)
     grad_wq = qkv_sum[:, :, : heads * fk].reshape(wq.shape)

time: 738 us -> 695 us (0.942)
  waiting for transfers between devices: 236 us -> 204 us
  Pallas kernels: 211 us -> 222 us
  local copies, waits for them, and re-layouts: 131 us -> 120 us
    ppermute x52, waiting for transfers between devices: 174 us -> 156 us  [shift(): return lax.ppermute(v, ax, [(i, (i + k) % n) for i in range(n)])]
    all_to_all x6, waiting for transfers between devices: 50.8 us -> 37.7 us  [exchange(): return lax.all_to_all(blocks, axes, 0, 0, tiled=True)]
    reduce_scatter x1, waiting for transfers between devices: 11.2 us -> 0.01 us  [per_device(): lax.psum_scatter(after(grad_down, dz), along, scatter_dimension=0, tiled=...]
    slice x10 -> x6, local copies, waits for them, and re-layouts: 15.7 us -> 5.74 us  [the longest x2 2.92 us: per_device(): dy_far = [shift(dy_x[:half], 'y'), shift(dy_y[half:], 'x')]]
    reduce_scatter x3, waiting for transfers between devices: 0.02 us -> 9.75 us  [the longest x1 8.47 us: per_device(): lax.psum_scatter(after(qkv_mine, in_sum, da_got), 'z', scatter_dimension=...]
    unnamed x223 -> x241, local copies, waits for them, and re-layouts: 86.4 us -> 94.8 us
  transfers between devices with their start and end apart: 64 -> 64, of which waited for: 25 -> 24; matrix products, arithmetic and copies ran while one was open for 17% -> 14% of each run, Pallas kernels for 22% -> 25%
where the time goes in v3:
time: 695 us; the launch traced here: 690 us
  Pallas kernels  222 us (32%)
  waiting for transfers between devices  204 us (29%)
  local copies, waits for them, and re-layouts  120 us (17%)
  starting transfers between devices  61.4 us (9%)
  other arithmetic  60.9 us (9%)
  between operations  15.5 us (2%)
    ppermute x52, waiting for transfers between devices, shift(): return lax.ppermute(v, ax, [(i, (i + k) % n) for i in range(n)])  156 us
    unnamed x241, local copies, waits for them, and re-layouts  94.8 us
    all_to_all x6, waiting for transfers between devices, exchange(): return lax.all_to_all(blocks, axes, 0, 0, tiled=True)  37.7 us
    ppermute x52, starting transfers between devices, shift(): return lax.ppermute(v, ax, [(i, (i + k) % n) for i in range(n)])  36.9 us
    pallas_call x3, Pallas kernels, ffn_back(): pl.pallas_call(ffn_back_kernel, grid=(count,), in_specs=[rows, rows, mat(...  34.3 us
    pallas_call x2, Pallas kernels, ffn_in(): pl.pallas_call(functools.partial(ffn_in_kernel, [len(some) for some in st...  30.3 us
    pallas_call x1, Pallas kernels, down_both(): pl.pallas_call(down_kernel, grid=(steps,), in_specs=[pl.BlockSpec((rows,...  27.4 us
    all_to_all x6, starting transfers between devices, exchange(): return lax.all_to_all(blocks, axes, 0, 0, tiled=True)  23.9 us
  transfers between devices with their start and end apart: 64, of which 24 were waited for; matrix products, arithmetic and copies ran while one was open for 14% of the time, Pallas kernels for 25%

profile of v3, /device:TPU:0, one launch (start us, length us, event | category | flops | bytes accessed | tf_op | source)
XLA Modules:
  0.0 689.8 jit_solution(12139146371905820694)
XLA Ops:
  11.7 4.2 all-to-all-start
  16.0 7.6 %all-to-all-done.refs_1_ = bf16[4,80,640]{2,1,0:T(8,128)(2,1)S(1)} async-done(((bf16[4,80,640]{2,1,0:T(8,128)(2,1)}), bf16[4,80,640]{2,1,0:T(8,128)(2,1)S(1)}, u32[]{:S(2)}, u32[]{:S(2)}) %all-to-all-start) | async-done | bytes 409632 | tf_op jit(solution)/shard_map/all_to_all | solution.py:64
  24.6 4.3 split.1
  39.7 21.8 %all-to-all-done.1.refs_1_ = bf16[8,3,64,688]{3,2,1,0:T(8,128)(2,1)S(1)} async-done(((bf16[8,3,64,688]{3,2,1,0:T(8,128)(2,1)}), bf16[8,3,64,688]{3,2,1,0:T(8,128)(2,1)S(1)}, u32[]{:S(2)}, u32[]{:S(2)}) %all-to-all-start.1) | async-done | bytes 2113568 | tf_op jit(solution)/shard_map/all_to_all | solution.py:64
  63.1 26.0 %collective-permute-done.1.refs_2_.refs_1_ = bf16[320,2048]{1,0:T(8,128)(2,1)} collective-permute-done((bf16[320,2048]{1,0:T(8,128)(2,1)}, bf16[320,2048]{1,0:T(8,128)(2,1)}, u32[]{:S(2)}, u32[]{:S(2)}) %collective-permute-start.1) | collective-permute-done | bytes 1310752 | tf_op jit(solution)/shard_map/ppermute | solution.py:24
  97.5 30.6 %collective-permute-done.3.refs_5_.refs_1_ = bf16[4,336,512]{2,1,0:T(8,128)(2,1)S(1)} collective-permute-done((bf16[4,336,512]{2,1,0:T(8,128)(2,1)S(1)}, bf16[4,336,512]{2,1,0:T(8,128)(2,1)S(1)}, u32[]{:S(2)}, u32[]{:S(2)}) %collective-permute-start.3) | collective-permute-done | bytes 1376288 | tf_op jit(solution)/shard_map/ppermute | solution.py:24
  129.5 4.4 all-to-all-start.2
  143.7 12.5 %qkv_in.1 = (bf16[1280,2048]{1,0:T(8,128)(2,1)}, bf16[1280,640]{1,0:T(8,128)(2,1)}, bf16[2048,640]{1,0:T(8,128)(2,1)}, f32[2,2048]{1,0:T(2,128)}) custom-call(s32[4]{0:T(128)} %pad_add_fusion.places, s32[2]{0:T(128)} %pad_add_fusion.1.at, bf16[320,2048]{1,0:T(8,128)(2,1)} %after.34.refs_0_, bf16[320,2048]{1,0:T(8,128)(2,1)} %collective-permute-done.refs_1_, ...), custom_call_target="tpu_custom_call" | custom-call | flops 3355443200 | bytes 15728640 | tf_op jit(solution)/shard_map/qkv_in/pallas_call | solution.py:313
  156.2 10.8 %attention.1 = (bf16[1280,512]{1,0:T(8,128)(2,1)}, f32[1280,512]{1,0:T(8,128)}, f32[1280,4]{1,0:T(8,128)}) custom-call(bf16[1280,640]{1,0:T(8,128)(2,1)} %get-tuple-element.49.qkv, s32[1,1280]{1,0:T(1,128)} %reshape.142.doc_row, s32[1280,1]{1,0:T(8,128)} %reshape.147.doc_col), custom_call_target="tpu_custom_call" | custom-call | flops 3355443200 | bytes 7680000 | tf_op jit(solution)/shard_map/attention/pallas_call | solution.py:199
  168.3 5.3 collective-permute-done.7.refs_3_
  174.6 7.1 %out_terms.1 = bf16[1280,2048]{1,0:T(8,128)(2,1)} custom-call(bf16[1280,512]{1,0:T(8,128)(2,1)} %copy-done.47, bf16[8,4,64,512]{3,2,1,0:T(8,128)(2,1)} %bitcast.17.w.refs_4_), custom_call_target="tpu_custom_call" | custom-call | flops 2684354560 | bytes 8650752 | tf_op jit(solution)/shard_map/out_terms/pallas_call | solution.py:695
  194.5 28.5 %collective-permute-done.10 = bf16[320,2048]{1,0:T(8,128)(2,1)} collective-permute-done((bf16[320,2048]{1,0:T(8,128)(2,1)}, bf16[320,2048]{1,0:T(8,128)(2,1)}, u32[]{:S(2)}, u32[]{:S(2)}) %collective-permute-start.10) | collective-permute-done | bytes 1310752 | tf_op jit(solution)/shard_map/ppermute | solution.py:24
  232.9 24.2 %collective-permute-done.16.refs_2_ = bf16[320,2048]{1,0:T(8,128)(2,1)S(1)} collective-permute-done((bf16[320,2048]{1,0:T(8,128)(2,1)S(1)}, bf16[320,2048]{1,0:T(8,128)(2,1)S(1)}, u32[]{:S(2)}, u32[]{:S(2)}) %collective-permute-start.16) | collective-permute-done | bytes 1310752 | tf_op jit(solution)/shard_map/ppermute | solution.py:24
  269.1 20.5 %ffn_in.2 = (bf16[2560,2048]{1,0:T(8,128)(2,1)}, f32[2560,688]{1,0:T(8,128)}, f32[2560,688]{1,0:T(8,128)}, bf16[2560,688]{1,0:T(8,128)(2,1)}) custom-call(bf16[320,2048]{1,0:T(8,128)(2,1)} %copy-done.46, bf16[320,2048]{1,0:T(8,128)(2,1)} %copy-done.106, bf16[320,2048]{1,0:T(8,128)(2,1)} %copy-done.95, bf16[320,2048]{1,0:T(8,128)(2,1)} %copy-done.107, ...), custom_call_target="tpu_custom_call" | custom-call | flops 10821304320 | bytes 34574336 | tf_op jit(solution)/shard_map/ffn_in/pallas_call | solution.py:433
  297.0 9.8 %ffn_in.3 = (bf16[2560,2048]{1,0:T(8,128)(2,1)}, f32[2560,688]{1,0:T(8,128)}, f32[2560,688]{1,0:T(8,128)}, bf16[2560,688]{1,0:T(8,128)(2,1)}) custom-call(bf16[160,2048]{1,0:T(8,128)(2,1)} %copy-done.61, bf16[160,2048]{1,0:T(8,128)(2,1)} %copy-done.62, ...), custom_call_target="tpu_custom_call", output_to_operand_aliasing={{0}: (6, {}), {1}: (7, {}), {2}: (8, {}), {3}: (9, {})} | custom-call | flops 3607101440 | bytes 15282176 | tf_op jit(solution)/shard_map/ffn_in/pallas_call | solution.py:433
  306.9 17.9 %ffn_mid.1 = (bf16[2560,688]{1,0:T(8,128)(2,1)}, bf16[2560,688]{1,0:T(8,128)(2,1)}) custom-call(f32[2560,688]{1,0:T(8,128)} %get-tuple-element.57.gate, f32[2560,688]{1,0:T(8,128)} %get-tuple-element.58.up, bf16[2560,2048]{1,0:T(8,128)(2,1)} %copy-done.10, bf16[4,3,512,688]{3,2,1,0:T(8,128)(2,1)} %bitcast.88), custom_call_target="tpu_custom_call" | custom-call | flops 7214202880 | bytes 34439168 | tf_op jit(solution)/shard_map/ffn_mid/pallas_call | solution.py:463
  324.8 9.4 %ffn_back.3 = (bf16[320,2048]{1,0:T(8,128)(2,1)}, bf16[320,2048]{1,0:T(8,128)(2,1)}) custom-call(bf16[2560,688]{1,0:T(8,128)(2,1)} %get-tuple-element.59.dgate.refs_0_, bf16[2560,688]{1,0:T(8,128)(2,1)} %get-tuple-element.60.dup.b1, bf16[4,3,512,688]{3,2,1,0:T(8,128)(2,1)} %bitcast.89, bf16[4,3,512,688]{3,2,1,0:T(8,128)(2,1)} %bitcast.90), custom_call_target="tpu_custom_call" | custom-call | flops 3607101440 | bytes 10018816 | tf_op jit(solution)/shard_map/ffn_back/pallas_call | solution.py:488
  343.3 15.5 %ffn_back.4 = (bf16[320,2048]{1,0:T(8,128)(2,1)}, bf16[320,2048]{1,0:T(8,128)(2,1)}, bf16[320,2048]{1,0:T(8,128)(2,1)}, bf16[320,2048]{1,0:T(8,128)(2,1)}) custom-call(bf16[2560,688]{1,0:T(8,128)(2,1)} %copy-done.1, bf16[2560,688]{1,0:T(8,128)(2,1)} %get-tuple-element.60.dup.b1, bf16[4,3,512,688]{3,2,1,0:T(8,128)(2,1)} %bitcast.91, ...), custom_call_target="tpu_custom_call" | custom-call | flops 7214202880 | bytes 14401536 | tf_op jit(solution)/shard_map/ffn_back/pallas_call | solution.py:488
  370.2 9.4 %ffn_back.5 = (bf16[320,2048]{1,0:T(8,128)(2,1)}, bf16[320,2048]{1,0:T(8,128)(2,1)}) custom-call(bf16[2560,688]{1,0:T(8,128)(2,1)} %copy-done.3, bf16[2560,688]{1,0:T(8,128)(2,1)} %get-tuple-element.60.dup.b1, bf16[4,3,512,688]{3,2,1,0:T(8,128)(2,1)} %bitcast.93, bf16[4,3,512,688]{3,2,1,0:T(8,128)(2,1)} %bitcast.94), custom_call_target="tpu_custom_call" | custom-call | flops 3607101440 | bytes 10018816 | tf_op jit(solution)/shard_map/ffn_back/pallas_call | solution.py:488
  389.5 27.4 %down_both.1 = (bf16[2048,688]{1,0:T(8,128)(2,1)}, bf16[320,2048]{1,0:T(8,128)(2,1)}, bf16[320,2048]{1,0:T(8,128)(2,1)}, bf16[320,2048]{1,0:T(8,128)(2,1)}, bf16...) custom-call(bf16[2560,2048]{1,0:T(8,128)(2,1)} %copy-done.10, ...), custom_call_target="tpu_custom_call" | custom-call | flops 14428405760 | bytes 33652736 | tf_op jit(solution)/shard_map/down_both/pallas_call | solution.py:631
  439.8 22.4 %pair_grad.1 = (bf16[4,2,512,688]{3,2,1,0:T(8,128)(2,1)}, f32[8,128]{1,0:T(8,128)}) custom-call(bf16[2560,2048]{1,0:T(8,128)(2,1)} %get-tuple-element.73.a, bf16[2560,688]{1,0:T(8,128)(2,1)} %copy-done.5, bf16[2560,688]{1,0:T(8,128)(2,1)} %get-tuple-element.60.dup.b1), custom_call_target="tpu_custom_call" | custom-call | flops 14428405760 | bytes 23166976 | tf_op jit(solution)/shard_map/pair_grad/pallas_call | solution.py:662
  469.4 9.7 %dz_in.1 = (bf16[1280,2048]{1,0:T(8,128)(2,1)}, f32[1280,512]{1,0:T(8,128)}) custom-call(s32[4]{0:T(128)} %pad_add_fusion.places, bf16[320,2048]{1,0:T(8,128)(2,1)} %get-tuple-element.87.refs_0_.refs_1_, bf16[320,2048]{1,0:T(8,128)(2,1)} %collective-permute-done.35.refs_1_, bf16[320,2048]{1,0:T(8,128)(2,1)} %copy-done.20, ...), custom_call_target="tpu_custom_call" | custom-call | flops 2684354560 | bytes 15728640 | tf_op jit(solution)/shard_map/dz_in/pallas_call | solution.py:527
  479.1 4.4 collective-permute-done.41.refs_1_
  488.3 7.2 %weight_grad.2.refs_1_.refs_0_ = bf16[512,2048]{1,0:T(8,128)(2,1)} custom-call(bf16[1280,512]{1,0:T(8,128)(2,1)} %get-tuple-element.50.a, bf16[1280,2048]{1,0:T(8,128)(2,1)} %copy-done.49), custom_call_target="tpu_custom_call" | custom-call | flops 2684354560 | bytes 8650752 | tf_op jit(solution)/shard_map/weight_grad/pallas_call | solution.py:553
  511.9 20.2 %attention_back.1.refs_0_ = bf16[1280,640]{1,0:T(8,128)(2,1)} custom-call(bf16[1280,640]{1,0:T(8,128)(2,1)} %get-tuple-element.49.qkv, s32[1,1280]{1,0:T(1,128)} %reshape.142.doc_row, s32[1280,1]{1,0:T(8,128)} %reshape.147.doc_col, f32[1280,512]{1,0:T(8,128)} %get-tuple-element.71.out, f32[1280,4]{1,0:T(8,128)} %get-tuple-element.72.den, f32[1280,512]{1,0:T(8,128)} %copy-done.54), custom_call_target="tpu_custom_call" | custom-call | flops 8388608000 | bytes 10240000 | tf_op jit(solution)/shard_map/attention_back/pallas_call | solution.py:249
  543.9 6.6 fusion.22.refs_1_
  556.9 4.0 copy-done.12
  563.5 8.2 %weight_grad.3.refs_0_ = bf16[2048,640]{1,0:T(8,128)(2,1)} custom-call(bf16[1280,2048]{1,0:T(8,128)(2,1)} %get-tuple-element.70.a, bf16[1280,640]{1,0:T(8,128)(2,1)} %copy-done.26), custom_call_target="tpu_custom_call" | custom-call | flops 3355443200 | bytes 9502720 | tf_op jit(solution)/shard_map/weight_grad/pallas_call | solution.py:553
  593.0 17.2 %collective-permute-done.51 = bf16[4,256,640]{2,1,0:T(8,128)(2,1)} collective-permute-done((bf16[4,256,640]{2,1,0:T(8,128)(2,1)}, bf16[4,256,640]{2,1,0:T(8,128)(2,1)}, u32[]{:S(2)}, u32[]{:S(2)}) %collective-permute-start.51) | collective-permute-done | bytes 1310752 | tf_op jit(solution)/shard_map/ppermute | solution.py:24
  628.6 4.5 all-to-all-start.5
  642.8 8.5 %reduce-scatter.9.cloned.1.call-done.refs_0_.refs_1_ = bf16[256,640]{1,0:T(8,128)(2,1)} async-done(((bf16[1024,640]{1,0:T(8,128)(2,1)}), bf16[256,640]{1,0:T(8,128)(2,1)}) %reduce-scatter.9.cloned.1.call-update) | async-done | bytes 327696 | tf_op jit(solution)/shard_map/reduce_scatter | solution.py:937
  654.8 6.8 all-to-all-done.5.g
  (478 shorter events, 257.8 us)
Async XLA Ops:
  16.0 73.2 %all-gather.3.cloned.1.call-start = ((), (), s32[]{:S(2)}) async-start(), calls=%async_computation.10 | async-start | bytes 3031040 | tf_op jit(solution)/shard_map/all_gather | solution.py:773
  28.9 32.6 %all-to-all-start.1 = ((bf16[8,3,64,688]{3,2,1,0:T(8,128)(2,1)}), bf16[8,3,64,688]{3,2,1,0:T(8,128)(2,1)S(1)}, u32[]{:S(2)}, u32[]{:S(2)}) async-start(bf16[8,3,64,688]{3,2,1,0:T(8,128)(2,1)} %split.1), calls=%async_computation.1 | async-start | bytes 4718592 | tf_op jit(solution)/shard_map/all_to_all | solution.py:64
  32.5 236.6 %all-gather.5.cloned.1.call-start = ((), (), s32[]{:S(2)}) async-start(), calls=%async_computation.11 | async-start | bytes 11796480 | tf_op jit(solution)/shard_map/all_gather | solution.py:773
  36.3 52.8 %collective-permute-start.1 = (bf16[320,2048]{1,0:T(8,128)(2,1)}, bf16[320,2048]{1,0:T(8,128)(2,1)}, u32[]{:S(2)}, u32[]{:S(2)}) collective-permute-start(bf16[320,2048]{1,0:T(8,128)(2,1)} %after.34.refs_0_), channel_id=1, source_target_pairs={{0,2},{2,0},{1,3},{3,1},{4,6},{6,4},{5,7},{7,5},{8,10},{10,8},{9,1... | collective-permute-start | bytes 3932168 | tf_op jit(solution)/shard_map/ppermute | solution.py:24
  38.2 50.9 %collective-permute-start.5 = (bf16[320,2048]{1,0:T(8,128)(2,1)}, bf16[320,2048]{1,0:T(8,128)(2,1)}, u32[]{:S(2)}, u32[]{:S(2)}) collective-permute-start(bf16[320,2048]{1,0:T(8,128)(2,1)} %after.35.refs_0_), channel_id=1, source_target_pairs={{0,4},{4,0},{1,5},{5,1},{2,6},{6,2},{3,7},{7,3},{8,12},{12,8},{9,1... | collective-permute-start | bytes 3932168 | tf_op jit(solution)/shard_map/ppermute | solution.py:24
  94.0 49.7 %collective-permute-start = (bf16[320,2048]{1,0:T(8,128)(2,1)}, bf16[320,2048]{1,0:T(8,128)(2,1)}, u32[]{:S(2)}, u32[]{:S(2)}) collective-permute-start(bf16[320,2048]{1,0:T(8,128)(2,1)} %after.34.refs_0_), channel_id=1, source_target_pairs={{0,1},{1,0},{2,3},{3,2},{4,5},{5,4},{6,7},{7,6},{8,9},{9,8},{10,11... | collective-permute-start | bytes 3932168 | tf_op jit(solution)/shard_map/ppermute | solution.py:24
  94.1 49.6 %collective-permute-start.2 = (bf16[320,2048]{1,0:T(8,128)(2,1)}, bf16[320,2048]{1,0:T(8,128)(2,1)}, u32[]{:S(2)}, u32[]{:S(2)}) collective-permute-start(bf16[320,2048]{1,0:T(8,128)(2,1)} %collective-permute-done.1.refs_2_.refs_1_), channel_id=1, source_target_pairs={{0,1},{1,0},{2,3},{3,2},{4,5},{5,4},{6,7},{7,6},{8,9},{9,8},{10,11... | collective-permute-start | bytes 3932168 | tf_op jit(solution)/shard_map/ppermute | solution.py:24
  94.6 40.8 %collective-permute-start.4 = (bf16[320,2048]{1,0:T(8,128)(2,1)}, bf16[320,2048]{1,0:T(8,128)(2,1)S(1)}, u32[]{:S(2)}, u32[]{:S(2)}) collective-permute-start(bf16[320,2048]{1,0:T(8,128)(2,1)} %after.36), channel_id=1, source_target_pairs={{0,2},{2,0},{1,3},{3,1},{4,6},{6,4},{5,7},{7,5},{8,10},{10,8},{9,1... | collective-permute-start | bytes 3932168 | tf_op jit(solution)/shard_map/ppermute | solution.py:24
  96.2 31.9 %collective-permute-start.3 = (bf16[4,336,512]{2,1,0:T(8,128)(2,1)S(1)}, bf16[4,336,512]{2,1,0:T(8,128)(2,1)S(1)}, u32[]{:S(2)}, u32[]{:S(2)}) collective-permute-start(bf16[4,336,512]{2,1,0:T(8,128)(2,1)S(1)} %slice.207.refs_4_), channel_id=1, source_target_pairs={{0,4},{4,0},{1,5},{5,1},{2,6},{6,2},{3,7},{7,3},{8,12},{12,8},{9,1... | collective-permute-start | bytes 4128776 | tf_op jit(solution)/shard_map/ppermute | solution.py:24
  129.5 45.2 %all-to-all-start.2 = ((bf16[8,256,512]{2,1,0:T(8,128)(2,1)}), bf16[8,256,512]{2,1,0:T(8,128)(2,1)}, u32[]{:S(2)}, u32[]{:S(2)}) async-start(bf16[8,256,512]{2,1,0:T(8,128)(2,1)} %copy-done.39), calls=%async_computation.2 | async-start | bytes 4194304 | tf_op jit(solution)/shard_map/all_to_all | solution.py:64
  133.8 361.7 %reduce-scatter.5.cloned.1.call-start = ((), (), s32[]{:S(2)}) async-start(), calls=%async_computation.12 | async-start | bytes 3932160 | tf_op jit(solution)/shard_map/reduce_scatter | solution.py:892
  136.3 37.3 %collective-permute-start.7 = (bf16[160,2048]{1,0:T(8,128)(2,1)}, bf16[160,2048]{1,0:T(8,128)(2,1)}, u32[]{:S(2)}, u32[]{:S(2)}) collective-permute-start(bf16[160,2048]{1,0:T(8,128)(2,1)} %slice.210), channel_id=1, source_target_pairs={{0,4},{4,0},{1,5},{5,1},{2,6},{6,2},{3,7},{7,3},{8,12},{12,8},{9,1... | collective-permute-start | bytes 1966088 | tf_op jit(solution)/shard_map/ppermute | solution.py:24
  140.1 33.4 %collective-permute-start.6 = (bf16[160,2048]{1,0:T(8,128)(2,1)}, bf16[160,2048]{1,0:T(8,128)(2,1)}, u32[]{:S(2)}, u32[]{:S(2)}) collective-permute-start(bf16[160,2048]{1,0:T(8,128)(2,1)} %slice.209), channel_id=1, source_target_pairs={{0,2},{2,0},{1,3},{3,1},{4,6},{6,4},{5,7},{7,5},{8,10},{10,8},{9,1... | collective-permute-start | bytes 1966088 | tf_op jit(solution)/shard_map/ppermute | solution.py:24
  191.9 31.1 %collective-permute-start.10 = (bf16[320,2048]{1,0:T(8,128)(2,1)}, bf16[320,2048]{1,0:T(8,128)(2,1)}, u32[]{:S(2)}, u32[]{:S(2)}) collective-permute-start(bf16[320,2048]{1,0:T(8,128)(2,1)} %add_convert_fusion.5), channel_id=1, source_target_pairs={{0,2},{2,0},{1,3},{3,1},{4,6},{6,4},{5,7},{7,5},{8,10},{10,8},{9,1... | collective-permute-start | bytes 3932168 | tf_op jit(solution)/shard_map/ppermute | solution.py:24
  193.4 37.2 %collective-permute-start.11 = (bf16[320,2048]{1,0:T(8,128)(2,1)}, bf16[320,2048]{1,0:T(8,128)(2,1)S(1)}, u32[]{:S(2)}, u32[]{:S(2)}) collective-permute-start(bf16[320,2048]{1,0:T(8,128)(2,1)} %after.36), channel_id=1, source_target_pairs={{0,1},{1,0},{2,3},{3,2},{4,5},{5,4},{6,7},{7,6},{8,9},{9,8},{10,11... | collective-permute-start | bytes 3932168 | tf_op jit(solution)/shard_map/ppermute | solution.py:24
  193.4 39.3 %collective-permute-start.12 = (bf16[320,2048]{1,0:T(8,128)(2,1)}, bf16[320,2048]{1,0:T(8,128)(2,1)S(1)}, u32[]{:S(2)}, u32[]{:S(2)}) collective-permute-start(bf16[320,2048]{1,0:T(8,128)(2,1)} %after.38), channel_id=1, source_target_pairs={{0,1},{1,0},{2,3},{3,2},{4,5},{5,4},{6,7},{7,6},{8,9},{9,8},{10,11... | collective-permute-start | bytes 3932168 | tf_op jit(solution)/shard_map/ppermute | solution.py:24
  232.9 32.6 %collective-permute-start.18 = (bf16[320,2048]{1,0:T(8,128)(2,1)S(1)}, bf16[320,2048]{1,0:T(8,128)(2,1)S(1)}, u32[]{:S(2)}, u32[]{:S(2)}) collective-permute-start(bf16[320,2048]{1,0:T(8,128)(2,1)S(1)} %multiply_convert_fusion.refs_0_), channel_id=1, source_target_pairs={{0,1},{1,0},{2,3},{3,2},{4,5},{5,4},{6,7},{7,6},{8,9},{9,8},{10,11... | collective-permute-start | bytes 3932168 | tf_op jit(solution)/shard_map/ppermute | solution.py:24
  379.8 38.4 %collective-permute-start.31 = (bf16[160,2048]{1,0:T(8,128)(2,1)}, bf16[160,2048]{1,0:T(8,128)(2,1)}, u32[]{:S(2)}, u32[]{:S(2)}) collective-permute-start(bf16[160,2048]{1,0:T(8,128)(2,1)} %slice.281.refs_2_), channel_id=1, source_target_pairs={{0,2},{2,0},{1,3},{3,1},{4,6},{6,4},{5,7},{7,5},{8,10},{10,8},{9,1... | collective-permute-start | bytes 1966088 | tf_op jit(solution)/shard_map/ppermute | solution.py:24
  381.3 37.5 %collective-permute-start.33 = (bf16[160,2048]{1,0:T(8,128)(2,1)}, bf16[160,2048]{1,0:T(8,128)(2,1)}, u32[]{:S(2)}, u32[]{:S(2)}) collective-permute-start(bf16[160,2048]{1,0:T(8,128)(2,1)} %slice.282.refs_1_), channel_id=1, source_target_pairs={{0,4},{4,0},{1,5},{5,1},{2,6},{6,2},{3,7},{7,3},{8,12},{12,8},{9,1... | collective-permute-start | bytes 1966088 | tf_op jit(solution)/shard_map/ppermute | solution.py:24
  382.0 36.7 %collective-permute-start.34 = (bf16[160,2048]{1,0:T(8,128)(2,1)S(1)}, bf16[160,2048]{1,0:T(8,128)(2,1)}, u32[]{:S(2)}, u32[]{:S(2)}) collective-permute-start(bf16[160,2048]{1,0:T(8,128)(2,1)S(1)} %fusion.13.refs_2_), channel_id=1, source_target_pairs={{0,2},{2,0},{1,3},{3,1},{4,6},{6,4},{5,7},{7,5},{8,10},{10,8},{9,1... | collective-permute-start | bytes 1966088 | tf_op jit(solution)/shard_map/ppermute | solution.py:24
  384.8 33.9 %collective-permute-start.32 = (bf16[160,2048]{1,0:T(8,128)(2,1)S(1)}, bf16[160,2048]{1,0:T(8,128)(2,1)}, u32[]{:S(2)}, u32[]{:S(2)}) collective-permute-start(bf16[160,2048]{1,0:T(8,128)(2,1)S(1)} %fusion.14.refs_1_), channel_id=1, source_target_pairs={{0,4},{4,0},{1,5},{5,1},{2,6},{6,2},{3,7},{7,3},{8,12},{12,8},{9,1... | collective-permute-start | bytes 1966088 | tf_op jit(solution)/shard_map/ppermute | solution.py:24
  425.4 37.9 %collective-permute-start.36 = (bf16[320,2048]{1,0:T(8,128)(2,1)}, bf16[320,2048]{1,0:T(8,128)(2,1)S(1)}, u32[]{:S(2)}, u32[]{:S(2)}) collective-permute-start(bf16[320,2048]{1,0:T(8,128)(2,1)} %get-tuple-element.87.refs_0_.refs_1_), channel_id=1, source_target_pairs={{0,2},{2,0},{1,3},{3,1},{4,6},{6,4},{5,7},{7,5},{8,10},{10,8},{9,1... | collective-permute-start | bytes 3932168 | tf_op jit(solution)/shard_map/ppermute | solution.py:24
  428.6 186.6 %reduce-scatter.7.cloned.1.call-start = ((), (), s32[]{:S(2)}) async-start(), calls=%async_computation.13 | async-start | bytes 7864320 | tf_op jit(solution)/shard_map/reduce_scatter | solution.py:906
  432.6 31.6 %collective-permute-start.45 = (bf16[160,2048]{1,0:T(8,128)(2,1)}, bf16[160,2048]{1,0:T(8,128)(2,1)}, u32[]{:S(2)}, u32[]{:S(2)}) collective-permute-start(bf16[160,2048]{1,0:T(8,128)(2,1)} %get-tuple-element.99), channel_id=1, source_target_pairs={{0,4},{4,0},{1,5},{5,1},{2,6},{6,2},{3,7},{7,3},{8,12},{12,8},{9,1... | collective-permute-start | bytes 1966088 | tf_op jit(solution)/shard_map/ppermute | solution.py:24
  540.2 31.5 %all-to-all-start.3 = ((bf16[8,64,2048]{2,1,0:T(8,128)(2,1)}), bf16[8,64,2048]{2,1,0:T(8,128)(2,1)S(1)}, u32[]{:S(2)}, u32[]{:S(2)}) async-start(bf16[8,64,2048]{2,1,0:T(8,128)(2,1)} %bitcast.22), calls=%async_computation.3 | async-start | bytes 4194304 | tf_op jit(solution)/shard_map/all_to_all | solution.py:64
  543.8 107.5 %reduce-scatter.9.cloned.1.call-start = ((), (), s32[]{:S(2)}) async-start(), calls=%async_computation.14 | async-start | bytes 1638400 | tf_op jit(solution)/shard_map/reduce_scatter | solution.py:937
  556.7 64.4 %collective-permute-start.47 = (bf16[320,2048]{1,0:T(8,128)(2,1)}, bf16[320,2048]{1,0:T(8,128)(2,1)}, u32[]{:S(2)}, u32[]{:S(2)}) collective-permute-start(bf16[320,2048]{1,0:T(8,128)(2,1)} %get-tuple-element.84), channel_id=1, source_target_pairs={{0,1},{1,0},{2,3},{3,2},{4,5},{5,4},{6,7},{7,6},{8,9},{9,8},{10,11... | collective-permute-start | bytes 3932168 | tf_op jit(solution)/shard_map/ppermute | solution.py:24
  578.9 31.3 %collective-permute-start.51 = (bf16[4,256,640]{2,1,0:T(8,128)(2,1)}, bf16[4,256,640]{2,1,0:T(8,128)(2,1)}, u32[]{:S(2)}, u32[]{:S(2)}) collective-permute-start(bf16[4,256,640]{2,1,0:T(8,128)(2,1)} %dynamic-slice_bitcast_fusion), channel_id=1, source_target_pairs={{0,4},{4,0},{1,5},{5,1},{2,6},{6,2},{3,7},{7,3},{8,12},{12,8},{9,1... | collective-permute-start | bytes 3932168 | tf_op jit(solution)/shard_map/ppermute | solution.py:24
  584.3 30.9 %collective-permute-start.50 = (bf16[320,2048]{1,0:T(8,128)(2,1)}, bf16[320,2048]{1,0:T(8,128)(2,1)}, u32[]{:S(2)}, u32[]{:S(2)}) collective-permute-start(bf16[320,2048]{1,0:T(8,128)(2,1)} %add_convert_fusion), channel_id=1, source_target_pairs={{0,2},{2,0},{1,3},{3,1},{4,6},{6,4},{5,7},{7,5},{8,10},{10,8},{9,1... | collective-permute-start | bytes 3932168 | tf_op jit(solution)/shard_map/ppermute | solution.py:24
  589.5 45.7 %collective-permute-start.48 = (bf16[320,2048]{1,0:T(8,128)(2,1)}, bf16[320,2048]{1,0:T(8,128)(2,1)}, u32[]{:S(2)}, u32[]{:S(2)}) collective-permute-start(bf16[320,2048]{1,0:T(8,128)(2,1)} %get-tuple-element.91), channel_id=1, source_target_pairs={{0,1},{1,0},{2,3},{3,2},{4,5},{5,4},{6,7},{7,6},{8,9},{9,8},{10,11... | collective-permute-start | bytes 3932168 | tf_op jit(solution)/shard_map/ppermute | solution.py:24
  628.6 33.0 %all-to-all-start.5 = ((bf16[8,3,64,688]{3,2,1,0:T(8,128)(2,1)}), bf16[8,3,64,688]{3,2,1,0:T(8,128)(2,1)}, u32[]{:S(2)}, u32[]{:S(2)}) async-start(bf16[8,3,64,688]{3,2,1,0:T(8,128)(2,1)} %maximum_bitcast_fusion), calls=%async_computation.9 | async-start | bytes 4718592 | tf_op jit(solution)/shard_map/all_to_all | solution.py:64
  633.1 47.8 %reduce-scatter.11.cloned.1.call-start = ((), (), s32[]{:S(2)}) async-start(), calls=%async_computation.15 | async-start | bytes 1310720 | tf_op jit(solution)/shard_map/reduce_scatter | solution.py:962
  (140 other events, 860.1 us)
Sparse Core Ops, SparseCore 0:
  24.7 52.4 all-gather.2
  94.1 167.7 all-gather.4
  428.7 61.1 reduce-scatter.4
  502.2 112.1 reduce-scatter.6
  619.1 32.1 reduce-scatter.8
  655.0 25.9 reduce-scatter.10

commit v4 on v3

--- a/solution.py
+++ b/solution.py
@@ -761,11 +761,10 @@
     along = ("z",) if both else ("z", "x")
     na = nz if both else nz * nx
     blocks = split_columns(order_of(sizes), (wg, wu, wd))
-    vy = ring(after(tokens, pack), "y")
+    dy_x = shift(cotangent, "x")
+    vy = ring(after(tokens, pack, dy_x), "y")
     exchanged = exchange(blocks, group)
     got = exchanged.transpose(1, 0, 2, 3).reshape(-1, ff)
-    late = after(cotangent, pack)
-    dy_x = shift(late, "x")
 
     ndp = nz * nx
 
@@ -819,7 +818,7 @@
         gain_one, gain_two = gains[:, :own].reshape(1, d), gains[:, own:].reshape(1, d)
         a_all = norm_in(flat, places, gain_one)
         qkv = dot(a_all, qkv_mat, NN, BF)
-    late = after(late, exchanged)
+    late = after(cotangent, exchanged)
     if both:
         half = rows // 2
         dy_x, dy_y = after(dy_x, qkv_parts[-1]), after(shift(late, "y"), qkv_parts[-1])

time: 695 us -> 708 us (1.019)
  waiting for transfers between devices: 204 us -> 213 us
    ppermute x52, waiting for transfers between devices: 156 us -> 164 us  [shift(): return lax.ppermute(v, ax, [(i, (i + k) % n) for i in range(n)])]
where the time goes in v4:
time: 708 us; the launch traced here: 702 us
  Pallas kernels  222 us (31%)
  waiting for transfers between devices  213 us (30%)
  local copies, waits for them, and re-layouts  120 us (17%)
  other arithmetic  63 us (9%)
  starting transfers between devices  62.2 us (9%)
  between operations  15.5 us (2%)
    ppermute x52, waiting for transfers between devices, shift(): return lax.ppermute(v, ax, [(i, (i + k) % n) for i in range(n)])  164 us
    unnamed x241, local copies, waits for them, and re-layouts  95.5 us
    all_to_all x6, waiting for transfers between devices, exchange(): return lax.all_to_all(blocks, axes, 0, 0, tiled=True)  40.6 us
    ppermute x52, starting transfers between devices, shift(): return lax.ppermute(v, ax, [(i, (i + k) % n) for i in range(n)])  36.9 us
    pallas_call x3, Pallas kernels, ffn_back(): pl.pallas_call(ffn_back_kernel, grid=(count,), in_specs=[rows, rows, mat(...  34.3 us
    pallas_call x2, Pallas kernels, ffn_in(): pl.pallas_call(functools.partial(ffn_in_kernel, [len(some) for some in st...  30.3 us
    pallas_call x1, Pallas kernels, down_both(): pl.pallas_call(down_kernel, grid=(steps,), in_specs=[pl.BlockSpec((rows,...  27.4 us
    all_to_all x6, starting transfers between devices, exchange(): return lax.all_to_all(blocks, axes, 0, 0, tiled=True)  24.8 us
  transfers between devices with their start and end apart: 64, of which 24 were waited for; matrix products, arithmetic and copies ran while one was open for 14% of the time, Pallas kernels for 25%

profile of v4, /device:TPU:0, one launch (start us, length us, event | category | flops | bytes accessed | tf_op | source)
XLA Modules:
  0.0 702.4 jit_solution(18280573623405846282)
XLA Ops:
  16.0 7.6 %all-to-all-done.refs_1_ = bf16[4,80,640]{2,1,0:T(8,128)(2,1)S(1)} async-done(((bf16[4,80,640]{2,1,0:T(8,128)(2,1)}), bf16[4,80,640]{2,1,0:T(8,128)(2,1)S(1)}, u32[]{:S(2)}, u32[]{:S(2)}) %all-to-all-start) | async-done | bytes 409632 | tf_op jit(solution)/shard_map/all_to_all | solution.py:64
  31.1 4.5 all-to-all-start.1
  36.7 19.9 %collective-permute-done.refs_2_.refs_0_ = bf16[320,2048]{1,0:T(8,128)(2,1)S(1)} collective-permute-done((bf16[320,2048]{1,0:T(8,128)(2,1)}, bf16[320,2048]{1,0:T(8,128)(2,1)S(1)}, u32[]{:S(2)}, u32[]{:S(2)}) %collective-permute-start) | collective-permute-done | bytes 1310752 | tf_op jit(solution)/shard_map/ppermute | solution.py:24
  57.0 24.1 %all-to-all-done.1.refs_1_ = bf16[8,3,64,688]{3,2,1,0:T(8,128)(2,1)} async-done(((bf16[8,3,64,688]{3,2,1,0:T(8,128)(2,1)}), bf16[8,3,64,688]{3,2,1,0:T(8,128)(2,1)}, u32[]{:S(2)}, u32[]{:S(2)}) %all-to-all-start.1) | async-done | bytes 2113568 | tf_op jit(solution)/shard_map/all_to_all | solution.py:64
  84.3 13.5 %collective-permute-done.2.refs_2_.refs_1_ = bf16[320,2048]{1,0:T(8,128)(2,1)} collective-permute-done((bf16[320,2048]{1,0:T(8,128)(2,1)}, bf16[320,2048]{1,0:T(8,128)(2,1)}, u32[]{:S(2)}, u32[]{:S(2)}) %collective-permute-start.2) | collective-permute-done | bytes 1310752 | tf_op jit(solution)/shard_map/ppermute | solution.py:24
  109.0 30.3 %collective-permute-done.4.refs_5_.refs_1_ = bf16[4,336,512]{2,1,0:T(8,128)(2,1)S(1)} collective-permute-done((bf16[4,336,512]{2,1,0:T(8,128)(2,1)S(1)}, bf16[4,336,512]{2,1,0:T(8,128)(2,1)S(1)}, u32[]{:S(2)}, u32[]{:S(2)}) %collective-permute-start.4) | collective-permute-done | bytes 1376288 | tf_op jit(solution)/shard_map/ppermute | solution.py:24
  141.7 4.4 all-to-all-start.2
  156.2 12.5 %qkv_in.1 = (bf16[1280,2048]{1,0:T(8,128)(2,1)}, bf16[1280,640]{1,0:T(8,128)(2,1)}, bf16[2048,640]{1,0:T(8,128)(2,1)}, f32[2,2048]{1,0:T(2,128)}) custom-call(s32[4]{0:T(128)} %pad_add_fusion.places, s32[2]{0:T(128)} %pad_add_fusion.1.at, bf16[320,2048]{1,0:T(8,128)(2,1)} %after.33.refs_0_, bf16[320,2048]{1,0:T(8,128)(2,1)} %collective-permute-done.1.refs_1_, ...), custom_call_target="tpu_custom_call" | custom-call | flops 3355443200 | bytes 15728640 | tf_op jit(solution)/shard_map/qkv_in/pallas_call | solution.py:313
  168.8 10.8 %attention.1 = (bf16[1280,512]{1,0:T(8,128)(2,1)}, f32[1280,512]{1,0:T(8,128)}, f32[1280,4]{1,0:T(8,128)}) custom-call(bf16[1280,640]{1,0:T(8,128)(2,1)} %get-tuple-element.49.qkv, s32[1,1280]{1,0:T(1,128)} %reshape.142.doc_row, s32[1280,1]{1,0:T(8,128)} %reshape.147.doc_col), custom_call_target="tpu_custom_call" | custom-call | flops 3355443200 | bytes 7680000 | tf_op jit(solution)/shard_map/attention/pallas_call | solution.py:199
  180.8 5.0 collective-permute-done.7.refs_3_
  186.9 7.0 out_terms.1
  206.7 28.5 %collective-permute-done.10 = bf16[320,2048]{1,0:T(8,128)(2,1)} collective-permute-done((bf16[320,2048]{1,0:T(8,128)(2,1)}, bf16[320,2048]{1,0:T(8,128)(2,1)}, u32[]{:S(2)}, u32[]{:S(2)}) %collective-permute-start.10) | collective-permute-done | bytes 1310752 | tf_op jit(solution)/shard_map/ppermute | solution.py:24
  244.3 25.4 %collective-permute-done.16.refs_2_ = bf16[320,2048]{1,0:T(8,128)(2,1)S(1)} collective-permute-done((bf16[320,2048]{1,0:T(8,128)(2,1)S(1)}, bf16[320,2048]{1,0:T(8,128)(2,1)S(1)}, u32[]{:S(2)}, u32[]{:S(2)}) %collective-permute-start.16) | collective-permute-done | bytes 1310752 | tf_op jit(solution)/shard_map/ppermute | solution.py:24
  281.6 20.5 %ffn_in.2 = (bf16[2560,2048]{1,0:T(8,128)(2,1)}, f32[2560,688]{1,0:T(8,128)}, f32[2560,688]{1,0:T(8,128)}, bf16[2560,688]{1,0:T(8,128)(2,1)}) custom-call(bf16[320,2048]{1,0:T(8,128)(2,1)} %copy-done.48, bf16[320,2048]{1,0:T(8,128)(2,1)} %copy-done.106, bf16[320,2048]{1,0:T(8,128)(2,1)} %copy-done.95, bf16[320,2048]{1,0:T(8,128)(2,1)} %copy-done.107, ...), custom_call_target="tpu_custom_call" | custom-call | flops 10821304320 | bytes 34574336 | tf_op jit(solution)/shard_map/ffn_in/pallas_call | solution.py:433
  309.5 9.8 %ffn_in.3 = (bf16[2560,2048]{1,0:T(8,128)(2,1)}, f32[2560,688]{1,0:T(8,128)}, f32[2560,688]{1,0:T(8,128)}, bf16[2560,688]{1,0:T(8,128)(2,1)}) custom-call(bf16[160,2048]{1,0:T(8,128)(2,1)} %copy-done.63, bf16[160,2048]{1,0:T(8,128)(2,1)} %copy-done.64, ...), custom_call_target="tpu_custom_call", output_to_operand_aliasing={{0}: (6, {}), {1}: (7, {}), {2}: (8, {}), {3}: (9, {})} | custom-call | flops 3607101440 | bytes 15282176 | tf_op jit(solution)/shard_map/ffn_in/pallas_call | solution.py:433
  319.3 17.9 %ffn_mid.1 = (bf16[2560,688]{1,0:T(8,128)(2,1)}, bf16[2560,688]{1,0:T(8,128)(2,1)}) custom-call(f32[2560,688]{1,0:T(8,128)} %get-tuple-element.57.gate, f32[2560,688]{1,0:T(8,128)} %get-tuple-element.58.up, bf16[2560,2048]{1,0:T(8,128)(2,1)} %copy-done.10, bf16[4,3,512,688]{3,2,1,0:T(8,128)(2,1)} %bitcast.87), custom_call_target="tpu_custom_call" | custom-call | flops 7214202880 | bytes 34439168 | tf_op jit(solution)/shard_map/ffn_mid/pallas_call | solution.py:463
  337.2 9.4 %ffn_back.3 = (bf16[320,2048]{1,0:T(8,128)(2,1)}, bf16[320,2048]{1,0:T(8,128)(2,1)}) custom-call(bf16[2560,688]{1,0:T(8,128)(2,1)} %get-tuple-element.59.dgate.refs_0_, bf16[2560,688]{1,0:T(8,128)(2,1)} %get-tuple-element.60.dup.b1, bf16[4,3,512,688]{3,2,1,0:T(8,128)(2,1)} %bitcast.88, bf16[4,3,512,688]{3,2,1,0:T(8,128)(2,1)} %bitcast.89), custom_call_target="tpu_custom_call" | custom-call | flops 3607101440 | bytes 10018816 | tf_op jit(solution)/shard_map/ffn_back/pallas_call | solution.py:488
  356.3 15.5 %ffn_back.4 = (bf16[320,2048]{1,0:T(8,128)(2,1)}, bf16[320,2048]{1,0:T(8,128)(2,1)}, bf16[320,2048]{1,0:T(8,128)(2,1)}, bf16[320,2048]{1,0:T(8,128)(2,1)}) custom-call(bf16[2560,688]{1,0:T(8,128)(2,1)} %copy-done.1, bf16[2560,688]{1,0:T(8,128)(2,1)} %get-tuple-element.60.dup.b1, bf16[4,3,512,688]{3,2,1,0:T(8,128)(2,1)} %bitcast.90, ...), custom_call_target="tpu_custom_call" | custom-call | flops 7214202880 | bytes 14401536 | tf_op jit(solution)/shard_map/ffn_back/pallas_call | solution.py:488
  383.3 9.4 %ffn_back.5 = (bf16[320,2048]{1,0:T(8,128)(2,1)}, bf16[320,2048]{1,0:T(8,128)(2,1)}) custom-call(bf16[2560,688]{1,0:T(8,128)(2,1)} %copy-done.3, bf16[2560,688]{1,0:T(8,128)(2,1)} %get-tuple-element.60.dup.b1, bf16[4,3,512,688]{3,2,1,0:T(8,128)(2,1)} %bitcast.92, bf16[4,3,512,688]{3,2,1,0:T(8,128)(2,1)} %bitcast.93), custom_call_target="tpu_custom_call" | custom-call | flops 3607101440 | bytes 10018816 | tf_op jit(solution)/shard_map/ffn_back/pallas_call | solution.py:488
  402.5 27.4 %down_both.1 = (bf16[2048,688]{1,0:T(8,128)(2,1)}, bf16[320,2048]{1,0:T(8,128)(2,1)}, bf16[320,2048]{1,0:T(8,128)(2,1)}, bf16[320,2048]{1,0:T(8,128)(2,1)}, bf16...) custom-call(bf16[2560,2048]{1,0:T(8,128)(2,1)} %copy-done.10, ...), custom_call_target="tpu_custom_call" | custom-call | flops 14428405760 | bytes 33652736 | tf_op jit(solution)/shard_map/down_both/pallas_call | solution.py:631
  434.9 4.3 fusion.16
  452.8 22.4 %pair_grad.1 = (bf16[4,2,512,688]{3,2,1,0:T(8,128)(2,1)}, f32[8,128]{1,0:T(8,128)}) custom-call(bf16[2560,2048]{1,0:T(8,128)(2,1)} %get-tuple-element.73.a, bf16[2560,688]{1,0:T(8,128)(2,1)} %copy-done.5, bf16[2560,688]{1,0:T(8,128)(2,1)} %get-tuple-element.60.dup.b1), custom_call_target="tpu_custom_call" | custom-call | flops 14428405760 | bytes 23166976 | tf_op jit(solution)/shard_map/pair_grad/pallas_call | solution.py:662
  482.5 9.6 %dz_in.1 = (bf16[1280,2048]{1,0:T(8,128)(2,1)}, f32[1280,512]{1,0:T(8,128)}) custom-call(s32[4]{0:T(128)} %pad_add_fusion.places, bf16[320,2048]{1,0:T(8,128)(2,1)} %get-tuple-element.87.refs_0_.refs_1_, bf16[320,2048]{1,0:T(8,128)(2,1)} %collective-permute-done.35.refs_1_, bf16[320,2048]{1,0:T(8,128)(2,1)} %copy-done.20, ...), custom_call_target="tpu_custom_call" | custom-call | flops 2684354560 | bytes 15728640 | tf_op jit(solution)/shard_map/dz_in/pallas_call | solution.py:527
  492.1 4.4 collective-permute-done.41.refs_1_
  501.4 7.2 %weight_grad.2.refs_1_.refs_0_ = bf16[512,2048]{1,0:T(8,128)(2,1)} custom-call(bf16[1280,512]{1,0:T(8,128)(2,1)} %get-tuple-element.50.a, bf16[1280,2048]{1,0:T(8,128)(2,1)} %copy-done.51), custom_call_target="tpu_custom_call" | custom-call | flops 2684354560 | bytes 8650752 | tf_op jit(solution)/shard_map/weight_grad/pallas_call | solution.py:553
  525.0 20.2 %attention_back.1.refs_0_ = bf16[1280,640]{1,0:T(8,128)(2,1)} custom-call(bf16[1280,640]{1,0:T(8,128)(2,1)} %get-tuple-element.49.qkv, s32[1,1280]{1,0:T(1,128)} %reshape.142.doc_row, s32[1280,1]{1,0:T(8,128)} %reshape.147.doc_col, f32[1280,512]{1,0:T(8,128)} %get-tuple-element.71.out, f32[1280,4]{1,0:T(8,128)} %get-tuple-element.72.den, f32[1280,512]{1,0:T(8,128)} %copy-done.56), custom_call_target="tpu_custom_call" | custom-call | flops 8388608000 | bytes 10240000 | tf_op jit(solution)/shard_map/attention_back/pallas_call | solution.py:249
  557.0 6.6 fusion.22.refs_1_
  576.7 8.2 %weight_grad.3.refs_0_ = bf16[2048,640]{1,0:T(8,128)(2,1)} custom-call(bf16[1280,2048]{1,0:T(8,128)(2,1)} %get-tuple-element.70.a, bf16[1280,640]{1,0:T(8,128)(2,1)} %copy-done.26), custom_call_target="tpu_custom_call" | custom-call | flops 3355443200 | bytes 9502720 | tf_op jit(solution)/shard_map/weight_grad/pallas_call | solution.py:553
  606.4 17.1 %collective-permute-done.51 = bf16[4,256,640]{2,1,0:T(8,128)(2,1)} collective-permute-done((bf16[4,256,640]{2,1,0:T(8,128)(2,1)}, bf16[4,256,640]{2,1,0:T(8,128)(2,1)}, u32[]{:S(2)}, u32[]{:S(2)}) %collective-permute-start.51) | collective-permute-done | bytes 1310752 | tf_op jit(solution)/shard_map/ppermute | solution.py:24
  641.9 4.5 all-to-all-start.5
  656.2 7.8 %reduce-scatter.9.cloned.1.call-done.refs_0_.refs_1_ = bf16[256,640]{1,0:T(8,128)(2,1)} async-done(((bf16[1024,640]{1,0:T(8,128)(2,1)}), bf16[256,640]{1,0:T(8,128)(2,1)}) %reduce-scatter.9.cloned.1.call-update) | async-done | bytes 327696 | tf_op jit(solution)/shard_map/reduce_scatter | solution.py:936
  667.5 7.5 %all-to-all-done.5.g = bf16[8,3,64,688]{3,2,1,0:T(8,128)(2,1)} async-done(((bf16[8,3,64,688]{3,2,1,0:T(8,128)(2,1)}), bf16[8,3,64,688]{3,2,1,0:T(8,128)(2,1)}, u32[]{:S(2)}, u32[]{:S(2)}) %all-to-all-start.5) | async-done | bytes 2113568 | tf_op jit(solution)/shard_map/all_to_all | solution.py:64
  (477 shorter events, 263.7 us)
Async XLA Ops:
  16.0 81.9 %all-gather.3.cloned.1.call-start = ((), (), s32[]{:S(2)}) async-start(), calls=%async_computation.10 | async-start | bytes 3031040 | tf_op jit(solution)/shard_map/all_gather | solution.py:772
  24.6 32.0 %collective-permute-start = (bf16[320,2048]{1,0:T(8,128)(2,1)}, bf16[320,2048]{1,0:T(8,128)(2,1)S(1)}, u32[]{:S(2)}, u32[]{:S(2)}) collective-permute-start(bf16[320,2048]{1,0:T(8,128)(2,1)} %param.14), channel_id=1, source_target_pairs={{0,4},{4,0},{1,5},{5,1},{2,6},{6,2},{3,7},{7,3},{8,12},{12,8},{9,1... | collective-permute-start | bytes 3932168 | tf_op jit(solution)/shard_map/ppermute | solution.py:24
  31.1 50.0 %all-to-all-start.1 = ((bf16[8,3,64,688]{3,2,1,0:T(8,128)(2,1)}), bf16[8,3,64,688]{3,2,1,0:T(8,128)(2,1)}, u32[]{:S(2)}, u32[]{:S(2)}) async-start(bf16[8,3,64,688]{3,2,1,0:T(8,128)(2,1)} %split.1), calls=%async_computation.1 | async-start | bytes 4718592 | tf_op jit(solution)/shard_map/all_to_all | solution.py:64
  35.6 246.0 %all-gather.5.cloned.1.call-start = ((), (), s32[]{:S(2)}) async-start(), calls=%async_computation.11 | async-start | bytes 11796480 | tf_op jit(solution)/shard_map/all_gather | solution.py:772
  56.7 41.2 %collective-permute-start.2 = (bf16[320,2048]{1,0:T(8,128)(2,1)}, bf16[320,2048]{1,0:T(8,128)(2,1)}, u32[]{:S(2)}, u32[]{:S(2)}) collective-permute-start(bf16[320,2048]{1,0:T(8,128)(2,1)} %after.33.refs_0_), channel_id=1, source_target_pairs={{0,2},{2,0},{1,3},{3,1},{4,6},{6,4},{5,7},{7,5},{8,10},{10,8},{9,1... | collective-permute-start | bytes 3932168 | tf_op jit(solution)/shard_map/ppermute | solution.py:24
  105.2 51.0 %collective-permute-start.1 = (bf16[320,2048]{1,0:T(8,128)(2,1)}, bf16[320,2048]{1,0:T(8,128)(2,1)}, u32[]{:S(2)}, u32[]{:S(2)}) collective-permute-start(bf16[320,2048]{1,0:T(8,128)(2,1)} %after.33.refs_0_), channel_id=1, source_target_pairs={{0,1},{1,0},{2,3},{3,2},{4,5},{5,4},{6,7},{7,6},{8,9},{9,8},{10,11... | collective-permute-start | bytes 3932168 | tf_op jit(solution)/shard_map/ppermute | solution.py:24
  105.2 42.4 %collective-permute-start.5 = (bf16[320,2048]{1,0:T(8,128)(2,1)}, bf16[320,2048]{1,0:T(8,128)(2,1)S(1)}, u32[]{:S(2)}, u32[]{:S(2)}) collective-permute-start(bf16[320,2048]{1,0:T(8,128)(2,1)} %after.34), channel_id=1, source_target_pairs={{0,2},{2,0},{1,3},{3,1},{4,6},{6,4},{5,7},{7,5},{8,10},{10,8},{9,1... | collective-permute-start | bytes 3932168 | tf_op jit(solution)/shard_map/ppermute | solution.py:24
  106.6 49.7 %collective-permute-start.3 = (bf16[320,2048]{1,0:T(8,128)(2,1)}, bf16[320,2048]{1,0:T(8,128)(2,1)}, u32[]{:S(2)}, u32[]{:S(2)}) collective-permute-start(bf16[320,2048]{1,0:T(8,128)(2,1)} %collective-permute-done.2.refs_2_.refs_1_), channel_id=1, source_target_pairs={{0,1},{1,0},{2,3},{3,2},{4,5},{5,4},{6,7},{7,6},{8,9},{9,8},{10,11... | collective-permute-start | bytes 3932168 | tf_op jit(solution)/shard_map/ppermute | solution.py:24
  107.0 32.3 %collective-permute-start.4 = (bf16[4,336,512]{2,1,0:T(8,128)(2,1)S(1)}, bf16[4,336,512]{2,1,0:T(8,128)(2,1)S(1)}, u32[]{:S(2)}, u32[]{:S(2)}) collective-permute-start(bf16[4,336,512]{2,1,0:T(8,128)(2,1)S(1)} %slice.207.refs_4_), channel_id=1, source_target_pairs={{0,4},{4,0},{1,5},{5,1},{2,6},{6,2},{3,7},{7,3},{8,12},{12,8},{9,1... | collective-permute-start | bytes 4128776 | tf_op jit(solution)/shard_map/ppermute | solution.py:24
  141.7 45.2 %all-to-all-start.2 = ((bf16[8,256,512]{2,1,0:T(8,128)(2,1)}), bf16[8,256,512]{2,1,0:T(8,128)(2,1)}, u32[]{:S(2)}, u32[]{:S(2)}) async-start(bf16[8,256,512]{2,1,0:T(8,128)(2,1)} %copy-done.41), calls=%async_computation.2 | async-start | bytes 4194304 | tf_op jit(solution)/shard_map/all_to_all | solution.py:64
  146.1 362.5 %reduce-scatter.5.cloned.1.call-start = ((), (), s32[]{:S(2)}) async-start(), calls=%async_computation.12 | async-start | bytes 3932160 | tf_op jit(solution)/shard_map/reduce_scatter | solution.py:891
  149.9 36.0 %collective-permute-start.7 = (bf16[160,2048]{1,0:T(8,128)(2,1)}, bf16[160,2048]{1,0:T(8,128)(2,1)}, u32[]{:S(2)}, u32[]{:S(2)}) collective-permute-start(bf16[160,2048]{1,0:T(8,128)(2,1)} %slice.210), channel_id=1, source_target_pairs={{0,4},{4,0},{1,5},{5,1},{2,6},{6,2},{3,7},{7,3},{8,12},{12,8},{9,1... | collective-permute-start | bytes 1966088 | tf_op jit(solution)/shard_map/ppermute | solution.py:24
  152.6 33.2 %collective-permute-start.6 = (bf16[160,2048]{1,0:T(8,128)(2,1)}, bf16[160,2048]{1,0:T(8,128)(2,1)}, u32[]{:S(2)}, u32[]{:S(2)}) collective-permute-start(bf16[160,2048]{1,0:T(8,128)(2,1)} %slice.209), channel_id=1, source_target_pairs={{0,2},{2,0},{1,3},{3,1},{4,6},{6,4},{5,7},{7,5},{8,10},{10,8},{9,1... | collective-permute-start | bytes 1966088 | tf_op jit(solution)/shard_map/ppermute | solution.py:24
  204.1 31.1 %collective-permute-start.10 = (bf16[320,2048]{1,0:T(8,128)(2,1)}, bf16[320,2048]{1,0:T(8,128)(2,1)}, u32[]{:S(2)}, u32[]{:S(2)}) collective-permute-start(bf16[320,2048]{1,0:T(8,128)(2,1)} %add_convert_fusion.5), channel_id=1, source_target_pairs={{0,2},{2,0},{1,3},{3,1},{4,6},{6,4},{5,7},{7,5},{8,10},{10,8},{9,1... | collective-permute-start | bytes 3932168 | tf_op jit(solution)/shard_map/ppermute | solution.py:24
  205.6 37.6 %collective-permute-start.11 = (bf16[320,2048]{1,0:T(8,128)(2,1)}, bf16[320,2048]{1,0:T(8,128)(2,1)S(1)}, u32[]{:S(2)}, u32[]{:S(2)}) collective-permute-start(bf16[320,2048]{1,0:T(8,128)(2,1)} %after.34), channel_id=1, source_target_pairs={{0,1},{1,0},{2,3},{3,2},{4,5},{5,4},{6,7},{7,6},{8,9},{9,8},{10,11... | collective-permute-start | bytes 3932168 | tf_op jit(solution)/shard_map/ppermute | solution.py:24
  205.6 38.4 %collective-permute-start.12 = (bf16[320,2048]{1,0:T(8,128)(2,1)S(1)}, bf16[320,2048]{1,0:T(8,128)(2,1)S(1)}, u32[]{:S(2)}, u32[]{:S(2)}) collective-permute-start(bf16[320,2048]{1,0:T(8,128)(2,1)S(1)} %after.36), channel_id=1, source_target_pairs={{0,1},{1,0},{2,3},{3,2},{4,5},{5,4},{6,7},{7,6},{8,9},{9,8},{10,11... | collective-permute-start | bytes 3932168 | tf_op jit(solution)/shard_map/ppermute | solution.py:24
  244.2 33.6 %collective-permute-start.18 = (bf16[320,2048]{1,0:T(8,128)(2,1)S(1)}, bf16[320,2048]{1,0:T(8,128)(2,1)S(1)}, u32[]{:S(2)}, u32[]{:S(2)}) collective-permute-start(bf16[320,2048]{1,0:T(8,128)(2,1)S(1)} %multiply_convert_fusion.refs_0_), channel_id=1, source_target_pairs={{0,1},{1,0},{2,3},{3,2},{4,5},{5,4},{6,7},{7,6},{8,9},{9,8},{10,11... | collective-permute-start | bytes 3932168 | tf_op jit(solution)/shard_map/ppermute | solution.py:24
  392.9 38.4 %collective-permute-start.31 = (bf16[160,2048]{1,0:T(8,128)(2,1)}, bf16[160,2048]{1,0:T(8,128)(2,1)}, u32[]{:S(2)}, u32[]{:S(2)}) collective-permute-start(bf16[160,2048]{1,0:T(8,128)(2,1)} %slice.281.refs_2_), channel_id=1, source_target_pairs={{0,2},{2,0},{1,3},{3,1},{4,6},{6,4},{5,7},{7,5},{8,10},{10,8},{9,1... | collective-permute-start | bytes 1966088 | tf_op jit(solution)/shard_map/ppermute | solution.py:24
  393.8 38.0 %collective-permute-start.33 = (bf16[160,2048]{1,0:T(8,128)(2,1)}, bf16[160,2048]{1,0:T(8,128)(2,1)}, u32[]{:S(2)}, u32[]{:S(2)}) collective-permute-start(bf16[160,2048]{1,0:T(8,128)(2,1)} %slice.282.refs_1_), channel_id=1, source_target_pairs={{0,4},{4,0},{1,5},{5,1},{2,6},{6,2},{3,7},{7,3},{8,12},{12,8},{9,1... | collective-permute-start | bytes 1966088 | tf_op jit(solution)/shard_map/ppermute | solution.py:24
  394.5 37.3 %collective-permute-start.34 = (bf16[160,2048]{1,0:T(8,128)(2,1)S(1)}, bf16[160,2048]{1,0:T(8,128)(2,1)}, u32[]{:S(2)}, u32[]{:S(2)}) collective-permute-start(bf16[160,2048]{1,0:T(8,128)(2,1)S(1)} %fusion.13.refs_2_), channel_id=1, source_target_pairs={{0,2},{2,0},{1,3},{3,1},{4,6},{6,4},{5,7},{7,5},{8,10},{10,8},{9,1... | collective-permute-start | bytes 1966088 | tf_op jit(solution)/shard_map/ppermute | solution.py:24
  397.3 34.5 %collective-permute-start.32 = (bf16[160,2048]{1,0:T(8,128)(2,1)S(1)}, bf16[160,2048]{1,0:T(8,128)(2,1)}, u32[]{:S(2)}, u32[]{:S(2)}) collective-permute-start(bf16[160,2048]{1,0:T(8,128)(2,1)S(1)} %fusion.14.refs_1_), channel_id=1, source_target_pairs={{0,4},{4,0},{1,5},{5,1},{2,6},{6,2},{3,7},{7,3},{8,12},{12,8},{9,1... | collective-permute-start | bytes 1966088 | tf_op jit(solution)/shard_map/ppermute | solution.py:24
  439.2 37.3 %collective-permute-start.36 = (bf16[320,2048]{1,0:T(8,128)(2,1)}, bf16[320,2048]{1,0:T(8,128)(2,1)S(1)}, u32[]{:S(2)}, u32[]{:S(2)}) collective-permute-start(bf16[320,2048]{1,0:T(8,128)(2,1)} %get-tuple-element.87.refs_0_.refs_1_), channel_id=1, source_target_pairs={{0,2},{2,0},{1,3},{3,1},{4,6},{6,4},{5,7},{7,5},{8,10},{10,8},{9,1... | collective-permute-start | bytes 3932168 | tf_op jit(solution)/shard_map/ppermute | solution.py:24
  441.8 186.7 %reduce-scatter.7.cloned.1.call-start = ((), (), s32[]{:S(2)}) async-start(), calls=%async_computation.13 | async-start | bytes 7864320 | tf_op jit(solution)/shard_map/reduce_scatter | solution.py:905
  445.8 31.5 %collective-permute-start.45 = (bf16[160,2048]{1,0:T(8,128)(2,1)}, bf16[160,2048]{1,0:T(8,128)(2,1)}, u32[]{:S(2)}, u32[]{:S(2)}) collective-permute-start(bf16[160,2048]{1,0:T(8,128)(2,1)} %get-tuple-element.99), channel_id=1, source_target_pairs={{0,4},{4,0},{1,5},{5,1},{2,6},{6,2},{3,7},{7,3},{8,12},{12,8},{9,1... | collective-permute-start | bytes 1966088 | tf_op jit(solution)/shard_map/ppermute | solution.py:24
  553.4 31.5 %all-to-all-start.3 = ((bf16[8,64,2048]{2,1,0:T(8,128)(2,1)}), bf16[8,64,2048]{2,1,0:T(8,128)(2,1)S(1)}, u32[]{:S(2)}, u32[]{:S(2)}) async-start(bf16[8,64,2048]{2,1,0:T(8,128)(2,1)} %bitcast.22), calls=%async_computation.3 | async-start | bytes 4194304 | tf_op jit(solution)/shard_map/all_to_all | solution.py:64
  557.0 106.9 %reduce-scatter.9.cloned.1.call-start = ((), (), s32[]{:S(2)}) async-start(), calls=%async_computation.14 | async-start | bytes 1638400 | tf_op jit(solution)/shard_map/reduce_scatter | solution.py:936
  569.9 64.6 %collective-permute-start.47 = (bf16[320,2048]{1,0:T(8,128)(2,1)}, bf16[320,2048]{1,0:T(8,128)(2,1)}, u32[]{:S(2)}, u32[]{:S(2)}) collective-permute-start(bf16[320,2048]{1,0:T(8,128)(2,1)} %get-tuple-element.84), channel_id=1, source_target_pairs={{0,1},{1,0},{2,3},{3,2},{4,5},{5,4},{6,7},{7,6},{8,9},{9,8},{10,11... | collective-permute-start | bytes 3932168 | tf_op jit(solution)/shard_map/ppermute | solution.py:24
  592.1 31.4 %collective-permute-start.51 = (bf16[4,256,640]{2,1,0:T(8,128)(2,1)}, bf16[4,256,640]{2,1,0:T(8,128)(2,1)}, u32[]{:S(2)}, u32[]{:S(2)}) collective-permute-start(bf16[4,256,640]{2,1,0:T(8,128)(2,1)} %dynamic-slice_bitcast_fusion), channel_id=1, source_target_pairs={{0,4},{4,0},{1,5},{5,1},{2,6},{6,2},{3,7},{7,3},{8,12},{12,8},{9,1... | collective-permute-start | bytes 3932168 | tf_op jit(solution)/shard_map/ppermute | solution.py:24
  597.6 30.9 %collective-permute-start.50 = (bf16[320,2048]{1,0:T(8,128)(2,1)}, bf16[320,2048]{1,0:T(8,128)(2,1)}, u32[]{:S(2)}, u32[]{:S(2)}) collective-permute-start(bf16[320,2048]{1,0:T(8,128)(2,1)} %add_convert_fusion), channel_id=1, source_target_pairs={{0,2},{2,0},{1,3},{3,1},{4,6},{6,4},{5,7},{7,5},{8,10},{10,8},{9,1... | collective-permute-start | bytes 3932168 | tf_op jit(solution)/shard_map/ppermute | solution.py:24
  602.9 45.7 %collective-permute-start.48 = (bf16[320,2048]{1,0:T(8,128)(2,1)}, bf16[320,2048]{1,0:T(8,128)(2,1)}, u32[]{:S(2)}, u32[]{:S(2)}) collective-permute-start(bf16[320,2048]{1,0:T(8,128)(2,1)} %get-tuple-element.91), channel_id=1, source_target_pairs={{0,1},{1,0},{2,3},{3,2},{4,5},{5,4},{6,7},{7,6},{8,9},{9,8},{10,11... | collective-permute-start | bytes 3932168 | tf_op jit(solution)/shard_map/ppermute | solution.py:24
  641.9 33.0 %all-to-all-start.5 = ((bf16[8,3,64,688]{3,2,1,0:T(8,128)(2,1)}), bf16[8,3,64,688]{3,2,1,0:T(8,128)(2,1)}, u32[]{:S(2)}, u32[]{:S(2)}) async-start(bf16[8,3,64,688]{3,2,1,0:T(8,128)(2,1)} %maximum_bitcast_fusion), calls=%async_computation.9 | async-start | bytes 4718592 | tf_op jit(solution)/shard_map/all_to_all | solution.py:64
  646.4 47.1 %reduce-scatter.11.cloned.1.call-start = ((), (), s32[]{:S(2)}) async-start(), calls=%async_computation.15 | async-start | bytes 1310720 | tf_op jit(solution)/shard_map/reduce_scatter | solution.py:961
  (140 other events, 788.7 us)
Sparse Core Ops, SparseCore 0:
  24.7 52.4 all-gather.2
  102.8 167.9 all-gather.4
  441.9 60.6 reduce-scatter.4
  515.4 111.2 reduce-scatter.6
  632.4 31.4 reduce-scatter.8
  667.6 25.9 reduce-scatter.10
